TPU v7x, 32 devices: a whole 2x2x4 slice. The times are simulated.
32 devices in a mesh: seq: 16 (over z, y, x), chan: 2 (over core).
Axes of the slice: x: 2, y: 2, z: 4, core: 2. Of those that a mesh axis runs over, the one named last changes fastest.
Arguments:
- layer_input: bfloat16 [8192, 1024], P('seq', 'chan'), may hold values from -24 to 24
- gain_first: float32 [1024], replicated, may hold values from 0.5 to 1.5
- in_weight: bfloat16 [1024, 3, 1024], P(None, None, 'chan'), may hold values from -0.1875 to 0.1875
- short_weight: float32 [3, 3, 1024], P(None, None, 'chan'), may hold values from -3.5 to 3.5
- filt_in: bfloat16 [25, 64], replicated, may hold values from -4 to 4
- filt_bias: float32 [64], replicated, may hold values from -3.140625 to 3.140625
- filt_mid: bfloat16 [64, 64], replicated, may hold values from -1 to 1
- filt_out: bfloat16 [64, 1024], P(None, 'chan'), may hold values from -0.0625 to 0.0625
- decay_rate: float32 [1024], P('chan'), may hold values from 0.05 to 273.06667
- conv_bias: float32 [1024], P('chan'), may hold values from -4 to 4
- out_weight: bfloat16 [1024, 1024], P('chan'), may hold values from -0.25 to 0.25
- gain_second: float32 [1024], replicated, may hold values from 0.5 to 1.5
- up_weight: bfloat16 [1024, 4096], P(None, 'chan'), may hold values from -0.1875 to 0.1875
- down_weight: bfloat16 [4096, 1024], P('chan'), may hold values from -0.125 to 0.125
Outputs:
- block_out: bfloat16 [8192, 1024], P('seq', 'chan')
All inputs are finite; a program needn't handle non-finite values.
Results may differ from a plain program's by a relative error of at most 0.01.
The roundings to bfloat16 on the way count: a program that leaves them out, or rounds other values in their place, can miss the bound.
Values may be sent and summed in bfloat16 or wider, within the bound.
No kernel may reach another device: no remote copies, remote signals or barrier semaphores. Data moves between devices by JAX's collectives and lax.ppermute only.
A program may use at most 128 MiB of HBM per device.

v0:
```python
import jax
import jax.numpy as jnp
from jax import lax
from jax.sharding import PartitionSpec as P

D = 1024
BANDS = 12
KSHORT = 3
N1 = 128


EPS = 1e-05
TWO_PI = 6.283185307179586
HIGH = lax.Precision.HIGHEST


def shifted(array, axis, by):
    count = lax.axis_size(axis)
    pairs = [(i, i + by) for i in range(count) if 0 <= i + by < count]
    return lax.ppermute(array, axis, pairs)


def phase_table(left_ids, right_ids, modulus):
    product = left_ids[:, None] * right_ids[None, :] % modulus
    angles = product.astype(jnp.float32) * (TWO_PI / modulus)
    return (jnp.cos(angles), jnp.sin(angles))


def layer_norm(rows_in, gain_row):
    values = rows_in.astype(jnp.float32)
    row_mean = jnp.mean(values, axis=-1, keepdims=True)
    centered = values - row_mean
    spread = jnp.mean(centered * centered, axis=-1, keepdims=True)
    return (centered * lax.rsqrt(spread + EPS) * gain_row).astype(jnp.bfloat16)


def filter_hidden(positions, full_length, filt_in, filt_bias, filt_mid):
    powers = 2 ** jnp.arange(BANDS, dtype=jnp.int32)
    angles = (positions[None, :] * powers[:, None] % full_length).astype(jnp.float32) * (
        TWO_PI / full_length
    )
    ramp_row = positions.astype(jnp.float32)[None, :] / full_length
    features = jnp.concatenate([ramp_row, jnp.cos(angles), jnp.sin(angles)], 0).astype(jnp.bfloat16)
    first_layer = lax.dot_general(
        filt_in, features, (((0,), (0,)), ((), ())), preferred_element_type=jnp.float32
    )
    first_layer = jnp.sin(first_layer + filt_bias[:, None]).astype(jnp.bfloat16)
    second_layer = lax.dot_general(
        filt_mid, first_layer, (((0,), (0,)), ((), ())), preferred_element_type=jnp.float32
    )
    return jnp.sin(second_layer).astype(jnp.bfloat16)


def forward_rows(real_rows, cosine_rows, sine_rows):
    flat_rows = real_rows.reshape(real_rows.shape[0], -1)
    out_shape = (cosine_rows.shape[0],) + real_rows.shape[1:]
    real_part = jnp.dot(cosine_rows, flat_rows, precision=HIGH, preferred_element_type=jnp.float32)
    imag_part = -jnp.dot(sine_rows, flat_rows, precision=HIGH, preferred_element_type=jnp.float32)
    return (real_part.reshape(out_shape), imag_part.reshape(out_shape))


def inverse_rows(real_part, imag_part, cosine_rows, sine_rows, full_length):
    dims = (((0,), (0,)), ((), ()))
    flat_real = real_part.reshape(real_part.shape[0], -1)
    flat_imag = imag_part.reshape(imag_part.shape[0], -1)
    values = lax.dot_general(
        cosine_rows, flat_real, dims, precision=HIGH, preferred_element_type=jnp.float32
    )
    values = values - lax.dot_general(
        sine_rows, flat_imag, dims, precision=HIGH, preferred_element_type=jnp.float32
    )
    return (values / full_length).reshape((cosine_rows.shape[1],) + real_part.shape[1:])


def rotate(real_part, imag_part, turn_cos, turn_sin, direction):
    return (
        real_part * turn_cos + direction * imag_part * turn_sin,
        imag_part * turn_cos - direction * real_part * turn_sin,
    )


def mix_middle(real_part, imag_part, cosine_mid, sine_mid, direction):

    def contract(matrix, operand):
        return jnp.einsum(
            "kn,anc->akc", matrix, operand, precision=HIGH, preferred_element_type=jnp.float32
        )

    return (
        contract(cosine_mid, real_part) + direction * contract(sine_mid, imag_part),
        contract(cosine_mid, imag_part) - direction * contract(sine_mid, real_part),
    )


def per_device(
    layer_input,
    gain_first,
    in_weight,
    short_weight,
    filt_in,
    filt_bias,
    filt_mid,
    filt_out,
    decay_rate,
    conv_bias,
    out_weight,
    gain_second,
    up_weight,
    down_weight,
):
    tokens, channels = layer_input.shape
    groups = lax.axis_size("seq")
    seq_place = lax.axis_index("seq")
    length = tokens * groups
    full_length = 2 * length
    blocks = tokens // N1
    kept_rows = length // N1
    second_factor = full_length // N1
    whole_input = lax.all_gather(layer_input, "chan", axis=1, tiled=True)
    normed = layer_norm(whole_input, gain_first)
    projected = jnp.dot(
        normed, in_weight.reshape(in_weight.shape[0], -1), preferred_element_type=jnp.float32
    ).astype(jnp.bfloat16)
    earlier = shifted(projected[tokens - (KSHORT - 1) :], "seq", 1)
    padded = (
        jnp.concatenate([earlier, projected], 0)
        .astype(jnp.float32)
        .reshape(tokens + KSHORT - 1, 3, channels)
    )
    shorted = short_weight[0] * padded[KSHORT - 1 :]
    for lag_index in range(1, KSHORT):
        shorted = (
            shorted
            + short_weight[lag_index]
            * padded[KSHORT - 1 - lag_index : KSHORT - 1 - lag_index + tokens]
        )
    gate_out = shorted[:, 0]
    gate_in = shorted[:, 1]
    value_part = shorted[:, 2]
    gated_value = value_part * gate_in
    frequencies = jnp.arange(second_factor, dtype=jnp.int32)
    row_ids = jnp.arange(kept_rows, dtype=jnp.int32)
    cosine_rows, sine_rows = phase_table(frequencies, row_ids, second_factor)
    mid_ids = jnp.arange(N1, dtype=jnp.int32)
    cosine_mid, sine_mid = phase_table(mid_ids, mid_ids, N1)
    share_rows = N1 // groups
    starts = seq_place * share_rows + jnp.arange(share_rows, dtype=jnp.int32)
    turn_cos, turn_sin = phase_table(frequencies, starts, full_length)
    turn_cos = turn_cos[:, :, None]
    turn_sin = turn_sin[:, :, None]
    regrouped = lax.all_to_all(
        gated_value.reshape(blocks, N1, channels), "seq", split_axis=1, concat_axis=0, tiled=True
    )
    signal_real, signal_imag = forward_rows(regrouped, cosine_rows, sine_rows)
    signal_real, signal_imag = rotate(signal_real, signal_imag, turn_cos, turn_sin, 1.0)
    signal_real, signal_imag = (
        lax.all_to_all(signal_real, "seq", split_axis=0, concat_axis=1, tiled=True),
        lax.all_to_all(signal_imag, "seq", split_axis=0, concat_axis=1, tiled=True),
    )
    signal_real, signal_imag = mix_middle(signal_real, signal_imag, cosine_mid, sine_mid, 1.0)
    freq_share = second_factor // groups
    own_freqs = seq_place * freq_share + jnp.arange(freq_share, dtype=jnp.int32)
    own_cos, own_sin = phase_table(own_freqs, row_ids, second_factor)
    own_turn_cos, own_turn_sin = phase_table(own_freqs, mid_ids, full_length)
    own_turn_cos = own_turn_cos[:, :, None]
    own_turn_sin = own_turn_sin[:, :, None]
    row_block = kept_rows // 4
    block_ids = jnp.arange(row_block * N1, dtype=jnp.int32)

    def add_rows(carry, step_id):
        acc_real, acc_imag = carry
        positions = step_id * (row_block * N1) + block_ids
        block_layer = filter_hidden(positions, length, filt_in, filt_bias, filt_mid)
        response = lax.dot_general(
            block_layer, filt_out, (((0,), (0,)), ((), ())), preferred_element_type=jnp.float32
        )
        response = response * jnp.exp(
            -decay_rate[None, :] * (positions.astype(jnp.float32)[:, None] / length)
        )
        response = response.reshape(row_block, N1, channels)
        cos_part = lax.dynamic_slice_in_dim(own_cos, step_id * row_block, row_block, 1)
        sin_part = lax.dynamic_slice_in_dim(own_sin, step_id * row_block, row_block, 1)
        part_real, part_imag = forward_rows(response, cos_part, sin_part)
        return ((acc_real + part_real, acc_imag + part_imag), None)

    empty = jnp.zeros((freq_share, N1, channels), jnp.float32)
    (filter_real, filter_imag), unused = lax.scan(
        add_rows, (empty, empty), jnp.arange(4, dtype=jnp.int32)
    )
    filter_real, filter_imag = rotate(filter_real, filter_imag, own_turn_cos, own_turn_sin, 1.0)
    filter_real, filter_imag = mix_middle(filter_real, filter_imag, cosine_mid, sine_mid, 1.0)
    product_real = signal_real * filter_real - signal_imag * filter_imag
    product_imag = signal_real * filter_imag + signal_imag * filter_real
    product_real, product_imag = mix_middle(product_real, product_imag, cosine_mid, sine_mid, -1.0)
    product_real, product_imag = (
        lax.all_to_all(product_real, "seq", split_axis=1, concat_axis=0, tiled=True),
        lax.all_to_all(product_imag, "seq", split_axis=1, concat_axis=0, tiled=True),
    )
    product_real, product_imag = rotate(product_real, product_imag, turn_cos, turn_sin, -1.0)
    result = inverse_rows(product_real, product_imag, cosine_rows, sine_rows, full_length)
    convolved = lax.all_to_all(result, "seq", split_axis=0, concat_axis=1, tiled=True).reshape(
        tokens, channels
    )
    mixed_rows = ((convolved + conv_bias * gated_value) * gate_out).astype(jnp.bfloat16)
    partial_value = jnp.dot(mixed_rows, out_weight, preferred_element_type=jnp.float32)
    chan_start = lax.axis_index("chan") * channels
    attended = lax.psum_scatter(partial_value, "chan", scatter_dimension=1, tiled=True)
    residual = (layer_input.astype(jnp.float32) + attended).astype(jnp.bfloat16)
    values = residual.astype(jnp.float32)
    total_sum, total_square = lax.psum(
        (jnp.sum(values, axis=1), jnp.sum(values * values, axis=1)), "chan"
    )
    row_mean = total_sum / D
    spread = total_square / D - row_mean * row_mean
    gain_part = lax.dynamic_slice_in_dim(gain_second, chan_start, channels, 0)
    normed_part = (
        (values - row_mean[:, None]) * lax.rsqrt(spread + EPS)[:, None] * gain_part
    ).astype(jnp.bfloat16)
    lifted = jnp.dot(
        lax.all_gather(normed_part, "chan", axis=1, tiled=True),
        up_weight,
        preferred_element_type=jnp.float32,
    )
    hidden = jax.nn.gelu(lifted, approximate=False).astype(jnp.bfloat16)
    down_sums = lax.psum_scatter(
        jnp.dot(hidden, down_weight, preferred_element_type=jnp.float32),
        "chan",
        scatter_dimension=1,
        tiled=True,
    )
    return (residual.astype(jnp.float32) + down_sums).astype(jnp.bfloat16)


def solution(mesh):
    placed = (
        P("seq", "chan"),
        P(),
        P(None, None, "chan"),
        P(None, None, "chan"),
        P(),
        P(),
        P(),
        P(None, "chan"),
        P("chan"),
        P("chan"),
        P("chan", None),
        P(),
        P(None, "chan"),
        P("chan", None),
    )
    return jax.shard_map(
        per_device, mesh=mesh, in_specs=placed, out_specs=P("seq", "chan"), check_vma=False
    )
```

profile of v0, /device:TPU:0, one launch (start us, length us, event | category | flops | bytes accessed | tf_op | source)
XLA Modules:
  0.0 525.6 jit_solution(15790046618448944950)
XLA Ops:
  7.3 4.7 copy.185
  11.9 8.7 %all-gather.3.cloned.1.call-done = bf16[512,1024]{1,0:T(8,128)(2,1)} async-done(((bf16[512,512]{1,0:T(8,128)(2,1)}), bf16[512,1024]{1,0:T(8,128)(2,1)}) %all-gather.3.cloned.1.call-update) | async-done | bytes 1048592 | tf_op jit(solution)/shard_map/all_gather | solution.py:119
  23.9 3.8 convolution_convert_fusion
  27.7 3.6 collective-permute-start
  33.2 3.8 fusion.272
  36.9 3.6 copy.188
  40.5 3.6 copy.187
  44.1 3.6 copy.186
  47.7 4.2 multiply_add_fusion
  55.4 7.8 %all-to-all-start = ((f32[4,128,512]{2,0,1:T(4,128)}), f32[4,128,512]{2,0,1:T(4,128)S(1)}, u32[]{:S(2)}, u32[]{:S(2)}) async-start(f32[4,128,512]{2,0,1:T(4,128)} %copy.189), calls=%async_computation | async-start | bytes 2097152 | tf_op jit(solution)/shard_map/all_to_all | solution.py:151
  63.9 23.0 %all-to-all-done = f32[4,128,512]{2,0,1:T(4,128)S(1)} async-done(((f32[4,128,512]{2,0,1:T(4,128)}), f32[4,128,512]{2,0,1:T(4,128)S(1)}, u32[]{:S(2)}, u32[]{:S(2)}) %all-to-all-start) | async-done | bytes 1048608 | tf_op jit(solution)/shard_map/all_to_all | solution.py:151
  97.1 5.7 %multiply_add_fusion.3 = (f32[128,8,512]{2,0,1:T(8,128)}, f32[128,8,512]{2,0,1:T(8,128)S(1)}) fusion(f32[128,8,512]{2,0,1:T(8,128)} %copy.194, f32[128,8]{0,1:T(8,128)S(1)} %get-tuple-element.244, f32[128,8]{0,1:T(8,128)S(1)} %get-tuple-element.245, f32[8,8,8,512]{3,2,1,0:T(8,128)S(1)} %bitcast.202), kind=kOutput, calls=%fused_computation.109 | convolution fusion | flops 405913600 | bytes 7348224 | tf_op jit(solution)/shard_map/dot_general | solution.py:57
  105.4 6.0 %all-to-all-start.2 = ((f32[128,8,512]{2,1,0:T(8,128)}), f32[128,8,512]{2,1,0:T(8,128)}, u32[]{:S(2)}, u32[]{:S(2)}) async-start(f32[128,8,512]{2,1,0:T(8,128)} %copy.199), calls=%async_computation.2 | async-start | bytes 4194304 | tf_op jit(solution)/shard_map/all_to_all | solution.py:158
  112.7 4.2 copy.195
  116.8 36.4 %all-to-all-done.2 = f32[128,8,512]{2,1,0:T(8,128)} async-done(((f32[128,8,512]{2,1,0:T(8,128)}), f32[128,8,512]{2,1,0:T(8,128)}, u32[]{:S(2)}, u32[]{:S(2)}) %all-to-all-start.2) | async-done | bytes 2097184 | tf_op jit(solution)/shard_map/all_to_all | solution.py:158
  153.2 10.0 %all-to-all-start.1 = ((f32[128,8,512]{2,1,0:T(8,128)}), f32[128,8,512]{2,1,0:T(8,128)}, u32[]{:S(2)}, u32[]{:S(2)}) async-start(f32[128,8,512]{2,1,0:T(8,128)} %copy.195), calls=%async_computation.1 | async-start | bytes 4194304 | tf_op jit(solution)/shard_map/all_to_all | solution.py:157
  163.3 98.6 %while.15 = (s32[]{:T(128)}, f32[8,128,512]{2,0,1:T(8,128)}, f32[8,128,512]{2,0,1:T(8,128)S(1)}, s32[4]{0:T(128)S(1)}, f32[8,64]{1,0:T(8,128)}, /*index=5*/bf16[...) while((s32[]{:T(128)}, f32[8,128,512]{2,0,1:T(8,128)}, ...), condition=%wide.region_3.4_spmd.clone, body=%wide.region_2.3_spmd.clone.sunk | while | flops 364697920 | bytes 51202024 | solution.py:187
  166.0 4.5 fusion.309
  174.0 3.9 reshape.270
  178.7 5.8 %select_add_fusion.4 = f32[8,128,512]{2,0,1:T(8,128)} fusion(f32[8,128,512]{2,0,1:T(8,128)} %get-tuple-element.342, f32[2,128,8,512]{3,2,1,0:T(8,128)} %bitcast.192, pred[]{:T(512)S(6)} %compare.19, f32[8,64]{1,0:T(8,128)S(1)} %copy-done.15, s32[]{:T(128)S(6)} %select_n.315), kind=kOutput, calls=%fused_computation.12.clone.1 | convolution fusion | flops 101711872 | bytes 8390661 | tf_op jit(solution)/shard_map/while/body/eval_jaxpr/dot_general | solution.py:57
  190.1 4.5 fusion.309
  198.1 3.9 reshape.270
  202.8 6.5 %select_add_fusion.4 = f32[8,128,512]{2,0,1:T(8,128)} fusion(f32[8,128,512]{2,0,1:T(8,128)} %get-tuple-element.342, f32[2,128,8,512]{3,2,1,0:T(8,128)} %bitcast.192, pred[]{:T(512)S(6)} %compare.19, f32[8,64]{1,0:T(8,128)S(1)} %copy-done.15, s32[]{:T(128)S(6)} %select_n.315), kind=kOutput, calls=%fused_computation.12.clone.1 | convolution fusion | flops 101711872 | bytes 8390661 | tf_op jit(solution)/shard_map/while/body/eval_jaxpr/dot_general | solution.py:57
  214.9 4.5 fusion.309
  219.4 3.6 exponential_multiply_fusion.2
  223.0 3.9 reshape.270
  227.6 6.5 %select_add_fusion.4 = f32[8,128,512]{2,0,1:T(8,128)} fusion(f32[8,128,512]{2,0,1:T(8,128)} %get-tuple-element.342, f32[2,128,8,512]{3,2,1,0:T(8,128)} %bitcast.192, pred[]{:T(512)S(6)} %compare.19, f32[8,64]{1,0:T(8,128)S(1)} %copy-done.15, s32[]{:T(128)S(6)} %select_n.315), kind=kOutput, calls=%fused_computation.12.clone.1 | convolution fusion | flops 101711872 | bytes 8390661 | tf_op jit(solution)/shard_map/while/body/eval_jaxpr/dot_general | solution.py:57
  239.8 4.5 fusion.309
  244.3 3.5 exponential_multiply_fusion.2
  247.8 3.9 reshape.270
  252.5 6.5 %select_add_fusion.4 = f32[8,128,512]{2,0,1:T(8,128)} fusion(f32[8,128,512]{2,0,1:T(8,128)} %get-tuple-element.342, f32[2,128,8,512]{3,2,1,0:T(8,128)} %bitcast.192, pred[]{:T(512)S(6)} %compare.19, f32[8,64]{1,0:T(8,128)S(1)} %copy-done.15, s32[]{:T(128)S(6)} %select_n.315), kind=kOutput, calls=%fused_computation.12.clone.1 | convolution fusion | flops 101711872 | bytes 8390661 | tf_op jit(solution)/shard_map/while/body/eval_jaxpr/dot_general | solution.py:57
  262.9 4.2 multiply_subtract_fusion.1
  283.5 5.3 %fusion.60 = f32[8,512,128]{2,1,0:T(8,128)S(1)} fusion(f32[8,16,8,512]{3,2,0,1:T(8,128)} %bitcast.17), kind=kOutput, calls=%fused_computation.89 | convolution fusion | flops 805535744 | bytes 4194304 | tf_op jit(solution)/shard_map/kn,anc->akc/dot_general | solution.py:85
  288.8 6.5 %fusion.58 = f32[8,512,128]{2,1,0:T(8,128)} fusion(f32[8,16,8,512]{3,2,0,1:T(8,128)} %bitcast.17), kind=kOutput, calls=%fused_computation.87 | convolution fusion | flops 805535744 | bytes 4194304 | tf_op jit(solution)/shard_map/kn,anc->akc/dot_general | solution.py:85
  295.4 5.3 %fusion.79 = f32[8,512,128]{2,1,0:T(8,128)S(1)} fusion(f32[8,512,128]{2,1,0:T(8,128)S(1)} %fusion.60, f32[8,16,8,512]{3,2,0,1:T(8,128)} %bitcast.13), kind=kOutput, calls=%fused_computation.119 | convolution fusion | flops 806060032 | bytes 6291456 | tf_op jit(solution)/shard_map/kn,anc->akc/dot_general | solution.py:85
  300.7 5.3 %multiply_subtract_fusion = (f32[8,512,128]{2,1,0:T(8,128)S(1)}, f32[8,512,128]{2,1,0:T(8,128)S(1)}) fusion(f32[8,512,128]{2,1,0:T(8,128)S(1)} %copy-done.9, f32[8,512,128]{2,1,0:T(8,128)S(1)} %fusion.79, f32[8,512,128]{2,1,0:T(8,128)S(1)} %copy-done.10, f32[8,512,128]{2,1,0:T(8,128)S(1)} %copy-done.11, f32[8,16,8,512]{3,2,0,1:T(8,128)} %bitcast.13), kind=kOutput, calls=%fused_computation.105 | convolution fusion | flops 809205760 | bytes 14680064 | tf_op jit(solution)/shard_map/kn,anc->akc/dot_general | solution.py:85
  315.2 7.1 %all-to-all-start.4 = ((f32[8,128,512]{2,0,1:T(8,128)}), f32[8,128,512]{2,0,1:T(8,128)}, u32[]{:S(2)}, u32[]{:S(2)}) async-start(f32[8,128,512]{2,0,1:T(8,128)} %copy.215), calls=%async_computation.4 | async-start | bytes 4194304 | tf_op jit(solution)/shard_map/all_to_all | solution.py:197
  322.3 3.7 fusion.52
  332.5 31.5 %all-to-all-done.4 = f32[8,128,512]{2,0,1:T(8,128)} async-done(((f32[8,128,512]{2,0,1:T(8,128)}), f32[8,128,512]{2,0,1:T(8,128)}, u32[]{:S(2)}, u32[]{:S(2)}) %all-to-all-start.4) | async-done | bytes 2097184 | tf_op jit(solution)/shard_map/all_to_all | solution.py:197
  364.0 9.8 %all-to-all-start.3 = ((f32[8,128,512]{2,0,1:T(8,128)}), f32[8,128,512]{2,0,1:T(8,128)S(1)}, u32[]{:S(2)}, u32[]{:S(2)}) async-start(f32[8,128,512]{2,0,1:T(8,128)} %copy.210), calls=%async_computation.3 | async-start | bytes 4194304 | tf_op jit(solution)/shard_map/all_to_all | solution.py:196
  381.6 34.6 %all-to-all-done.3 = f32[8,128,512]{2,0,1:T(8,128)S(1)} async-done(((f32[8,128,512]{2,0,1:T(8,128)}), f32[8,128,512]{2,0,1:T(8,128)S(1)}, u32[]{:S(2)}, u32[]{:S(2)}) %all-to-all-start.3) | async-done | bytes 2097184 | tf_op jit(solution)/shard_map/all_to_all | solution.py:196
  416.3 4.6 fusion.69
  424.9 35.2 %all_to_all.102 = f32[64,8,512]{2,1,0:T(8,128)S(1)} all-to-all(f32[64,8,512]{2,1,0:T(8,128)S(1)} %bitcast.209), channel_id=1, replica_groups=mesh['seq'=16,'chan'=2] {'seq'}, dimensions={0} | all-to-all | bytes 2097152 | tf_op jit(solution)/shard_map/all_to_all | solution.py:201
  461.5 3.8 fusion.104
  466.1 7.3 %reduce-scatter.3.cloned.1.call-done = f32[512,512]{1,0:T(8,128)} async-done(((f32[512,1024]{1,0:T(8,128)}), f32[512,512]{1,0:T(8,128)}) %reduce-scatter.3.cloned.1.call-update) | async-done | bytes 1048592 | tf_op jit(solution)/shard_map/reduce_scatter | solution.py:207
  478.6 10.1 %all-gather.5.cloned.1.call-done = bf16[512,1024]{1,0:T(8,128)(2,1)} async-done(((bf16[512,512]{1,0:T(8,128)(2,1)}), bf16[512,1024]{1,0:T(8,128)(2,1)}) %all-gather.5.cloned.1.call-update) | async-done | bytes 1048592 | tf_op jit(solution)/shard_map/all_gather | solution.py:220
  488.8 17.0 %fusion.73 = f32[512,1024]{1,0:T(8,128)} fusion(bf16[2048,1024]{1,0:T(8,128)(2,1)} %param.29, bf16[512,1024]{1,0:T(8,128)(2,1)} %all-gather.5.cloned.1.call-done, bf16[1024,2048]{1,0:T(8,128)(2,1)} %param.28), kind=kOutput, calls=%fused_computation.110 | convolution fusion | flops 4363124736 | bytes 11534336 | tf_op jit(solution)/shard_map/dot_general | solution.py:226
  505.8 10.9 %reduce-scatter.5.cloned.1.call-done = f32[512,512]{1,0:T(8,128)} async-done(((f32[512,1024]{1,0:T(8,128)}), f32[512,512]{1,0:T(8,128)}) %reduce-scatter.5.cloned.1.call-update) | async-done | bytes 1048592 | tf_op jit(solution)/shard_map/reduce_scatter | solution.py:225
  (183 shorter events, 104.9 us)
Async XLA Ops:
  6.5 454.9 %copy-start = (bf16[512,1024]{1,0:T(8,128)(2,1)S(1)}, bf16[512,1024]{1,0:T(8,128)(2,1)}, u32[]{:S(2)}) copy-start(bf16[512,1024]{1,0:T(8,128)(2,1)} %param.26) | copy-start | bytes 3145732
  6.5 14.1 %all-gather.3.cloned.1.call-start = ((), (), s32[]{:S(2)}) async-start(), calls=%async_computation.8 | async-start | bytes 1572864 | tf_op jit(solution)/shard_map/all_gather | solution.py:119
  11.9 11.9 %copy-start.25 = (f32[1024]{0:T(1024)S(1)}, f32[1024]{0:T(1024)}, u32[]{:S(2)}) copy-start(f32[1024]{0:T(1024)} %param.17) | copy-start | bytes 12292
  20.7 3.2 copy-start.12
  23.9 7.5 %copy-start.19 = (f32[3,3,512]{2,1,0:T(4,128)S(1)}, f32[3,3,512]{2,1,0:T(4,128)}, u32[]{:S(2)}) copy-start(f32[3,3,512]{2,1,0:T(4,128)} %param.19) | copy-start | bytes 55300
  27.7 5.0 collective-permute-start
  51.8 1.6 copy-start.6
  53.7 1.7 copy-start.7
  55.4 31.6 %all-to-all-start = ((f32[4,128,512]{2,0,1:T(4,128)}), f32[4,128,512]{2,0,1:T(4,128)S(1)}, u32[]{:S(2)}, u32[]{:S(2)}) async-start(f32[4,128,512]{2,0,1:T(4,128)} %copy.189), calls=%async_computation | async-start | bytes 2097152 | tf_op jit(solution)/shard_map/all_to_all | solution.py:151
  63.2 48.7 %copy-start.21 = (s32[8]{0:T(128)}, s32[8]{0:T(128)S(1)}, u32[]{:S(2)}) copy-start(s32[8]{0:T(128)S(1)} %iota_add_fusion.1) | copy-start | bytes 100
  63.9 33.2 %copy-start.17 = (f32[128,8]{0,1:T(8,128)}, f32[128,8]{0,1:T(8,128)S(1)}, u32[]{:S(2)}) copy-start(f32[128,8]{0,1:T(8,128)S(1)} %get-tuple-element.245) | copy-start | bytes 12292
  105.4 6.0 %copy-start.23 = (f32[512]{0:T(512)S(1)}, f32[512]{0:T(512)}, u32[]{:S(2)}) copy-start(f32[512]{0:T(512)} %param.24) | copy-start | bytes 6148
  105.4 47.8 %all-to-all-start.2 = ((f32[128,8,512]{2,1,0:T(8,128)}), f32[128,8,512]{2,1,0:T(8,128)}, u32[]{:S(2)}, u32[]{:S(2)}) async-start(f32[128,8,512]{2,1,0:T(8,128)} %copy.199), calls=%async_computation.2 | async-start | bytes 4194304 | tf_op jit(solution)/shard_map/all_to_all | solution.py:158
  116.8 46.5 %copy-start.14 = (bf16[64,512]{1,0:T(8,128)(2,1)S(1)}, bf16[64,512]{1,0:T(8,128)(2,1)}, u32[]{:S(2)}) copy-start(bf16[64,512]{1,0:T(8,128)(2,1)} %param.23) | copy-start | bytes 196612
  153.2 142.2 %all-to-all-start.1 = ((f32[128,8,512]{2,1,0:T(8,128)}), f32[128,8,512]{2,1,0:T(8,128)}, u32[]{:S(2)}, u32[]{:S(2)}) async-start(f32[128,8,512]{2,1,0:T(8,128)} %copy.195), calls=%async_computation.1 | async-start | bytes 4194304 | tf_op jit(solution)/shard_map/all_to_all | solution.py:157
  163.3 1.4 copy-start.26
  174.0 4.6 copy-start.15
  178.6 5.9 %copy-start.1 = (f32[16,65536]{1,0:T(8,128)S(1)}, f32[16,65536]{1,0:T(8,128)}, u32[]{:S(2)}) copy-start(f32[16,65536]{1,0:T(8,128)} %reshape.270) | copy-start | bytes 12582916 | tf_op jit(solution)/shard_map/while
  178.6 5.9 %copy-start.16 = (f32[8,64]{1,0:T(8,128)S(1)}, f32[8,64]{1,0:T(8,128)}, u32[]{:S(2)}) copy-start(f32[8,64]{1,0:T(8,128)} %get-tuple-element.367) | copy-start | bytes 6148 | tf_op jit(solution)/shard_map/while
  187.5 1.4 copy-start.26
  198.1 4.6 copy-start.15
  202.8 6.5 %copy-start.1 = (f32[16,65536]{1,0:T(8,128)S(1)}, f32[16,65536]{1,0:T(8,128)}, u32[]{:S(2)}) copy-start(f32[16,65536]{1,0:T(8,128)} %reshape.270) | copy-start | bytes 12582916 | tf_op jit(solution)/shard_map/while
  202.8 6.5 %copy-start.16 = (f32[8,64]{1,0:T(8,128)S(1)}, f32[8,64]{1,0:T(8,128)}, u32[]{:S(2)}) copy-start(f32[8,64]{1,0:T(8,128)} %get-tuple-element.367) | copy-start | bytes 6148 | tf_op jit(solution)/shard_map/while
  212.3 1.4 copy-start.26
  223.0 4.6 copy-start.15
  227.6 6.5 %copy-start.1 = (f32[16,65536]{1,0:T(8,128)S(1)}, f32[16,65536]{1,0:T(8,128)}, u32[]{:S(2)}) copy-start(f32[16,65536]{1,0:T(8,128)} %reshape.270) | copy-start | bytes 12582916 | tf_op jit(solution)/shard_map/while
  227.6 6.5 %copy-start.16 = (f32[8,64]{1,0:T(8,128)S(1)}, f32[8,64]{1,0:T(8,128)}, u32[]{:S(2)}) copy-start(f32[8,64]{1,0:T(8,128)} %get-tuple-element.367) | copy-start | bytes 6148 | tf_op jit(solution)/shard_map/while
  237.1 1.4 copy-start.26
  247.8 4.6 copy-start.15
  252.4 6.5 %copy-start.1 = (f32[16,65536]{1,0:T(8,128)S(1)}, f32[16,65536]{1,0:T(8,128)}, u32[]{:S(2)}) copy-start(f32[16,65536]{1,0:T(8,128)} %reshape.270) | copy-start | bytes 12582916 | tf_op jit(solution)/shard_map/while
  252.5 6.5 %copy-start.16 = (f32[8,64]{1,0:T(8,128)S(1)}, f32[8,64]{1,0:T(8,128)}, u32[]{:S(2)}) copy-start(f32[8,64]{1,0:T(8,128)} %get-tuple-element.367) | copy-start | bytes 6148 | tf_op jit(solution)/shard_map/while
  272.4 2.2 copy-start.3
  295.4 5.3 %copy-start.9 = (f32[8,512,128]{2,1,0:T(8,128)S(1)}, f32[8,512,128]{2,1,0:T(8,128)}, u32[]{:S(2)}) copy-start(f32[8,512,128]{2,1,0:T(8,128)} %convolution_subtract_fusion.1) | copy-start | bytes 6291460
  295.4 5.3 %copy-start.10 = (f32[8,512,128]{2,1,0:T(8,128)S(1)}, f32[8,512,128]{2,1,0:T(8,128)}, u32[]{:S(2)}) copy-start(f32[8,512,128]{2,1,0:T(8,128)} %convolution_add_fusion.1) | copy-start | bytes 6291460
  295.4 5.3 %copy-start.11 = (f32[8,512,128]{2,1,0:T(8,128)S(1)}, f32[8,512,128]{2,1,0:T(8,128)}, u32[]{:S(2)}) copy-start(f32[8,512,128]{2,1,0:T(8,128)} %fusion.58) | copy-start | bytes 6291460
  306.0 2.6 copy-start.2
  315.2 48.8 %all-to-all-start.4 = ((f32[8,128,512]{2,0,1:T(8,128)}), f32[8,128,512]{2,0,1:T(8,128)}, u32[]{:S(2)}, u32[]{:S(2)}) async-start(f32[8,128,512]{2,0,1:T(8,128)} %copy.215), calls=%async_computation.4 | async-start | bytes 4194304 | tf_op jit(solution)/shard_map/all_to_all | solution.py:197
  332.5 41.3 %copy-start.20 = (f32[128,8]{0,1:T(8,128)S(1)}, f32[128,8]{0,1:T(8,128)}, u32[]{:S(2)}) copy-start(f32[128,8]{0,1:T(8,128)} %get-tuple-element.243) | copy-start | bytes 12292
  364.0 52.2 %all-to-all-start.3 = ((f32[8,128,512]{2,0,1:T(8,128)}), f32[8,128,512]{2,0,1:T(8,128)S(1)}, u32[]{:S(2)}, u32[]{:S(2)}) async-start(f32[8,128,512]{2,0,1:T(8,128)} %copy.210), calls=%async_computation.3 | async-start | bytes 4194304 | tf_op jit(solution)/shard_map/all_to_all | solution.py:196
  373.8 99.6 %reduce-scatter.3.cloned.1.call-start = ((), (), s32[]{:S(2)}) async-start(), calls=%async_computation.9 | async-start | bytes 3145728 | tf_op jit(solution)/shard_map/reduce_scatter | solution.py:207
  374.2 3.0 copy-start.18
  416.3 4.6 copy-start.4
  416.3 4.6 copy-start.5
  460.1 1.4 copy-start.8
  460.1 1.4 copy-start.22
  465.3 8.0 %copy-start.13 = (bf16[512,512]{1,0:T(8,128)(2,1)S(1)}, bf16[512,512]{1,0:T(8,128)(2,1)}, u32[]{:S(2)}) copy-start(bf16[512,512]{1,0:T(8,128)(2,1)} %param.16) | copy-start | bytes 1572868
  465.3 23.4 %all-gather.5.cloned.1.call-start = ((), (), s32[]{:S(2)}) async-start(), calls=%async_computation.10 | async-start | bytes 1572864 | tf_op jit(solution)/shard_map/all_gather | solution.py:220
  478.4 38.3 %reduce-scatter.5.cloned.1.call-start = ((), (), s32[]{:S(2)}) async-start(), calls=%async_computation.11 | async-start | bytes 3145728 | tf_op jit(solution)/shard_map/reduce_scatter | solution.py:225
  (5 other events, 3.6 us)
Sparse Core Ops, SparseCore 0:
  8.9 11.7 all-gather.2
  465.5 7.8 reduce-scatter.2
  478.5 10.1 all-gather.4
  505.9 10.7 reduce-scatter.4
where the time goes:
time: 532 us; the launch traced here: 526 us
  waiting for transfers between devices  165 us (31%)
  matrix products  155 us (29%)
  local copies, waits for them, and re-layouts  76.8 us (14%)
  starting transfers between devices  44.6 us (8%)
  blocking collectives  37.7 us (7%)
  other arithmetic  27.5 us (5%)
  between operations  13.8 us (3%)
  loops' own time  5.99 us (1%)
    dot_general x12, matrix products, contract(): jnp.einsum('kn,anc->akc', matrix, operand, precision=HIGH, preferred_elem...  46.7 us
    all_to_all x1, waiting for transfers between devices, per_device(): lax.all_to_all(signal_imag, 'seq', split_axis=0, concat_axis=1, tiled=True)  36.4 us
    all_to_all x1, blocking collectives, per_device(): lax.all_to_all(result, 'seq', split_axis=0, concat_axis=1, tiled=True)  35.2 us
    all_to_all x1, waiting for transfers between devices, per_device(): lax.all_to_all(product_real, 'seq', split_axis=1, concat_axis=0, tiled=True)  34.6 us
    all_to_all x1, waiting for transfers between devices, per_device(): lax.all_to_all(product_imag, 'seq', split_axis=1, concat_axis=0, tiled=True)  31.5 us
    dot_general x5, matrix products, forward_rows(): jnp.dot(cosine_rows, flat_rows, precision=HIGH, preferred_element_type=jn...  31.1 us
    all_to_all x1, waiting for transfers between devices, per_device(): lax.all_to_all(gated_value.reshape(blocks, N1, channels), 'seq', split_ax...  23 us
    dot_general x4, matrix products, filter_hidden(): lax.dot_general(filt_mid, first_layer, (((0,), (0,)), ((), ())), preferre...  17.9 us
  transfers between devices with their start and end apart: 10, of which 9 were waited for; matrix products, arithmetic and copies ran while one was open for 29% of the time, Pallas kernels for 0%

commit v1 on v0

v1 whole, which is shorter than its diff:
```python
import functools

import jax
import jax.numpy as jnp
import ml_dtypes
import numpy as np
from jax import lax
from jax.experimental import pallas as pl
from jax.experimental.pallas import tpu as pltpu
from jax.sharding import PartitionSpec as P

BANDS = 12
KSHORT = 3
LANES = 128
HALO = 16
EPS = 1e-05
PI_HIGH = 3.140625
PI_LOW = 9.67653589793e-4
F32 = jnp.float32
BF16 = jnp.bfloat16
VMEM_BYTES = 60 * 1024 * 1024


def matmul(left, right):
    return jnp.dot(left, right, preferred_element_type=F32)


def split_parts(values):
    high = values.astype(BF16)
    return high, (values - high.astype(F32)).astype(BF16)


def split_table(table):
    high = table.astype(np.float32).astype(ml_dtypes.bfloat16)
    low = (table - high.astype(np.float64)).astype(np.float32).astype(ml_dtypes.bfloat16)
    return high, low


def transform_tables(length):
    rows = length // LANES
    period = 2 * rows
    full = 2 * length
    kept = rows + 1
    padded = -(-kept // 8) * 8
    k2 = np.arange(padded)
    valid = (k2 < kept).astype(np.float64)[:, None]
    n2 = np.arange(rows)
    n1 = np.arange(LANES)
    first = 2 * np.pi / period * (k2[:, None] * n2[None, :] % period)
    forward = np.concatenate([np.cos(first) * valid, -np.sin(first) * valid], 0)
    weight = np.where((k2 == 0) | (k2 == rows), 1.0, 2.0)[:, None] * valid
    inverse = np.concatenate([np.cos(first) * weight, -np.sin(first) * weight], 0).T
    turn = 2 * np.pi / full * (k2[:, None] * n1[None, :] % full)
    second = 2 * np.pi / LANES * (n1[:, None] * n1[None, :] % LANES)
    cos2, sin2 = np.cos(second), np.sin(second)
    mid = np.concatenate(
        [np.concatenate([cos2, -sin2], 1), np.concatenate([sin2, cos2], 1)], 0
    )
    back = np.concatenate(
        [np.concatenate([cos2, sin2], 1), np.concatenate([-sin2, cos2], 1)], 0
    ) / full
    f_high, f_low = split_table(forward)
    i_high, i_low = split_table(inverse)
    return {
        "forward2": np.concatenate([f_high, f_low], 1),
        "forward3": np.concatenate([f_high, f_high, f_low], 1),
        "inverse3": np.concatenate([i_high, i_high, i_low], 1),
        "turn_cos": np.tile(np.cos(turn), (1, 2)).astype(np.float32),
        "turn_sin": np.tile(np.sin(turn), (1, 2)).astype(np.float32),
        "mid": np.stack(split_table(mid)),
        "back": np.stack(split_table(back)),
    }


def sine(values):
    count = jnp.floor(values * (1.0 / np.pi) + 0.5)
    rest = (values - count * PI_HIGH) - count * PI_LOW
    half = count * 0.5
    sign = 1.0 - 4.0 * (half - jnp.floor(half))
    return sign * sine_poly(rest)


def sine_poly(rest):
    square = rest * rest
    poly = -2.5052108385441720e-08
    poly = poly * square + 2.7557319223985893e-06
    poly = poly * square - 1.9841269841269841e-04
    poly = poly * square + 8.3333333333333333e-03
    poly = poly * square - 1.6666666666666667e-01
    return rest + rest * square * poly


def sine_turns(turns):
    count = jnp.floor(turns * 2.0 + 0.5)
    rest = (turns - count * 0.5) * (2.0 * np.pi)
    half = count * 0.5
    sign = 1.0 - 4.0 * (half - jnp.floor(half))
    return sign * sine_poly(rest)


def rows_to_spectrum(load_pair, group, table_ref, turn_cos, turn_sin, mid_ref, padded):
    stacked = []
    for pair in range(group // 2):
        first = matmul(table_ref[...], load_pair(pair))
        real, imag = first[:padded], first[padded:]
        turned_real = real * turn_cos + imag * turn_sin
        turned_imag = imag * turn_cos - real * turn_sin
        for side in range(2):
            lanes = slice(side * LANES, (side + 1) * LANES)
            stacked.append(jnp.concatenate([turned_real[:, lanes], turned_imag[:, lanes]], 1))
    high, low = split_parts(jnp.concatenate(stacked, 0))
    return matmul(high, mid_ref[0]) + matmul(low, mid_ref[0]) + matmul(high, mid_ref[1])


def project_kernel(me_ref, *refs, pieces, tokens, width):
    x_refs, refs = refs[:pieces], refs[pieces:]
    halo_refs, refs = refs[:pieces], refs[pieces:]
    gain_ref, w_in_ref, w_value_ref, taps_ref, normed_ref, gated_ref, proj_ref = refs
    me = me_ref[0]
    places = [lax.rem(me + p, pieces) for p in range(pieces)]
    total = pieces * width

    def norm_rows(parts, start, size):
        values = [part.astype(F32) for part in parts]
        mean = sum(jnp.sum(v, axis=1, keepdims=True) for v in values) / total
        centered = [v - mean for v in values]
        spread = sum(jnp.sum(c * c, axis=1, keepdims=True) for c in centered) / total
        scale = lax.rsqrt(spread + EPS)
        for p in range(pieces):
            gain = gain_ref[places[p]]
            normed_ref[p, start : start + size, :] = (centered[p] * scale * gain).astype(BF16)

    norm_rows([ref[...] for ref in halo_refs], 0, HALO)
    chunk = 128
    for start in range(0, tokens, chunk):
        norm_rows([ref[start : start + chunk, :] for ref in x_refs], HALO + start, chunk)
    step = min(width, 256)
    for col in range(0, width, step):
        cols = slice(col, col + step)
        for role, w_ref in enumerate((w_in_ref, w_value_ref)):
            sums = 0.0
            for p in range(pieces):
                rows = pl.ds(pl.multiple_of(places[p] * width, width), width)
                sums = sums + matmul(normed_ref[p], w_ref[0, rows, cols])
            proj_ref[role] = sums.astype(BF16).astype(F32)
        shorted = []
        for role in range(2):
            value = taps_ref[0, role + 1 : role + 2, cols] * proj_ref[role, HALO : HALO + tokens, :]
            for lag in range(1, KSHORT):
                value = (
                    value
                    + taps_ref[lag, role + 1 : role + 2, cols]
                    * proj_ref[role, HALO - lag : HALO - lag + tokens, :]
                )
            shorted.append(value)
        gated = shorted[1] * shorted[0]
        gated_ref[cols, :] = gated.T.astype(BF16)


def gate_kernel(me_ref, normed_ref, *refs, pieces, share, width):
    w_refs, refs = refs[:pieces], refs[pieces:]
    tap_refs, refs = refs[:pieces], refs[pieces:]
    gate_ref, proj_ref = refs
    me = me_ref[0]
    places = [lax.rem(me + p, pieces) for p in range(pieces)]
    own = pl.ds(pl.multiple_of(me * share, 16), share + HALO)
    for out in range(pieces):
        sums = 0.0
        for p in range(pieces):
            rows = pl.ds(pl.multiple_of(places[p] * width, width), width)
            sums = sums + matmul(normed_ref[p, own, :], w_refs[out][0, rows, :])
        proj_ref[...] = sums.astype(BF16).astype(F32)
        value = tap_refs[out][0, 0:1, :] * proj_ref[HALO : HALO + share, :]
        for lag in range(1, KSHORT):
            value = value + tap_refs[out][lag, 0:1, :] * proj_ref[HALO - lag : HALO - lag + share, :]
        gate_ref[out] = value.T


def filter_kernel(
    in_ref, bias_ref, mid_w_ref, out_w_ref, decay_ref, forward_ref, cos_ref, sin_ref, mid_ref,
    spectrum_ref, response_ref, *, length, own, group, padded
):
    rows = length // LANES
    chunk = min(1024, length)
    feats = in_ref.shape[1]
    row_ids = lax.broadcasted_iota(jnp.int32, (feats, chunk), 0)
    band = jnp.where(row_ids > BANDS, row_ids - (BANDS + 1), row_ids - 1)
    band = jnp.clip(band, 0, BANDS - 1)
    quarter = jnp.where(row_ids <= BANDS, 0.25, 0.0)
    for start in range(0, length, chunk):
        places = lax.broadcasted_iota(jnp.int32, (feats, chunk), 1) + start
        phase = lax.shift_left(places, band) & (length - 1)
        turns = phase.astype(F32) * (1.0 / length)
        waves = sine_turns(turns + quarter)
        features = jnp.where(
            row_ids == 0,
            places.astype(F32) / length,
            jnp.where(row_ids <= 2 * BANDS, waves, 0.0),
        ).astype(BF16)
        first = sine(matmul(in_ref[...], features) + bias_ref[...]).astype(BF16)
        second = sine(matmul(mid_w_ref[...], first)).astype(BF16)
        ramp = (lax.broadcasted_iota(jnp.int32, (1, chunk), 1) + start).astype(F32) / length
        response = matmul(out_w_ref[...], second) * jnp.exp(-decay_ref[...] * ramp)
        for part in range(chunk // LANES):
            row = start // LANES + part
            response_ref[pl.ds(row, own, stride=rows), :] = response[:, part * LANES : (part + 1) * LANES]

    def one_group(step, carry):
        def load_pair(pair):
            base = (step * group + 2 * pair) * rows
            both = [
                response_ref[pl.ds(pl.multiple_of(base + side * rows, 8), rows), :] for side in range(2)
            ]
            high, low = split_parts(jnp.concatenate(both, 1))
            return jnp.concatenate([high, low, high], 0)

        spectrum = rows_to_spectrum(
            load_pair, group, forward_ref, cos_ref[...], sin_ref[...], mid_ref, padded
        )
        spectrum_ref[pl.ds(pl.multiple_of(step * group * padded, 8), group * padded), :] = spectrum
        return carry

    lax.fori_loop(0, own // group, one_group, 0)


def convolve_kernel(
    x_ref, spectrum_ref, bias_ref, forward_ref, inverse_ref, cos_ref, sin_ref, mid_ref, back_ref,
    out_ref, signal_ref, result_ref, *, length, own, group, padded, tokens, places
):
    rows = length // LANES
    per_block = tokens // LANES
    for row in range(rows):
        block, part = divmod(row, per_block)
        values = x_ref[block, :, part * LANES : (part + 1) * LANES].astype(F32)
        signal_ref[pl.ds(row, own, stride=rows), :] = values
    turn_cos, turn_sin = cos_ref[...], sin_ref[...]

    def one_group(step, carry):
        def load_pair(pair):
            base = (step * group + 2 * pair) * rows
            both = [
                signal_ref[pl.ds(pl.multiple_of(base + side * rows, 8), rows), :] for side in range(2)
            ]
            values = jnp.concatenate(both, 1).astype(BF16)
            return jnp.concatenate([values, values], 0)

        signal = rows_to_spectrum(load_pair, group, forward_ref, turn_cos, turn_sin, mid_ref, padded)
        other = spectrum_ref[pl.ds(pl.multiple_of(step * group * padded, 8), group * padded), :]
        s_real, s_imag = signal[:, :LANES], signal[:, LANES:]
        f_real, f_imag = other[:, :LANES], other[:, LANES:]
        product = jnp.concatenate(
            [s_real * f_real - s_imag * f_imag, s_real * f_imag + s_imag * f_real], 1
        )
        high, low = split_parts(product)
        mixed = matmul(high, back_ref[0]) + matmul(low, back_ref[0]) + matmul(high, back_ref[1])
        for pair in range(group // 2):
            first = mixed[2 * pair * padded : (2 * pair + 1) * padded]
            second = mixed[(2 * pair + 1) * padded : (2 * pair + 2) * padded]
            real = jnp.concatenate([first[:, :LANES], second[:, :LANES]], 1)
            imag = jnp.concatenate([first[:, LANES:], second[:, LANES:]], 1)
            turned = jnp.concatenate(
                [real * turn_cos - imag * turn_sin, imag * turn_cos + real * turn_sin], 0
            )
            t_high, t_low = split_parts(turned)
            values = matmul(inverse_ref[...], jnp.concatenate([t_high, t_low, t_high], 0))
            base = (step * group + 2 * pair) * rows
            for side in range(2):
                result_ref[pl.ds(pl.multiple_of(base + side * rows, 8), rows), :] = values[
                    :, side * LANES : (side + 1) * LANES
                ]
        return carry

    lax.fori_loop(0, own // group, one_group, 0)
    bias = bias_ref[...]
    share_rows = per_block // places
    for row in range(rows):
        block, part = divmod(row, per_block)
        place, lane = divmod(part, share_rows)
        values = result_ref[pl.ds(row, own, stride=rows), :]
        values = values + bias * x_ref[block, :, part * LANES : (part + 1) * LANES].astype(F32)
        target = place * (rows // per_block) + block
        out_ref[target, :, lane * LANES : (lane + 1) * LANES] = values.astype(BF16)


def gelu(values):
    return values * (lax.erf(values * np.float32(0.5**0.5)) + 1.0) * 0.5


def tail_kernel(me_ref, z_ref, gate_ref, gain_ref, *refs, pieces, share, width, steps):
    x_refs, refs = refs[:pieces], refs[pieces:]
    mix_refs, refs = refs[:pieces], refs[pieces:]
    up_refs, refs = refs[:pieces], refs[pieces:]
    down_refs, refs = refs[:pieces], refs[pieces:]
    out_ref, sums_ref, normed_ref = refs
    me = me_ref[0]
    places = [lax.rem(me + p, pieces) for p in range(pieces)]
    total = pieces * width
    dims = (((0,), (0,)), ((), ()))

    @pl.when(pl.program_id(0) == 0)
    def _():
        sums = 0.0
        for p in range(pieces):
            mixed = (z_ref[places[p]].astype(F32) * gate_ref[p]).astype(BF16)
            sums = sums + lax.dot_general(mixed, mix_refs[p][...], dims, preferred_element_type=F32)
        sums_ref[...] = sums
        own = pl.ds(pl.multiple_of(me * share, 16), share)
        for p in range(pieces):
            cols = pl.ds(pl.multiple_of(places[p] * width, LANES), width)
            residual = x_refs[p][own, :].astype(F32) + sums_ref[:, cols]
            sums_ref[:, cols] = residual.astype(BF16).astype(F32)
        values = sums_ref[...]
        mean = jnp.sum(values, axis=1, keepdims=True) / total
        centered = values - mean
        spread = jnp.sum(centered * centered, axis=1, keepdims=True) / total
        normed_ref[...] = (centered * lax.rsqrt(spread + EPS) * gain_ref[...]).astype(BF16)

    sums = sums_ref[...]
    for p in range(pieces):
        hidden = gelu(matmul(normed_ref[...], up_refs[p][...])).astype(BF16)
        sums = sums + matmul(hidden, down_refs[p][...])
    sums_ref[...] = sums

    @pl.when(pl.program_id(0) == steps - 1)
    def _():
        for p in range(pieces):
            cols = pl.ds(pl.multiple_of(places[p] * width, LANES), width)
            out_ref[p] = sums_ref[:, cols].astype(BF16)


def call(kernel, out_shape, scratch=(), **extra):
    return pl.pallas_call(
        kernel,
        out_shape=out_shape,
        scratch_shapes=list(scratch),
        compiler_params=pltpu.CompilerParams(vmem_limit_bytes=VMEM_BYTES),
        **extra,
    )


def shape_of(shape, dtype):
    return jax.ShapeDtypeStruct(shape, dtype)


SCALAR = pl.BlockSpec(memory_space=pltpu.SMEM)
WHOLE = pl.BlockSpec(memory_space=pltpu.VMEM)


def per_device(
    layer_input, gain_first, in_weight, short_weight, filt_in, filt_bias, filt_mid, filt_out,
    decay_rate, conv_bias, out_weight, gain_second, up_weight, down_weight,
):
    tokens, width = layer_input.shape
    pieces = lax.axis_size("chan")
    groups = lax.axis_size("seq")
    seq_place = lax.axis_index("seq")
    chan_place = lax.axis_index("chan")
    model = pieces * width
    length = tokens * groups
    share = tokens // pieces
    own = width // groups
    me = chan_place.astype(jnp.int32).reshape(1)

    def turned(array, by):
        if by == 0:
            return array
        return lax.ppermute(array, "chan", [(i, (i - by) % pieces) for i in range(pieces)])

    def all_turned(array):
        return [turned(array, p) for p in range(pieces)]

    x_pieces = all_turned(layer_input)
    last_rows = layer_input[tokens - HALO :]
    halo_pieces = [
        lax.ppermute(
            last_rows,
            ("seq", "chan"),
            [
                (s * pieces + i, (s + 1) * pieces + (i - p) % pieces)
                for s in range(groups - 1)
                for i in range(pieces)
            ],
        )
        for p in range(pieces)
    ]
    by_role = jnp.transpose(in_weight, (1, 0, 2))
    gain_pieces = gain_first.reshape(pieces, 1, width)

    def role_spec(role):
        return pl.BlockSpec((1, model, width), lambda i, role=role: (role, 0, 0))

    def full_spec(shape):
        return pl.BlockSpec(shape, lambda i: (0,) * len(shape))

    normed, gated = call(
        functools.partial(project_kernel, pieces=pieces, tokens=tokens, width=width),
        (shape_of((pieces, tokens + HALO, width), BF16), shape_of((width, tokens), BF16)),
        [pltpu.VMEM((2, tokens + HALO, min(width, 256)), F32)],
        grid=(1,),
        in_specs=[SCALAR]
        + [full_spec((tokens, width))] * pieces
        + [full_spec((HALO, width))] * pieces
        + [full_spec((pieces, 1, width)), role_spec(1), role_spec(2), full_spec(short_weight.shape)],
        out_specs=(full_spec((pieces, tokens + HALO, width)), full_spec((width, tokens))),
    )(me, *x_pieces, *halo_pieces, gain_pieces, by_role, by_role, short_weight)

    regrouped = lax.all_to_all(
        gated.reshape(groups, own, tokens), "seq", split_axis=0, concat_axis=0, tiled=True
    )

    tables = transform_tables(length)
    padded = tables["turn_cos"].shape[0]
    rows = length // LANES
    group = min(8, own)
    feats = 2 * BANDS + 1
    in_columns = jnp.pad(filt_in, ((0, 32 - feats), (0, 0))).T
    own_out = lax.dynamic_slice_in_dim(filt_out, seq_place * own, own, 1).T
    own_decay = lax.dynamic_slice_in_dim(decay_rate, seq_place * own, own, 0)[:, None]
    own_bias = lax.dynamic_slice_in_dim(conv_bias, seq_place * own, own, 0)[:, None]
    spectrum = call(
        functools.partial(filter_kernel, length=length, own=own, group=group, padded=padded),
        shape_of((own * padded, 2 * LANES), F32),
        [pltpu.VMEM((own * rows, LANES), F32)],
    )(
        in_columns, filt_bias[:, None], filt_mid.T, own_out, own_decay,
        tables["forward3"], tables["turn_cos"], tables["turn_sin"], tables["mid"],
    )

    gate_weights = all_turned(by_role[:1])
    gate_taps = all_turned(short_weight[:, :1])
    mix_weights = all_turned(out_weight)
    up_weights = all_turned(up_weight)
    down_weights = all_turned(down_weight)
    gate = call(
        functools.partial(gate_kernel, pieces=pieces, share=share, width=width),
        shape_of((pieces, width, share), F32),
        [pltpu.VMEM((share + HALO, width), F32)],
        grid=(1,),
        in_specs=[SCALAR, full_spec((pieces, tokens + HALO, width))]
        + [full_spec((1, model, width))] * pieces
        + [full_spec((KSHORT, 1, width))] * pieces,
        out_specs=full_spec((pieces, width, share)),
    )(me, normed, by_role, *gate_weights[1:], *gate_taps)

    places = pieces if share % LANES == 0 else 1
    convolved = call(
        functools.partial(
            convolve_kernel, length=length, own=own, group=group, padded=padded, tokens=tokens, places=places
        ),
        shape_of((places * groups, own, tokens // places), BF16),
        [pltpu.VMEM((own * rows, LANES), F32), pltpu.VMEM((own * rows, LANES), F32)],
    )(
        regrouped, spectrum, own_bias, tables["forward2"], tables["inverse3"],
        tables["turn_cos"], tables["turn_sin"], tables["mid"], tables["back"],
    )
    if places != pieces:
        convolved = jnp.transpose(convolved.reshape(groups, own, pieces, share), (2, 0, 1, 3))
        convolved = convolved.reshape(pieces * groups, own, share)
    returned = lax.all_to_all(convolved, ("chan", "seq"), split_axis=0, concat_axis=0, tiled=True)
    returned = returned.reshape(pieces, width, share)

    hidden = up_weight.shape[1]
    block = min(512, hidden)
    steps = hidden // block
    results = call(
        functools.partial(tail_kernel, pieces=pieces, share=share, width=width, steps=steps),
        shape_of((pieces, share, width), BF16),
        [pltpu.VMEM((share, model), F32), pltpu.VMEM((share, model), BF16)],
        grid=(steps,),
        in_specs=[
            SCALAR,
            full_spec((pieces, width, share)),
            full_spec((pieces, width, share)),
            full_spec((1, model)),
        ]
        + [full_spec((tokens, width))] * pieces
        + [full_spec((width, model))] * pieces
        + [pl.BlockSpec((model, block), lambda i: (0, i))] * pieces
        + [pl.BlockSpec((block, model), lambda i: (i, 0))] * pieces,
        out_specs=full_spec((pieces, share, width)),
    )(
        me, returned, gate, gain_second[None, :], *x_pieces, *mix_weights, *up_weights, *down_weights,
    )
    received = [results[0]] + [
        lax.ppermute(results[p], "chan", [(i, (i + p) % pieces) for i in range(pieces)])
        for p in range(1, pieces)
    ]
    if pieces == 2:
        first = chan_place == 0
        return jnp.concatenate(
            [jnp.where(first, received[0], received[1]), jnp.where(first, received[1], received[0])], 0
        )
    block_out = jnp.zeros((tokens, width), BF16)
    for p in range(pieces):
        start = lax.rem(chan_place + pieces - p, pieces) * share
        block_out = lax.dynamic_update_slice_in_dim(block_out, received[p], start, 0)
    return block_out


def solution(mesh):
    placed = (
        P("seq", "chan"),
        P(),
        P(None, None, "chan"),
        P(None, None, "chan"),
        P(),
        P(),
        P(),
        P(None, "chan"),
        P("chan"),
        P("chan"),
        P("chan", None),
        P(),
        P(None, "chan"),
        P("chan", None),
    )
    return jax.shard_map(
        per_device, mesh=mesh, in_specs=placed, out_specs=P("seq", "chan"), check_vma=False
    )
```

time: 532 us -> 95.5 us (0.18); the launches traced: 526 us -> 94.8 us
  matrix products: 155 us -> 0 us
  waiting for transfers between devices: 165 us -> 13.8 us
  local copies, waits for them, and re-layouts: 76.8 us -> 12.9 us
  Pallas kernels: 0 us -> 43.5 us
  blocking collectives: 37.7 us -> 0 us
  other arithmetic: 27.5 us -> 1.82 us
  starting transfers between devices: 44.6 us -> 22.7 us
  between operations: 13.8 us -> 0.12 us
  loops' own time: 5.99 us -> 0 us
    dot_general x35 -> x0, matrix products: 155 us -> none  [the longest x12 46.7 us: contract(): jnp.einsum('kn,anc->akc', matrix, operand, precision=HIGH, preferred_elem...]
    all_to_all x5 -> x2, waiting for transfers between devices: 126 us -> 9.82 us  [the longest x1 9.82 us: per_device(): lax.all_to_all(convolved, ('chan', 'seq'), split_axis=0, concat_axis=0, t...]
    pallas_call x0 -> x5, Pallas kernels: none -> 43.5 us  [the longest x1 12.9 us: per_device(): call(functools.partial(tail_kernel, pieces=pieces, share=share, width=wid...]
    all_to_all x1 -> x0, blocking collectives: 35.2 us -> none  [per_device(): lax.all_to_all(result, 'seq', split_axis=0, concat_axis=1, tiled=True)]
    all_to_all x5 -> x2, starting transfers between devices: 40.6 us -> 13.4 us  [the longest x1 7.3 us: per_device(): lax.all_to_all(gated.reshape(groups, own, tokens), 'seq', split_axis=0, c...]
    reshape x6 -> x0, local copies, waits for them, and re-layouts: 20 us -> none  [the longest x4 15.7 us: forward_rows(): flat_rows = real_rows.reshape(real_rows.shape[0], -1)]
    all_gather x2 -> x0, waiting for transfers between devices: 18.9 us -> none  [the longest x1 10.1 us: per_device(): lax.all_gather(normed_part, 'chan', axis=1, tiled=True)]
    reduce_scatter x2 -> x0, waiting for transfers between devices: 18.2 us -> none  [the longest x1 10.9 us: per_device(): lax.psum_scatter(jnp.dot(hidden, down_weight, preferred_element_type=jnp....]
  transfers between devices with their start and end apart: 10 -> 11, of which waited for: 9 -> 4; matrix products, arithmetic and copies ran while one was open for 29% -> 9% of each run, Pallas kernels for 0% -> 32%
where the time goes in v1:
time: 95.5 us; the launch traced here: 94.8 us
  Pallas kernels  43.5 us (46%)
  starting transfers between devices  22.7 us (24%)
  waiting for transfers between devices  13.8 us (14%)
  local copies, waits for them, and re-layouts  12.9 us (14%)
  other arithmetic  1.82 us (2%)
    pallas_call x1, Pallas kernels, per_device(): call(functools.partial(tail_kernel, pieces=pieces, share=share, width=wid...  12.9 us
    pallas_call x1, Pallas kernels, per_device(): call(functools.partial(filter_kernel, length=length, own=own, group=group...  11.5 us
    pallas_call x1, Pallas kernels, per_device(): call(functools.partial(convolve_kernel, length=length, own=own, group=gro...  10.1 us
    all_to_all x1, waiting for transfers between devices, per_device(): lax.all_to_all(convolved, ('chan', 'seq'), split_axis=0, concat_axis=0, t...  9.82 us
    ppermute x2, starting transfers between devices, per_device(): lax.ppermute(last_rows, ('seq', 'chan'), [(s * pieces + i, (s + 1) * piec...  7.61 us
    all_to_all x1, starting transfers between devices, per_device(): lax.all_to_all(gated.reshape(groups, own, tokens), 'seq', split_axis=0, c...  7.3 us
    all_to_all x1, starting transfers between devices, per_device(): lax.all_to_all(convolved, ('chan', 'seq'), split_axis=0, concat_axis=0, t...  6.07 us
    pallas_call x1, Pallas kernels, per_device(): call(functools.partial(project_kernel, pieces=pieces, tokens=tokens, widt...  5.18 us
  transfers between devices with their start and end apart: 11, of which 4 were waited for; matrix products, arithmetic and copies ran while one was open for 9% of the time, Pallas kernels for 32%

profile of v1, /device:TPU:0, one launch (start us, length us, event | category | flops | bytes accessed | tf_op | source)
XLA Modules:
  0.0 94.8 jit_solution(11425400047824725514)
XLA Ops:
  0.0 0.5 collective-permute-start.6
  0.5 0.1 collective-permute-start.7
  0.5 0.4 collective-permute-start
  1.0 0.7 slice.15
  1.7 4.4 %collective-permute-start.1 = (bf16[16,512]{1,0:T(8,128)(2,1)S(1)}, bf16[16,512]{1,0:T(8,128)(2,1)S(1)}, u32[]{:S(2)}, u32[]{:S(2)}) collective-permute-start(bf16[16,512]{1,0:T(8,128)(2,1)S(1)} %slice.15), channel_id=1, source_target_pairs={{0,2},{1,3},{2,4},{3,5},{4,6},{5,7},{6,8},{7,9},{8,10},{9,11},{10,... | collective-permute-start | bytes 49160 | tf_op jit(solution)/shard_map/ppermute | solution.py:375
  6.1 3.2 %collective-permute-start.2 = (bf16[16,512]{1,0:T(8,128)(2,1)S(1)}, bf16[16,512]{1,0:T(8,128)(2,1)S(1)}, u32[]{:S(2)}, u32[]{:S(2)}) collective-permute-start(bf16[16,512]{1,0:T(8,128)(2,1)S(1)} %slice.15), channel_id=1, source_target_pairs={{0,3},{1,2},{2,5},{3,4},{4,7},{5,6},{6,9},{7,8},{8,11},{9,10},{10,... | collective-permute-start | bytes 49160 | tf_op jit(solution)/shard_map/ppermute | solution.py:375
  9.3 0.0 collective-permute-done.1.refs_2_
  9.3 1.4 %collective-permute-done.2.refs_3_ = bf16[16,512]{1,0:T(8,128)(2,1)S(1)} collective-permute-done((bf16[16,512]{1,0:T(8,128)(2,1)S(1)}, bf16[16,512]{1,0:T(8,128)(2,1)S(1)}, u32[]{:S(2)}, u32[]{:S(2)}) %collective-permute-start.2) | collective-permute-done | bytes 16416 | tf_op jit(solution)/shard_map/ppermute | solution.py:375
  10.7 0.0 collective-permute-done.refs_1_
  10.8 0.6 copy-done.7
  11.3 0.2 copy-done.2
  11.5 5.2 %shard_map.199 = (bf16[2,528,512]{2,1,0:T(8,128)(2,1)}, bf16[512,512]{1,0:T(8,128)(2,1)}) custom-call(s32[1]{0:T(128)} %bitcast.me_ref, bf16[512,512]{1,0:T(8,128)(2,1)} %refs_0_.3, bf16[512,512]{1,0:T(8,128)(2,1)} %copy-done.2, bf16[16,512]{1,0:T(8,128)(2,1)} %copy-done.6, bf16[16,512]{1,0:T(8,128)(2,1)} %copy-done.7, f32[2,1,512]{2,1,0:T(1,128)} %bitcast.31, ...), custom_call_target="tpu_custom_call" | custom-call | tf_op jit(solution)/shard_map/pallas_call | solution.py:395
  16.7 7.3 %all-to-all-start = ((bf16[16,32,512]{2,1,0:T(8,128)(2,1)}), bf16[16,32,512]{2,1,0:T(8,128)(2,1)S(1)}, u32[]{:S(2)}, u32[]{:S(2)}) async-start(bf16[16,32,512]{2,1,0:T(8,128)(2,1)} %bitcast.28), calls=%async_computation | async-start | bytes 1048576 | tf_op jit(solution)/shard_map/all_to_all | solution.py:407
  24.0 1.3 %slice.20 = bf16[1,1024,512]{2,1,0:T(8,128)(2,1)S(1)} slice(bf16[3,1024,512]{2,1,0:T(8,128)(2,1)} %bitcast.25), slice={[0:1], [0:1024], [0:512]} | slice | bytes 2097152 | tf_op jit(solution)/shard_map/slice | solution.py:429
  25.3 0.1 collective-permute-start.3
  25.4 0.5 collective-permute-start.5
  25.9 0.1 copy.22
  26.0 0.8 dynamic-slice_bitcast_fusion.1
  26.8 0.1 constant_dynamic-slice_fusion
  26.9 0.6 pad_bitcast_fusion.in_ref
  27.5 0.8 dynamic-slice_bitcast_fusion
  28.2 0.7 copy.28
  28.9 0.7 copy.26.decay_ref
  29.6 0.7 copy.25.bias_ref
  30.3 0.7 copy.23
  31.0 0.7 copy.27.bias_ref
  31.7 11.5 %shard_map.200.spectrum_ref = f32[2304,256]{1,0:T(8,128)} custom-call(bf16[64,32]{1,0:T(8,128)(2,1)} %pad_bitcast_fusion.in_ref, f32[64,1]{1,0:T(8,128)} %copy.25.bias_ref, bf16[64,64]{1,0:T(8,128)(2,1)} %bitcast.29, bf16[32,64]{1,0:T(8,128)(2,1)} %bitcast.30, f32[32,1]{1,0:T(8,128)} %copy.26.decay_ref, bf16[144,192]{1,0:T(8,128)(2,1)} %constant.30.clone.forward_ref, ...), custom_call_target="tpu_custom_call" | custom-call | tf_op jit(solution)/shard_map/pallas_call | solution.py:420
  43.1 0.0 all-to-all-done.x_ref
  43.1 0.8 copy-done.1
  43.9 10.1 %shard_map.201 = bf16[32,32,256]{2,1,0:T(8,128)(2,1)} custom-call(bf16[16,32,512]{2,1,0:T(8,128)(2,1)} %copy-done.1, f32[2304,256]{1,0:T(8,128)} %shard_map.200.spectrum_ref, f32[32,1]{1,0:T(8,128)} %copy.27.bias_ref, bf16[144,128]{1,0:T(8,128)(2,1)} %constant.34.clone.forward_ref, bf16[64,432]{1,0:T(8,128)(2,1)} %constant.35.clone.inverse_ref, ...), custom_call_target="tpu_custom_call" | custom-call | tf_op jit(solution)/shard_map/pallas_call | solution.py:446
  54.0 6.1 %all-to-all-start.1 = ((bf16[32,32,256]{2,1,0:T(8,128)(2,1)}), bf16[32,32,256]{2,1,0:T(8,128)(2,1)S(1)}, u32[]{:S(2)}, u32[]{:S(2)}) async-start(bf16[32,32,256]{2,1,0:T(8,128)(2,1)} %shard_map.201), calls=%async_computation.1 | async-start | bytes 1048576 | tf_op jit(solution)/shard_map/all_to_all | solution.py:459
  60.1 0.7 slice.17.refs_2_
  60.8 0.1 collective-permute-start.4
  60.9 1.1 %collective-permute-done.4.refs_3_ = f32[3,1,512]{2,1,0:T(1,128)S(1)} collective-permute-done((f32[3,1,512]{2,1,0:T(1,128)S(1)}, f32[3,1,512]{2,1,0:T(1,128)S(1)}, u32[]{:S(2)}, u32[]{:S(2)}) %collective-permute-start.4) | collective-permute-done | bytes 6176 | tf_op jit(solution)/shard_map/ppermute | solution.py:367
  62.0 0.0 collective-permute-done.3.refs_1_
  62.0 0.6 copy-done.10
  62.6 0.4 copy-done.4
  63.0 3.9 %shard_map.202.gate_ref = f32[2,512,256]{2,1,0:T(8,128)} custom-call(s32[1]{0:T(128)} %bitcast.me_ref, bf16[2,528,512]{2,1,0:T(8,128)(2,1)} %get-tuple-element.8.normed_ref, bf16[3,1024,512]{2,1,0:T(8,128)(2,1)} %bitcast.26, bf16[1,1024,512]{2,1,0:T(8,128)(2,1)} %copy-done.4, f32[3,1,512]{2,1,0:T(1,128)} %copy-done.5, f32[3,1,512]{2,1,0:T(1,128)} %copy-done.10), custom_call_target="tpu_custom_call" | custom-call | tf_op jit(solution)/shard_map/pallas_call | solution.py:434
  66.9 9.8 %all-to-all-done.1 = bf16[32,32,256]{2,1,0:T(8,128)(2,1)S(1)} async-done(((bf16[32,32,256]{2,1,0:T(8,128)(2,1)}), bf16[32,32,256]{2,1,0:T(8,128)(2,1)S(1)}, u32[]{:S(2)}, u32[]{:S(2)}) %all-to-all-start.1) | async-done | bytes 524320 | tf_op jit(solution)/shard_map/all_to_all | solution.py:459
  76.7 0.0 collective-permute-done.6.refs_5_
  76.8 0.0 collective-permute-done.7.refs_7_
  76.8 0.8 copy-done.3
  77.6 12.9 %shard_map.203 = bf16[2,256,512]{2,1,0:T(8,128)(2,1)} custom-call(s32[1]{0:T(128)} %bitcast.me_ref, bf16[2,512,256]{2,1,0:T(8,128)(2,1)} %bitcast.27, f32[2,512,256]{2,1,0:T(8,128)} %shard_map.202.gate_ref, f32[1,1024]{1,0:T(1,128)} %bitcast.32, bf16[512,512]{1,0:T(8,128)(2,1)} %refs_0_.3, bf16[512,512]{1,0:T(8,128)(2,1)} %copy-done.2, ...), custom_call_target="tpu_custom_call" | custom-call | tf_op jit(solution)/shard_map/pallas_call | solution.py:465
  90.4 1.0 %slice_bitcast_fusion = bf16[256,512]{1,0:T(8,128)(2,1)S(1)} fusion(bf16[2,256,512]{2,1,0:T(8,128)(2,1)} %shard_map.203), kind=kLoop, calls=%fused_computation.1 | loop fusion | bytes 524288 | tf_op jit(solution)/shard_map/squeeze | solution.py:485
  91.4 0.1 collective-permute-start.8
  91.5 1.5 %collective-permute-done.8 = bf16[256,512]{1,0:T(8,128)(2,1)S(1)} collective-permute-done((bf16[256,512]{1,0:T(8,128)(2,1)S(1)}, bf16[256,512]{1,0:T(8,128)(2,1)S(1)}, u32[]{:S(2)}, u32[]{:S(2)}) %collective-permute-start.8) | collective-permute-done | bytes 262176 | tf_op jit(solution)/shard_map/ppermute | solution.py:485
  93.0 1.0 %broadcast_select_fusion.1 = (bf16[256,512]{1,0:T(8,128)(2,1)S(1)}, bf16[256,512]{1,0:T(8,128)(2,1)S(1)}) fusion(bf16[256,512]{1,0:T(8,128)(2,1)S(1)} %collective-permute-done.8, pred[]{:T(512)S(6)} %eq.3, bf16[2,256,512]{2,1,0:T(8,128)(2,1)} %shard_map.203), kind=kLoop, calls=%fused_computation.4 | loop fusion | flops 262144 | bytes 1048577 | tf_op jit(solution)/shard_map/jit(_where)/select_n | solution.py:491
  94.0 0.8 pad_maximum_fusion
  (19 shorter events, 0.0 us)
Async XLA Ops:
  0.0 26.8 %copy-start = (bf16[64,512]{1,0:T(8,128)(2,1)S(1)}, bf16[64,512]{1,0:T(8,128)(2,1)}, u32[]{:S(2)}) copy-start(bf16[64,512]{1,0:T(8,128)(2,1)} %param.28) | copy-start | bytes 196612
  0.0 76.7 %collective-permute-start.6 = (bf16[1024,2048]{1,0:T(8,128)(2,1)}, bf16[1024,2048]{1,0:T(8,128)(2,1)}, u32[]{:S(2)}, u32[]{:S(2)}) collective-permute-start(bf16[1024,2048]{1,0:T(8,128)(2,1)} %refs_4_.1), channel_id=1, source_target_pairs={{0,1},{1,0},{2,3},{3,2},{4,5},{5,4},{6,7},{7,6},{8,9},{9,8},{10,11... | collective-permute-start | bytes 12582920 | tf_op jit(solution)/shard_map/ppermute | solution.py:367
  0.5 76.3 %collective-permute-start.7 = (bf16[2048,1024]{1,0:T(8,128)(2,1)}, bf16[2048,1024]{1,0:T(8,128)(2,1)}, u32[]{:S(2)}, u32[]{:S(2)}) collective-permute-start(bf16[2048,1024]{1,0:T(8,128)(2,1)} %refs_6_.1), channel_id=1, source_target_pairs={{0,1},{1,0},{2,3},{3,2},{4,5},{5,4},{6,7},{7,6},{8,9},{9,8},{10,11... | collective-permute-start | bytes 12582920 | tf_op jit(solution)/shard_map/ppermute | solution.py:367
  0.5 10.2 %collective-permute-start = (bf16[512,512]{1,0:T(8,128)(2,1)}, bf16[512,512]{1,0:T(8,128)(2,1)S(1)}, u32[]{:S(2)}, u32[]{:S(2)}) collective-permute-start(bf16[512,512]{1,0:T(8,128)(2,1)} %refs_0_.3), channel_id=1, source_target_pairs={{0,1},{1,0},{2,3},{3,2},{4,5},{5,4},{6,7},{7,6},{8,9},{9,8},{10,11... | collective-permute-start | bytes 1572872 | tf_op jit(solution)/shard_map/ppermute | solution.py:367
  1.7 7.6 %collective-permute-start.1 = (bf16[16,512]{1,0:T(8,128)(2,1)S(1)}, bf16[16,512]{1,0:T(8,128)(2,1)S(1)}, u32[]{:S(2)}, u32[]{:S(2)}) collective-permute-start(bf16[16,512]{1,0:T(8,128)(2,1)S(1)} %slice.15), channel_id=1, source_target_pairs={{0,2},{1,3},{2,4},{3,5},{4,6},{5,7},{6,8},{7,9},{8,10},{9,11},{10,... | collective-permute-start | bytes 49160 | tf_op jit(solution)/shard_map/ppermute | solution.py:375
  6.1 4.6 %collective-permute-start.2 = (bf16[16,512]{1,0:T(8,128)(2,1)S(1)}, bf16[16,512]{1,0:T(8,128)(2,1)S(1)}, u32[]{:S(2)}, u32[]{:S(2)}) collective-permute-start(bf16[16,512]{1,0:T(8,128)(2,1)S(1)} %slice.15), channel_id=1, source_target_pairs={{0,3},{1,2},{2,5},{3,4},{4,7},{5,6},{6,9},{7,8},{8,11},{9,10},{10,... | collective-permute-start | bytes 49160 | tf_op jit(solution)/shard_map/ppermute | solution.py:375
  9.3 1.4 %copy-start.6 = (bf16[16,512]{1,0:T(8,128)(2,1)}, bf16[16,512]{1,0:T(8,128)(2,1)S(1)}, u32[]{:S(2)}) copy-start(bf16[16,512]{1,0:T(8,128)(2,1)S(1)} %collective-permute-done.1.refs_2_) | copy-start | bytes 49156
  10.7 0.6 copy-start.7
  10.7 0.8 copy-start.2
  11.5 14.4 %copy-start.9 = (bf16[25,64]{1,0:T(8,128)(2,1)S(1)}, bf16[25,64]{1,0:T(8,128)(2,1)}, u32[]{:S(2)}) copy-start(bf16[25,64]{1,0:T(8,128)(2,1)} %param.25) | copy-start | bytes 9604
  11.5 18.0 %copy-start.11 = (f32[64]{0:T(128)S(1)}, f32[64]{0:T(128)}, u32[]{:S(2)}) copy-start(f32[64]{0:T(128)} %param.26) | copy-start | bytes 772
  11.5 18.8 %copy-start.8 = (bf16[64,64]{1,0:T(8,128)(2,1)S(1)}, bf16[64,64]{1,0:T(8,128)(2,1)}, u32[]{:S(2)}) copy-start(bf16[64,64]{1,0:T(8,128)(2,1)} %param.27) | copy-start | bytes 24580
  16.7 26.4 %all-to-all-start = ((bf16[16,32,512]{2,1,0:T(8,128)(2,1)}), bf16[16,32,512]{2,1,0:T(8,128)(2,1)S(1)}, u32[]{:S(2)}, u32[]{:S(2)}) async-start(bf16[16,32,512]{2,1,0:T(8,128)(2,1)} %bitcast.28), calls=%async_computation | async-start | bytes 1048576 | tf_op jit(solution)/shard_map/all_to_all | solution.py:407
  25.3 36.7 %collective-permute-start.3 = (bf16[1,1024,512]{2,1,0:T(8,128)(2,1)S(1)}, bf16[1,1024,512]{2,1,0:T(8,128)(2,1)S(1)}, u32[]{:S(2)}, u32[]{:S(2)}) collective-permute-start(bf16[1,1024,512]{2,1,0:T(8,128)(2,1)S(1)} %slice.20), channel_id=1, source_target_pairs={{0,1},{1,0},{2,3},{3,2},{4,5},{5,4},{6,7},{7,6},{8,9},{9,8},{10,11... | collective-permute-start | bytes 3145736 | tf_op jit(solution)/shard_map/ppermute | solution.py:367
  25.4 41.5 %collective-permute-start.5 = (bf16[512,1024]{1,0:T(8,128)(2,1)}, bf16[512,1024]{1,0:T(8,128)(2,1)}, u32[]{:S(2)}, u32[]{:S(2)}) collective-permute-start(bf16[512,1024]{1,0:T(8,128)(2,1)} %refs_2_.1), channel_id=1, source_target_pairs={{0,1},{1,0},{2,3},{3,2},{4,5},{5,4},{6,7},{7,6},{8,9},{9,8},{10,11... | collective-permute-start | bytes 3145736 | tf_op jit(solution)/shard_map/ppermute | solution.py:367
  43.1 0.8 copy-start.1
  54.0 22.7 %all-to-all-start.1 = ((bf16[32,32,256]{2,1,0:T(8,128)(2,1)}), bf16[32,32,256]{2,1,0:T(8,128)(2,1)S(1)}, u32[]{:S(2)}, u32[]{:S(2)}) async-start(bf16[32,32,256]{2,1,0:T(8,128)(2,1)} %shard_map.201), calls=%async_computation.1 | async-start | bytes 1048576 | tf_op jit(solution)/shard_map/all_to_all | solution.py:459
  60.8 1.2 %copy-start.5 = (f32[3,1,512]{2,1,0:T(1,128)}, f32[3,1,512]{2,1,0:T(1,128)S(1)}, u32[]{:S(2)}) copy-start(f32[3,1,512]{2,1,0:T(1,128)S(1)} %slice.17.refs_2_) | copy-start | bytes 18436
  60.8 1.2 %collective-permute-start.4 = (f32[3,1,512]{2,1,0:T(1,128)S(1)}, f32[3,1,512]{2,1,0:T(1,128)S(1)}, u32[]{:S(2)}, u32[]{:S(2)}) collective-permute-start(f32[3,1,512]{2,1,0:T(1,128)S(1)} %slice.17.refs_2_), channel_id=1, source_target_pairs={{0,1},{1,0},{2,3},{3,2},{4,5},{5,4},{6,7},{7,6},{8,9},{9,8},{10,11... | collective-permute-start | bytes 18440 | tf_op jit(solution)/shard_map/ppermute | solution.py:367
  62.0 0.6 copy-start.10
  62.0 1.0 %copy-start.4 = (bf16[1,1024,512]{2,1,0:T(8,128)(2,1)}, bf16[1,1024,512]{2,1,0:T(8,128)(2,1)S(1)}, u32[]{:S(2)}) copy-start(bf16[1,1024,512]{2,1,0:T(8,128)(2,1)S(1)} %collective-permute-done.3.refs_1_) | copy-start | bytes 3145732
  76.7 0.8 copy-start.3
  91.4 1.6 %collective-permute-start.8 = (bf16[256,512]{1,0:T(8,128)(2,1)S(1)}, bf16[256,512]{1,0:T(8,128)(2,1)S(1)}, u32[]{:S(2)}, u32[]{:S(2)}) collective-permute-start(bf16[256,512]{1,0:T(8,128)(2,1)S(1)} %slice_bitcast_fusion), channel_id=1, source_target_pairs={{0,1},{1,0},{2,3},{3,2},{4,5},{5,4},{6,7},{7,6},{8,9},{9,8},{10,11... | collective-permute-start | bytes 786440 | tf_op jit(solution)/shard_map/ppermute | solution.py:485

commit v2 on v1

v2 whole, which is shorter than its diff:
```python
import functools

import jax
import jax.numpy as jnp
import ml_dtypes
import numpy as np
from jax import lax
from jax.experimental import pallas as pl
from jax.experimental.pallas import tpu as pltpu
from jax.sharding import PartitionSpec as P

BANDS = 12
KSHORT = 3
LANES = 128
HALO = 16
AHEAD = 5
EPS = 1e-05
PI_HIGH = 3.140625
PI_LOW = 9.67653589793e-4
F32 = jnp.float32
BF16 = jnp.bfloat16
VMEM_BYTES = 60 * 1024 * 1024


def matmul(left, right):
    return jnp.dot(left, right, preferred_element_type=F32)


def split_parts(values):
    high = values.astype(BF16)
    return high, (values - high.astype(F32)).astype(BF16)


def split_table(table):
    high = table.astype(np.float32).astype(ml_dtypes.bfloat16)
    low = (table - high.astype(np.float64)).astype(np.float32).astype(ml_dtypes.bfloat16)
    return high, low


def transform_tables(length):
    rows = length // LANES
    period = 2 * rows
    full = 2 * length
    kept = rows + 1
    padded = -(-kept // 8) * 8
    k2 = np.arange(padded)
    valid = (k2 < kept).astype(np.float64)[:, None]
    n2 = np.arange(rows)
    n1 = np.arange(LANES)
    first = 2 * np.pi / period * (k2[:, None] * n2[None, :] % period)
    forward = np.concatenate([np.cos(first) * valid, -np.sin(first) * valid], 0)
    weight = np.where((k2 == 0) | (k2 == rows), 1.0, 2.0)[:, None] * valid
    inverse = np.concatenate([np.cos(first) * weight, -np.sin(first) * weight], 0).T
    turn = 2 * np.pi / full * (k2[:, None] * n1[None, :] % full)
    second = 2 * np.pi / LANES * (n1[:, None] * n1[None, :] % LANES)
    cos2, sin2 = np.cos(second), np.sin(second)
    mid = np.concatenate(
        [np.concatenate([cos2, -sin2], 1), np.concatenate([sin2, cos2], 1)], 0
    )
    back = np.concatenate(
        [np.concatenate([cos2, sin2], 1), np.concatenate([-sin2, cos2], 1)], 0
    ) / full
    f_high, f_low = split_table(forward)
    i_high, i_low = split_table(inverse)
    parts = [np.cos(turn), np.sin(turn)]
    parts = [np.tile(part, (1, 2)).astype(np.float32) for part in parts]
    for table in (mid, back, forward, inverse.T):
        for part in split_table(table):
            wide = np.zeros((part.shape[0], 2 * LANES), np.float32)
            wide[:, : part.shape[1]] = part.astype(np.float32)
            parts.append(wide)
    return np.concatenate(parts, 0), padded


class Packed:
    def __init__(self, own, padded, rows):
        self.padded, self.rows = padded, rows
        sizes = {
            "spectrum": own * padded, "cos": padded, "sin": padded,
            "mid_high": 2 * LANES, "mid_low": 2 * LANES, "back_high": 2 * LANES, "back_low": 2 * LANES,
            "forward_high": 2 * padded, "forward_low": 2 * padded,
            "inverse_high": 2 * padded, "inverse_low": 2 * padded,
            "direct": -(-own // 8) * 8,
        }
        self.start, self.size, place = {}, sizes, 0
        for name, size in sizes.items():
            self.start[name] = place
            place += size
        self.total = place

    def get(self, ref, name, lanes=2 * LANES, base=0):
        start = self.start[name] - base
        return ref[start : start + self.size[name], :lanes]

    def half(self, ref, name, lanes=2 * LANES, base=0):
        return self.get(ref, name, lanes, base).astype(BF16)


def sine(values):
    count = jnp.floor(values * (1.0 / np.pi) + 0.5)
    rest = (values - count * PI_HIGH) - count * PI_LOW
    half = count * 0.5
    sign = 1.0 - 4.0 * (half - jnp.floor(half))
    return sign * sine_poly(rest)


def sine_poly(rest):
    square = rest * rest
    poly = -2.5052108385441720e-08
    poly = poly * square + 2.7557319223985893e-06
    poly = poly * square - 1.9841269841269841e-04
    poly = poly * square + 8.3333333333333333e-03
    poly = poly * square - 1.6666666666666667e-01
    return rest + rest * square * poly


def sine_turns(turns):
    count = jnp.floor(turns * 2.0 + 0.5)
    rest = (turns - count * 0.5) * (2.0 * np.pi)
    half = count * 0.5
    sign = 1.0 - 4.0 * (half - jnp.floor(half))
    return sign * sine_poly(rest)


def rows_to_spectrum(load_pair, group, table, turn_cos, turn_sin, mid_high, mid_low, padded):
    stacked = []
    for pair in range(group // 2):
        first = matmul(table, load_pair(pair))
        real, imag = first[:padded], first[padded:]
        turned_real = real * turn_cos + imag * turn_sin
        turned_imag = imag * turn_cos - real * turn_sin
        for side in range(2):
            lanes = slice(side * LANES, (side + 1) * LANES)
            stacked.append(jnp.concatenate([turned_real[:, lanes], turned_imag[:, lanes]], 1))
    high, low = split_parts(jnp.concatenate(stacked, 0))
    return matmul(high, mid_high) + matmul(low, mid_high) + matmul(high, mid_low)


def project_kernel(
    place_ref, *refs, pieces, tokens, width, own, own_rows, share
):
    x_refs, refs = refs[:pieces], refs[pieces:]
    gain_ref, taps_ref, w_hbm, normed_hbm, edge_ref, rows_ref, out_hbm, refs = *refs[:7], refs[7:]
    w_ref, proj_ref, block_ref, normed_ref, w_sems, out_sems, normed_sem = refs
    me = place_ref[0]
    places = [lax.rem(me + p, pieces) for p in range(pieces)]
    total = pieces * width
    loads = [pltpu.make_async_copy(w_hbm.at[role + 1], w_ref.at[role], w_sems.at[role]) for role in range(2)]
    for load in loads:
        load.start()
    chunk = 128
    for start in range(0, tokens, chunk):
        values = [ref[start : start + chunk, :].astype(F32) for ref in x_refs]
        mean = sum(jnp.sum(v, axis=1, keepdims=True) for v in values) / total
        centered = [v - mean for v in values]
        spread = sum(jnp.sum(c * c, axis=1, keepdims=True) for c in centered) / total
        scale = lax.rsqrt(spread + EPS)
        for p in range(pieces):
            gain = gain_ref[places[p]]
            normed_ref[p, start : start + chunk, :] = (centered[p] * scale * gain).astype(BF16)
    mine = pl.ds(pl.multiple_of(me * share, 16), share)
    for p in range(pieces):
        edge_ref[p] = normed_ref[p, tokens - HALO :, :]
        rows_ref[p] = x_refs[p][mine, :]
    keep = pltpu.make_async_copy(normed_ref, normed_hbm, normed_sem)
    keep.start()
    step = min(width, 256)
    per_step = step // own
    parts = tokens // LANES
    proj_ref[:, :8, :] = jnp.zeros((2, 8, step), F32)
    for load in loads:
        load.wait()
    stores = []
    for col in range(0, width, step):
        cols = slice(col, col + step)
        for role in range(2):
            sums = 0.0
            for p in range(pieces):
                rows = pl.ds(pl.multiple_of(places[p] * width, width), width)
                sums = sums + matmul(normed_ref[p], w_ref[role, rows, cols])
            proj_ref[role, 8:, :] = sums.astype(BF16).astype(F32)
        shorted = []
        for role in range(2):
            value = taps_ref[0, role + 1 : role + 2, cols] * proj_ref[role, 8 : 8 + tokens, :]
            for lag in range(1, KSHORT):
                value = (
                    value
                    + taps_ref[lag, role + 1 : role + 2, cols] * proj_ref[role, 8 - lag : 8 - lag + tokens, :]
                )
            shorted.append(value)
        gated = (shorted[1] * shorted[0]).T
        edges = jnp.concatenate(
            [
                proj_ref[0, 8:10, :],
                proj_ref[0, 6 + tokens : 8 + tokens, :],
                proj_ref[1, 8:10, :],
                proj_ref[1, 6 + tokens : 8 + tokens, :],
                jnp.zeros((8, step), F32),
            ],
            0,
        )
        first = col // own
        for d in range(per_step):
            for part in range(parts):
                block_ref[first + d, part * own_rows : part * own_rows + own, :] = gated[
                    d * own : (d + 1) * own, part * LANES : (part + 1) * LANES
                ].astype(BF16)
            block_ref[first + d, parts * own_rows :, :] = jnp.concatenate(
                [edges[:, d * own : (d + 1) * own], jnp.zeros((16, LANES - own), F32)], 1
            ).astype(BF16)
        targets = pl.ds(first, per_step)
        store = pltpu.make_async_copy(block_ref.at[targets], out_hbm.at[targets], out_sems.at[col // step])
        store.start()
        stores.append(store)
    for store in stores:
        store.wait()
    keep.wait()


def gate_kernel(place_ref, normed_ref, halo_ref, *refs, pieces, share, width):
    tap_refs, refs = refs[:pieces], refs[pieces:]
    w_hbm, (gate_ref, w_ref, rows_ref, proj_ref, w_sems) = refs[:pieces], refs[pieces:]
    loads = [pltpu.make_async_copy(w_hbm[p].at[0], w_ref.at[p], w_sems.at[p]) for p in range(pieces)]
    for load in loads:
        load.start()
    me = place_ref[0]
    places = [lax.rem(me + p, pieces) for p in range(pieces)]
    mine = pl.ds(pl.multiple_of(me * share, 16), share)
    before = pl.ds(pl.multiple_of(jnp.maximum(me * share - HALO, 0), 16), HALO)
    for p in range(pieces):
        rows_ref[p, HALO:, :] = normed_ref[p, mine, :]
        rows_ref[p, :HALO, :] = jnp.where(
            me == 0, halo_ref[p].astype(F32), normed_ref[p, before, :].astype(F32)
        ).astype(BF16)
    for load in loads:
        load.wait()
    for out in range(pieces):
        sums = 0.0
        for p in range(pieces):
            rows = pl.ds(pl.multiple_of(places[p] * width, width), width)
            sums = sums + matmul(rows_ref[p], w_ref[out, rows, :])
        proj_ref[...] = sums.astype(BF16).astype(F32)
        value = tap_refs[out][0, 0:1, :] * proj_ref[HALO : HALO + share, :]
        for lag in range(1, KSHORT):
            value = value + tap_refs[out][lag, 0:1, :] * proj_ref[HALO - lag : HALO - lag + share, :]
        gate_ref[out] = value.T


def filter_kernel(
    place_ref, in_ref, bias_ref, mid_w_ref, out_w_ref, decay_ref, direct_ref, taps_ref,
    tables_ref, packed_ref, own_taps_ref, response_ref, columns_ref, scalars_ref, in_pad_ref, *, length, own, group, packed
):
    padded = packed.padded
    seq_place = place_ref[1]
    width = out_w_ref.shape[1]
    base = packed.start["cos"]
    packed_ref[base : base + tables_ref.shape[0], :] = tables_ref[...]
    feats = in_pad_ref.shape[0]
    in_pad_ref[...] = jnp.zeros(in_pad_ref.shape, F32)
    in_pad_ref[: in_ref.shape[0], :] = in_ref[...].astype(F32)
    in_columns = in_pad_ref[...].T.astype(BF16)
    mid_columns = mid_w_ref[...].astype(F32).T.astype(BF16)
    bias = jnp.broadcast_to(bias_ref[...], (8, bias_ref.shape[1])).T[:, :1]
    columns_ref[...] = out_w_ref[...].astype(F32).T
    scalars_ref[...] = jnp.concatenate(
        [jnp.broadcast_to(decay_ref[...], (4, width)), jnp.broadcast_to(direct_ref[...], (4, width))], 0
    ).T
    mine = pl.ds(seq_place * own, own)
    out_columns = columns_ref[mine, :].astype(BF16)
    decay = scalars_ref[mine, 0:1]
    at = packed.start["direct"]
    packed_ref[at : at + own, :] = jnp.broadcast_to(scalars_ref[mine, 4:5], (own, 2 * LANES))
    shift = lax.rem(width - seq_place * own, width)
    for lag in range(KSHORT):
        own_taps = pltpu.roll(jnp.concatenate([taps_ref[lag], jnp.zeros((5, width), F32)], 0), shift, 1)
        own_taps_ref[lag] = own_taps[:, :LANES]
    rows = length // LANES
    chunk = min(1024, length)
    row_ids = lax.broadcasted_iota(jnp.int32, (feats, chunk), 0)
    band = jnp.where(row_ids > BANDS, row_ids - (BANDS + 1), row_ids - 1)
    band = jnp.clip(band, 0, BANDS - 1)
    quarter = jnp.where(row_ids <= BANDS, 0.25, 0.0)
    for start in range(0, length, chunk):
        places = lax.broadcasted_iota(jnp.int32, (feats, chunk), 1) + start
        phase = lax.shift_left(places, band) & (length - 1)
        turns = phase.astype(F32) * (1.0 / length)
        waves = sine_turns(turns + quarter)
        features = jnp.where(
            row_ids == 0,
            places.astype(F32) / length,
            jnp.where(row_ids <= 2 * BANDS, waves, 0.0),
        ).astype(BF16)
        first = sine(matmul(in_columns, features) + bias).astype(BF16)
        second = sine(matmul(mid_columns, first)).astype(BF16)
        ramp = (lax.broadcasted_iota(jnp.int32, (1, chunk), 1) + start).astype(F32) / length
        response = matmul(out_columns, second) * jnp.exp(-decay * ramp)
        for part in range(chunk // LANES):
            row = start // LANES + part
            response_ref[pl.ds(row, own, stride=rows), :] = response[:, part * LANES : (part + 1) * LANES]

    high = packed.half(tables_ref, "forward_high", rows, base)
    table = jnp.concatenate([high, high, packed.half(tables_ref, "forward_low", rows, base)], 1)
    turn_cos, turn_sin = packed.get(tables_ref, "cos", base=base), packed.get(tables_ref, "sin", base=base)
    mid_high, mid_low = packed.half(tables_ref, "mid_high", base=base), packed.half(tables_ref, "mid_low", base=base)

    def one_group(step, carry):
        def load_pair(pair):
            base = (step * group + 2 * pair) * rows
            both = [
                response_ref[pl.ds(pl.multiple_of(base + side * rows, 8), rows), :] for side in range(2)
            ]
            high, low = split_parts(jnp.concatenate(both, 1))
            return jnp.concatenate([high, low, high], 0)

        spectrum = rows_to_spectrum(
            load_pair, group, table, turn_cos, turn_sin, mid_high, mid_low, padded
        )
        packed_ref[pl.ds(pl.multiple_of(step * group * padded, 8), group * padded), :] = spectrum
        return carry

    lax.fori_loop(0, own // group, one_group, 0)


def convolve_kernel(
    x_ref, taps_ref, packed_hbm, out_ref, signal_ref, result_ref, packed_ref, sem,
    *, length, own, own_rows, group, packed, tokens, places
):
    padded = packed.padded
    load = pltpu.make_async_copy(packed_hbm, packed_ref, sem)
    load.start()
    rows = length // LANES
    per_block = tokens // LANES
    blocks = length // tokens
    lane = lax.broadcasted_iota(jnp.int32, (own, LANES), 1)
    fixes = []
    last = [jnp.zeros((2, LANES), F32)] * 2
    for block in range(blocks):
        edge = x_ref[block, per_block * own_rows :, :].astype(F32)
        starts = []
        for role in range(2):
            here, before = edge[4 * role : 4 * role + 2], last[role]
            two_back = jnp.concatenate([before[1:2], here[0:1]], 0)
            starts.append(
                taps_ref[0, role + 1 : role + 2, :] * here
                + taps_ref[1, role + 1 : role + 2, :] * two_back
                + taps_ref[2, role + 1 : role + 2, :] * before
            )
            last[role] = edge[4 * role + 2 : 4 * role + 4]
        fixes.append(starts[1] * starts[0])
    fixed = jnp.concatenate(fixes, 0)
    if 2 * blocks < LANES:
        fixed = jnp.concatenate([fixed, jnp.zeros((LANES - 2 * blocks, LANES), F32)], 0)
    fixed = fixed.T[:own]
    for row in range(rows):
        block, part = divmod(row, per_block)
        values = x_ref[block, part * own_rows : part * own_rows + own, :].astype(F32)
        if part == 0:
            values = jnp.where(lane == 0, fixed[:, 2 * block : 2 * block + 1], values)
            values = jnp.where(lane == 1, fixed[:, 2 * block + 1 : 2 * block + 2], values)
        signal_ref[pl.ds(row, own, stride=rows), :] = values
    load.wait()
    turn_cos, turn_sin = packed.get(packed_ref, "cos"), packed.get(packed_ref, "sin")
    mid_high, mid_low = packed.half(packed_ref, "mid_high"), packed.half(packed_ref, "mid_low")
    back_high, back_low = packed.half(packed_ref, "back_high"), packed.half(packed_ref, "back_low")
    table = jnp.concatenate(
        [packed.half(packed_ref, "forward_high", rows), packed.half(packed_ref, "forward_low", rows)], 1
    )
    inverse = packed.get(packed_ref, "inverse_high", rows).T.astype(BF16)
    inverse = jnp.concatenate([inverse, inverse, packed.get(packed_ref, "inverse_low", rows).T.astype(BF16)], 1)

    def one_group(step, carry):
        def load_pair(pair):
            base = (step * group + 2 * pair) * rows
            both = [
                signal_ref[pl.ds(pl.multiple_of(base + side * rows, 8), rows), :] for side in range(2)
            ]
            values = jnp.concatenate(both, 1).astype(BF16)
            return jnp.concatenate([values, values], 0)

        signal = rows_to_spectrum(load_pair, group, table, turn_cos, turn_sin, mid_high, mid_low, padded)
        other = packed_ref[pl.ds(pl.multiple_of(step * group * padded, 8), group * padded), :]
        s_real, s_imag = signal[:, :LANES], signal[:, LANES:]
        f_real, f_imag = other[:, :LANES], other[:, LANES:]
        product = jnp.concatenate(
            [s_real * f_real - s_imag * f_imag, s_real * f_imag + s_imag * f_real], 1
        )
        high, low = split_parts(product)
        mixed = matmul(high, back_high) + matmul(low, back_high) + matmul(high, back_low)
        for pair in range(group // 2):
            first = mixed[2 * pair * padded : (2 * pair + 1) * padded]
            second = mixed[(2 * pair + 1) * padded : (2 * pair + 2) * padded]
            real = jnp.concatenate([first[:, :LANES], second[:, :LANES]], 1)
            imag = jnp.concatenate([first[:, LANES:], second[:, LANES:]], 1)
            turned = jnp.concatenate(
                [real * turn_cos - imag * turn_sin, imag * turn_cos + real * turn_sin], 0
            )
            t_high, t_low = split_parts(turned)
            values = matmul(inverse, jnp.concatenate([t_high, t_low, t_high], 0))
            base = (step * group + 2 * pair) * rows
            for side in range(2):
                result_ref[pl.ds(pl.multiple_of(base + side * rows, 8), rows), :] = values[
                    :, side * LANES : (side + 1) * LANES
                ]
        return carry

    lax.fori_loop(0, own // group, one_group, 0)
    bias = packed.get(packed_ref, "direct", LANES)[:own]
    share_rows = per_block // places
    for row in range(rows):
        block, part = divmod(row, per_block)
        place, side = divmod(part, share_rows)
        values = result_ref[pl.ds(row, own, stride=rows), :]
        values = values + bias * signal_ref[pl.ds(row, own, stride=rows), :]
        target = place * (rows // per_block) + block
        out_ref[target, :, side * LANES : (side + 1) * LANES] = values.astype(BF16)


def gelu(values):
    return values * (lax.erf(values * np.float32(0.5**0.5)) + 1.0) * 0.5


def tail_kernel(place_ref, z_ref, gate_ref, gain_ref, rows_ref, *refs, pieces, share, width, block):
    mix_hbm, refs = refs[:pieces], refs[pieces:]
    up_hbm, refs = refs[:pieces], refs[pieces:]
    down_hbm, refs = refs[:pieces], refs[pieces:]
    out_refs, refs = refs[:pieces], refs[pieces:]
    sums_ref, hidden_ref, mix_ref, up_ref, down_ref, mix_sems, up_sems, down_sems = refs
    total = pieces * width
    units = hidden_ref.shape[2]
    steps = units // block
    copies = []
    for p in range(pieces):
        copies.append(pltpu.make_async_copy(mix_hbm[p], mix_ref.at[p], mix_sems.at[p]))
    for p in range(pieces):
        for k in range(steps):
            cols = pl.ds(k * block, block)
            copies.append(pltpu.make_async_copy(up_hbm[p].at[:, cols], up_ref.at[p, :, cols], up_sems.at[p, k]))
    for p in range(pieces):
        for k in range(steps):
            cols = pl.ds(k * block, block)
            copies.append(pltpu.make_async_copy(down_hbm[p].at[cols], down_ref.at[p, cols], down_sems.at[p, k]))
    started, waited = [0], [0]

    def start_until(count):
        while started[0] < min(count, len(copies)):
            copies[started[0]].start()
            started[0] += 1

    def next_copy():
        start_until(waited[0] + AHEAD)
        copies[waited[0]].wait()
        waited[0] += 1

    start_until(AHEAD)
    me = place_ref[0]
    places = [lax.rem(me + p, pieces) for p in range(pieces)]
    dims = (((0,), (0,)), ((), ()))
    mixed = [(z_ref[places[p]].astype(F32) * gate_ref[p]).astype(BF16) for p in range(pieces)]
    sums = 0.0
    for p in range(pieces):
        next_copy()
        sums = sums + lax.dot_general(mixed[p], mix_ref[p], dims, preferred_element_type=F32)
    sums_ref[...] = sums
    for p in range(pieces):
        cols = pl.ds(pl.multiple_of(places[p] * width, LANES), width)
        residual = rows_ref[p].astype(F32) + sums_ref[:, cols]
        sums_ref[:, cols] = residual.astype(BF16).astype(F32)
    values = sums_ref[...]
    mean = jnp.sum(values, axis=1, keepdims=True) / total
    centered = values - mean
    spread = jnp.sum(centered * centered, axis=1, keepdims=True) / total
    normed = (centered * lax.rsqrt(spread + EPS) * gain_ref[...]).astype(BF16)
    for p in range(pieces):
        for k in range(steps):
            next_copy()
            cols = slice(k * block, (k + 1) * block)
            hidden_ref[p, :, cols] = gelu(matmul(normed, up_ref[p, :, cols])).astype(BF16)
    sums = sums_ref[...]
    for p in range(pieces):
        for k in range(steps):
            next_copy()
        sums = sums + matmul(hidden_ref[p], down_ref[p])
    sums_ref[...] = sums
    for p in range(pieces):
        cols = pl.ds(pl.multiple_of(places[p] * width, LANES), width)
        out_refs[p][...] = sums_ref[:, cols].astype(BF16)


def join_kernel(place_ref, *refs, pieces, share):
    out_ref = refs[pieces]
    me = place_ref[0]
    for p in range(pieces):
        start = lax.rem(me + pieces - p, pieces) * share
        out_ref[pl.ds(pl.multiple_of(start, 16), share), :] = refs[p][...]


HBM = pl.BlockSpec(memory_space=pltpu.HBM)
VMEM = pl.BlockSpec(memory_space=pltpu.VMEM)
SMEM = pl.BlockSpec(memory_space=pltpu.SMEM)


def call(kernel, in_specs, out_specs, out_shape, scratch, megabytes, *args):
    kinds = {"s": SMEM, "h": HBM, "v": VMEM, "c": VMEM}
    spaces = {"h": pltpu.HBM, "v": pltpu.VMEM, "c": pltpu.HBM}
    placed = [
        pltpu.with_memory_space_constraint(arg, spaces[kind]) if kind in spaces else arg
        for kind, arg in zip(in_specs, args, strict=True)
    ]
    return pl.pallas_call(
        kernel,
        in_specs=[kinds[kind] for kind in in_specs],
        out_specs=out_specs,
        out_shape=out_shape,
        scratch_shapes=scratch,
        compiler_params=pltpu.CompilerParams(vmem_limit_bytes=megabytes * 1024 * 1024),
    )(*placed)


def shape_of(shape, dtype):
    return jax.ShapeDtypeStruct(shape, dtype)


def per_device(
    layer_input, gain_first, in_weight, short_weight, filt_in, filt_bias, filt_mid, filt_out,
    decay_rate, conv_bias, out_weight, gain_second, up_weight, down_weight,
):
    tokens, width = layer_input.shape
    pieces = lax.axis_size("chan")
    groups = lax.axis_size("seq")
    chan_place = lax.axis_index("chan")
    model = pieces * width
    length = tokens * groups
    share = tokens // pieces
    own = width // groups
    own_rows = -(-own // 16) * 16
    block_rows = tokens // LANES * own_rows + 16
    place = jnp.stack([chan_place, lax.axis_index("seq")]).astype(jnp.int32)

    def turned(array, by):
        if by == 0:
            return array
        return lax.ppermute(array, "chan", [(i, (i - by) % pieces) for i in range(pieces)])

    def all_turned(array):
        return [turned(array, p) for p in range(pieces)]

    x_pieces = all_turned(layer_input)
    by_role = jnp.transpose(in_weight, (1, 0, 2))
    step = min(width, 256)
    normed, edges, my_rows, gated = call(
        functools.partial(
            project_kernel, pieces=pieces, tokens=tokens, width=width, own=own, own_rows=own_rows, share=share
        ),
        "sc" + "v" * (pieces - 1) + "cch",
        (HBM, VMEM, VMEM, HBM),
        (
            pltpu.HBM((pieces, tokens, width), BF16),
            shape_of((pieces, HALO, width), BF16),
            pltpu.VMEM((pieces, share, width), BF16),
            pltpu.HBM((groups, block_rows, LANES), BF16),
        ),
        [
            pltpu.VMEM((2, model, width), BF16),
            pltpu.VMEM((2, tokens + 8, step), F32),
            pltpu.VMEM((groups, block_rows, LANES), BF16),
            pltpu.VMEM((pieces, tokens, width), BF16),
            pltpu.SemaphoreType.DMA((2,)),
            pltpu.SemaphoreType.DMA((width // step,)),
            pltpu.SemaphoreType.DMA,
        ],
        20,
        place, *x_pieces, gain_first.reshape(pieces, 1, width), short_weight, by_role,
    )
    by_role, out_weight, up_weight, down_weight, gated = lax.optimization_barrier(
        (by_role, out_weight, up_weight, down_weight, gated)
    )
    regrouped = lax.all_to_all(gated, "seq", split_axis=0, concat_axis=0, tiled=True)

    tables, padded = transform_tables(length)
    rows = length // LANES
    packed = Packed(own, padded, rows)
    group = min(8, own)
    filters = filt_mid.shape[0]
    spectrum, own_taps = call(
        functools.partial(filter_kernel, length=length, own=own, group=group, packed=packed),
        "s" + "c" * 8,
        (VMEM, VMEM),
        (pltpu.HBM((packed.total, 2 * LANES), F32), pltpu.VMEM((KSHORT, 8, LANES), F32)),
        [
            pltpu.VMEM((own * rows, LANES), F32),
            pltpu.VMEM((width, filters), F32),
            pltpu.VMEM((width, 8), F32),
            pltpu.VMEM((32, filters), F32),
        ],
        24,
        place, filt_in, filt_bias[None, :], filt_mid, filt_out, decay_rate[None, :], conv_bias[None, :],
        short_weight, jnp.asarray(tables),
    )
    places = pieces if share % LANES == 0 else 1
    convolved = call(
        functools.partial(
            convolve_kernel, length=length, own=own, own_rows=own_rows, group=group, packed=packed,
            tokens=tokens, places=places,
        ),
        "vvh",
        VMEM,
        pltpu.HBM((places * groups, own, tokens // places), BF16),
        [
            pltpu.VMEM((own * rows, LANES), F32),
            pltpu.VMEM((own * rows, LANES), F32),
            pltpu.VMEM((packed.total, 2 * LANES), F32),
            pltpu.SemaphoreType.DMA,
        ],
        24,
        regrouped, own_taps, spectrum,
    )
    edges, late_place, convolved = lax.optimization_barrier((edges, place, convolved))
    if places != pieces:
        convolved = jnp.transpose(convolved.reshape(groups, own, pieces, share), (2, 0, 1, 3))
        convolved = convolved.reshape(pieces * groups, own, share)
    returned = lax.all_to_all(convolved, ("chan", "seq"), split_axis=0, concat_axis=0, tiled=True)
    returned = returned.reshape(pieces, width, share)

    halo = lax.ppermute(edges, "seq", [(i, i + 1) for i in range(groups - 1)])
    mix_weights = all_turned(out_weight)
    up_weights = all_turned(up_weight)
    down_weights = all_turned(down_weight)
    big = [*mix_weights, *up_weights, *down_weights]
    gate = call(
        functools.partial(gate_kernel, pieces=pieces, share=share, width=width),
        "scvc" + "v" * (pieces - 1) + "h" * pieces,
        VMEM,
        pltpu.VMEM((pieces, width, share), F32),
        [
            pltpu.VMEM((pieces, model, width), BF16),
            pltpu.VMEM((pieces, share + HALO, width), BF16),
            pltpu.VMEM((share + HALO, width), F32),
            pltpu.SemaphoreType.DMA((pieces,)),
        ],
        16,
        late_place, normed, halo, *all_turned(short_weight), *all_turned(by_role),
    )
    units = up_weight.shape[1]
    block = min(512, units)
    results = call(
        functools.partial(tail_kernel, pieces=pieces, share=share, width=width, block=block),
        "svvcv" + "h" * (3 * pieces),
        (VMEM,) * pieces,
        tuple(shape_of((share, width), BF16) for p in range(pieces)),
        [
            pltpu.VMEM((share, model), F32),
            pltpu.VMEM((pieces, share, units), BF16),
            pltpu.VMEM((pieces, width, model), BF16),
            pltpu.VMEM((pieces, model, units), BF16),
            pltpu.VMEM((pieces, units, model), BF16),
            pltpu.SemaphoreType.DMA((pieces,)),
            pltpu.SemaphoreType.DMA((pieces, units // block)),
            pltpu.SemaphoreType.DMA((pieces, units // block)),
        ],
        44,
        place, returned, gate, gain_second[None, :], my_rows, *big,
    )
    received = [results[0]] + [
        lax.ppermute(results[p], "chan", [(i, (i + p) % pieces) for i in range(pieces)])
        for p in range(1, pieces)
    ]
    return call(
        functools.partial(join_kernel, pieces=pieces, share=share),
        "s" + "v" * pieces,
        VMEM,
        shape_of((tokens, width), BF16),
        [],
        8,
        place, *received,
    )


def solution(mesh):
    placed = (
        P("seq", "chan"),
        P(),
        P(None, None, "chan"),
        P(None, None, "chan"),
        P(),
        P(),
        P(),
        P(None, "chan"),
        P("chan"),
        P("chan"),
        P("chan", None),
        P(),
        P(None, "chan"),
        P("chan", None),
    )
    return jax.shard_map(
        per_device, mesh=mesh, in_specs=placed, out_specs=P("seq", "chan"), check_vma=False
    )
```

time: 95.5 us -> 79.7 us (0.83)
  the two profiles are of different devices: /device:TPU:0 before, /device:TPU:17 now
where the time goes in v2:
time: 79.7 us; the launch traced here: 79.2 us
  Pallas kernels  44.6 us (56%)
  starting transfers between devices  18.8 us (24%)
  waiting for transfers between devices  15.6 us (20%)
    pallas_call x6, Pallas kernels, call(): pl.pallas_call(kernel, in_specs=[kinds[kind] for kind in in_specs], out_s...  44.6 us
    ppermute x1, waiting for transfers between devices, per_device(): halo = lax.ppermute(edges, 'seq', [(i, i + 1) for i in range(groups - 1)])  10.7 us
    all_to_all x1, starting transfers between devices, per_device(): lax.all_to_all(gated, 'seq', split_axis=0, concat_axis=0, tiled=True)  6.55 us
    all_to_all x1, starting transfers between devices, per_device(): lax.all_to_all(convolved, ('chan', 'seq'), split_axis=0, concat_axis=0, t...  5.65 us
    ppermute x1, starting transfers between devices, per_device(): halo = lax.ppermute(edges, 'seq', [(i, i + 1) for i in range(groups - 1)])  3.3 us
    ppermute x6, starting transfers between devices, turned(): lax.ppermute(array, 'chan', [(i, (i - by) % pieces) for i in range(pieces)])  2.82 us
    ppermute x6, waiting for transfers between devices, turned(): lax.ppermute(array, 'chan', [(i, (i - by) % pieces) for i in range(pieces)])  2.53 us
  transfers between devices with their start and end apart: 10, of which 5 were waited for; matrix products, arithmetic and copies ran while one was open for 0% of the time, Pallas kernels for 33%

profile of v2, /device:TPU:17, one launch (start us, length us, event | category | flops | bytes accessed | tf_op | source)
XLA Modules:
  0.0 79.2 jit_solution(4461391945840522484)
XLA Ops:
  0.0 0.0 copy-start
  0.0 0.7 collective-permute-start
  0.7 0.1 pad_add_fusion.place_ref
  0.8 1.7 %collective-permute-done.refs_1_ = bf16[512,512]{1,0:T(8,128)(2,1)S(1)} collective-permute-done((bf16[512,512]{1,0:T(8,128)(2,1)}, bf16[512,512]{1,0:T(8,128)(2,1)S(1)}, u32[]{:S(2)}, u32[]{:S(2)}) %collective-permute-start) | collective-permute-done | bytes 524320 | tf_op jit(solution)/shard_map/ppermute | solution.py:542
  2.4 5.3 %shard_map.145 = (bf16[2,512,512]{2,1,0:T(8,128)(2,1)}, bf16[2,16,512]{2,1,0:T(8,128)(2,1)S(1)}, bf16[2,256,512]{2,1,0:T(8,128)(2,1)S(1)}, bf16[16,144,128]{2,1,0:T(8,128)(2,1)}) custom-call(s32[2]{0:T(128)S(1)} %pad_add_fusion.place_ref, bf16[512,512]{1,0:T(8,128)(2,1)} %refs_0_.2, bf16[512,512]{1,0:T(8,128)(2,1)S(1)} %collective-permute-done.refs_1_, ...), custom_call_target="tpu_custom_call" | custom-call | tf_op jit(solution)/shard_map/pallas_call | solution.py:509
  7.7 0.4 collective-permute-start.5
  8.2 0.1 collective-permute-start.6
  8.3 0.4 collective-permute-start.3
  8.7 6.6 %all-to-all-start = ((bf16[16,144,128]{2,1,0:T(8,128)(2,1)}), bf16[16,144,128]{2,1,0:T(8,128)(2,1)S(1)}, u32[]{:S(2)}, u32[]{:S(2)}) async-start(bf16[16,144,128]{2,1,0:T(8,128)(2,1)} %get-tuple-element.23), calls=%async_computation | async-start | bytes 1179648 | tf_op jit(solution)/shard_map/all_to_all | solution.py:577
  15.2 0.0 copy-done
  15.2 0.0 copy-start.1
  15.3 0.8 collective-permute-start.4
  16.0 12.5 %shard_map.146 = (f32[4080,256]{1,0:T(8,128)}, f32[3,8,128]{2,1,0:T(8,128)S(1)}) custom-call(s32[2]{0:T(128)S(1)} %pad_add_fusion.place_ref, bf16[25,64]{1,0:T(8,128)(2,1)} %in_ref.1, f32[1,64]{1,0:T(1,128)} %bitcast.14, bf16[64,64]{1,0:T(8,128)(2,1)} %mid_w_ref.1, bf16[64,512]{1,0:T(8,128)(2,1)} %out_w_ref.1, f32[1,512]{1,0:T(1,128)} %bitcast.12, ...), custom_call_target="tpu_custom_call" | custom-call | tf_op jit(solution)/shard_map/pallas_call | solution.py:509
  28.6 1.2 %all-to-all-done.x_ref = bf16[16,144,128]{2,1,0:T(8,128)(2,1)S(1)} async-done(((bf16[16,144,128]{2,1,0:T(8,128)(2,1)}), bf16[16,144,128]{2,1,0:T(8,128)(2,1)S(1)}, u32[]{:S(2)}, u32[]{:S(2)}) %all-to-all-start) | async-done | bytes 589856 | tf_op jit(solution)/shard_map/all_to_all | solution.py:577
  29.7 10.1 %shard_map.147 = bf16[32,32,256]{2,1,0:T(8,128)(2,1)} custom-call(bf16[16,144,128]{2,1,0:T(8,128)(2,1)S(1)} %all-to-all-done.x_ref, f32[3,8,128]{2,1,0:T(8,128)S(1)} %get-tuple-element.24.taps_ref, f32[4080,256]{1,0:T(8,128)} %get-tuple-element.25.packed_hbm), custom_call_target="tpu_custom_call" | custom-call | tf_op jit(solution)/shard_map/pallas_call | solution.py:509
  39.8 5.6 %all-to-all-start.1 = ((bf16[32,32,256]{2,1,0:T(8,128)(2,1)}), bf16[32,32,256]{2,1,0:T(8,128)(2,1)S(1)}, u32[]{:S(2)}, u32[]{:S(2)}) async-start(bf16[32,32,256]{2,1,0:T(8,128)(2,1)} %shard_map.147), calls=%async_computation.1 | async-start | bytes 1048576 | tf_op jit(solution)/shard_map/all_to_all | solution.py:621
  45.5 0.0 copy-done.1
  45.5 0.4 collective-permute-start.2
  45.9 0.8 %collective-permute-done.2.refs_1_ = f32[3,3,512]{2,1,0:T(4,128)S(1)} collective-permute-done((f32[3,3,512]{2,1,0:T(4,128)S(1)}, f32[3,3,512]{2,1,0:T(4,128)S(1)}, u32[]{:S(2)}, u32[]{:S(2)}) %collective-permute-start.2) | collective-permute-done | bytes 18464 | tf_op jit(solution)/shard_map/ppermute | solution.py:542
  46.7 3.3 %collective-permute-start.1 = (bf16[2,16,512]{2,1,0:T(8,128)(2,1)S(1)}, bf16[2,16,512]{2,1,0:T(8,128)(2,1)S(1)}, u32[]{:S(2)}, u32[]{:S(2)}) collective-permute-start(bf16[2,16,512]{2,1,0:T(8,128)(2,1)S(1)} %get-tuple-element.29), channel_id=1, source_target_pairs={{0,2},{2,4},{4,6},{6,8},{8,10},{10,12},{12,14},{14,16},{16,18},{18... | collective-permute-start | bytes 98312 | tf_op jit(solution)/shard_map/ppermute | solution.py:624
  50.0 10.7 %collective-permute-done.1.halo_ref = bf16[2,16,512]{2,1,0:T(8,128)(2,1)S(1)} collective-permute-done((bf16[2,16,512]{2,1,0:T(8,128)(2,1)S(1)}, bf16[2,16,512]{2,1,0:T(8,128)(2,1)S(1)}, u32[]{:S(2)}, u32[]{:S(2)}) %collective-permute-start.1) | collective-permute-done | bytes 32800 | tf_op jit(solution)/shard_map/ppermute | solution.py:624
  60.8 0.0 collective-permute-done.3.refs_3_
  60.8 3.8 %shard_map.148.gate_ref = f32[2,512,256]{2,1,0:T(8,128)S(1)} custom-call(s32[2]{0:T(128)S(1)} %pad_add_fusion.place_ref, bf16[2,512,512]{2,1,0:T(8,128)(2,1)} %get-tuple-element.28.normed_ref, bf16[2,16,512]{2,1,0:T(8,128)(2,1)S(1)} %collective-permute-done.1.halo_ref, f32[3,3,512]{2,1,0:T(4,128)} %refs_0_.3, ...), custom_call_target="tpu_custom_call" | custom-call | tf_op jit(solution)/shard_map/pallas_call | solution.py:509
  64.5 0.0 collective-permute-done.4.refs_1_
  64.5 0.0 all-to-all-done.1
  64.5 0.0 collective-permute-done.5.refs_3_
  64.6 0.0 collective-permute-done.6.refs_5_
  64.6 11.5 %shard_map.149 = (bf16[256,512]{1,0:T(8,128)(2,1)S(1)}, bf16[256,512]{1,0:T(8,128)(2,1)S(1)}) custom-call(s32[2]{0:T(128)S(1)} %pad_add_fusion.place_ref, bf16[2,512,256]{2,1,0:T(8,128)(2,1)S(1)} %bitcast.9, f32[2,512,256]{2,1,0:T(8,128)S(1)} %shard_map.148.gate_ref, f32[1,1024]{1,0:T(1,128)} %bitcast.11, ...), custom_call_target="tpu_custom_call" | custom-call | tf_op jit(solution)/shard_map/pallas_call | solution.py:509
  76.1 0.5 collective-permute-start.7
  76.6 1.2 %collective-permute-done.7.refs_1_ = bf16[256,512]{1,0:T(8,128)(2,1)S(1)} collective-permute-done((bf16[256,512]{1,0:T(8,128)(2,1)S(1)}, bf16[256,512]{1,0:T(8,128)(2,1)S(1)}, u32[]{:S(2)}, u32[]{:S(2)}) %collective-permute-start.7) | collective-permute-done | bytes 262176 | tf_op jit(solution)/shard_map/ppermute | solution.py:664
  77.8 1.4 %shard_map.150 = bf16[512,512]{1,0:T(8,128)(2,1)} custom-call(s32[2]{0:T(128)S(1)} %pad_add_fusion.place_ref, bf16[256,512]{1,0:T(8,128)(2,1)S(1)} %get-tuple-element.35.refs_0_, bf16[256,512]{1,0:T(8,128)(2,1)S(1)} %collective-permute-done.7.refs_1_), custom_call_target="tpu_custom_call" | custom-call | tf_op jit(solution)/shard_map/pallas_call | solution.py:509
Async XLA Ops:
  0.0 15.2 %copy-start = (bf16[512,1024]{1,0:T(8,128)(2,1)S(1)}, bf16[512,1024]{1,0:T(8,128)(2,1)}, u32[]{:S(2)}) copy-start(bf16[512,1024]{1,0:T(8,128)(2,1)} %refs_0_.4) | copy-start | bytes 3145732
  0.0 2.4 %collective-permute-start = (bf16[512,512]{1,0:T(8,128)(2,1)}, bf16[512,512]{1,0:T(8,128)(2,1)S(1)}, u32[]{:S(2)}, u32[]{:S(2)}) collective-permute-start(bf16[512,512]{1,0:T(8,128)(2,1)} %refs_0_.2), channel_id=1, source_target_pairs={{0,1},{1,0},{2,3},{3,2},{4,5},{5,4},{6,7},{7,6},{8,9},{9,8},{10,11... | collective-permute-start | bytes 1572872 | tf_op jit(solution)/shard_map/ppermute | solution.py:542
  7.7 56.8 %collective-permute-start.5 = (bf16[1024,2048]{1,0:T(8,128)(2,1)}, bf16[1024,2048]{1,0:T(8,128)(2,1)}, u32[]{:S(2)}, u32[]{:S(2)}) collective-permute-start(bf16[1024,2048]{1,0:T(8,128)(2,1)} %refs_2_), channel_id=1, source_target_pairs={{0,1},{1,0},{2,3},{3,2},{4,5},{5,4},{6,7},{7,6},{8,9},{9,8},{10,11... | collective-permute-start | bytes 12582920 | tf_op jit(solution)/shard_map/ppermute | solution.py:542
  8.2 56.4 %collective-permute-start.6 = (bf16[2048,1024]{1,0:T(8,128)(2,1)}, bf16[2048,1024]{1,0:T(8,128)(2,1)}, u32[]{:S(2)}, u32[]{:S(2)}) collective-permute-start(bf16[2048,1024]{1,0:T(8,128)(2,1)} %refs_4_), channel_id=1, source_target_pairs={{0,1},{1,0},{2,3},{3,2},{4,5},{5,4},{6,7},{7,6},{8,9},{9,8},{10,11... | collective-permute-start | bytes 12582920 | tf_op jit(solution)/shard_map/ppermute | solution.py:542
  8.3 52.5 %collective-permute-start.3 = (bf16[3,1024,512]{2,1,0:T(8,128)(2,1)}, bf16[3,1024,512]{2,1,0:T(8,128)(2,1)}, u32[]{:S(2)}, u32[]{:S(2)}) collective-permute-start(bf16[3,1024,512]{2,1,0:T(8,128)(2,1)} %bitcast.3.refs_4_.refs_2_), channel_id=1, source_target_pairs={{0,1},{1,0},{2,3},{3,2},{4,5},{5,4},{6,7},{7,6},{8,9},{9,8},{10,11... | collective-permute-start | bytes 9437192 | tf_op jit(solution)/shard_map/ppermute | solution.py:542
  8.7 21.0 %all-to-all-start = ((bf16[16,144,128]{2,1,0:T(8,128)(2,1)}), bf16[16,144,128]{2,1,0:T(8,128)(2,1)S(1)}, u32[]{:S(2)}, u32[]{:S(2)}) async-start(bf16[16,144,128]{2,1,0:T(8,128)(2,1)} %get-tuple-element.23), calls=%async_computation | async-start | bytes 1179648 | tf_op jit(solution)/shard_map/all_to_all | solution.py:577
  15.2 30.2 %copy-start.1 = (f32[3,3,512]{2,1,0:T(4,128)S(1)}, f32[3,3,512]{2,1,0:T(4,128)}, u32[]{:S(2)}) copy-start(f32[3,3,512]{2,1,0:T(4,128)} %refs_0_.3) | copy-start | bytes 55300
  15.3 49.3 %collective-permute-start.4 = (bf16[512,1024]{1,0:T(8,128)(2,1)S(1)}, bf16[512,1024]{1,0:T(8,128)(2,1)}, u32[]{:S(2)}, u32[]{:S(2)}) collective-permute-start(bf16[512,1024]{1,0:T(8,128)(2,1)S(1)} %copy-done), channel_id=1, source_target_pairs={{0,1},{1,0},{2,3},{3,2},{4,5},{5,4},{6,7},{7,6},{8,9},{9,8},{10,11... | collective-permute-start | bytes 3145736 | tf_op jit(solution)/shard_map/ppermute | solution.py:542
  39.8 24.7 %all-to-all-start.1 = ((bf16[32,32,256]{2,1,0:T(8,128)(2,1)}), bf16[32,32,256]{2,1,0:T(8,128)(2,1)S(1)}, u32[]{:S(2)}, u32[]{:S(2)}) async-start(bf16[32,32,256]{2,1,0:T(8,128)(2,1)} %shard_map.147), calls=%async_computation.1 | async-start | bytes 1048576 | tf_op jit(solution)/shard_map/all_to_all | solution.py:621
  45.5 1.3 %collective-permute-start.2 = (f32[3,3,512]{2,1,0:T(4,128)S(1)}, f32[3,3,512]{2,1,0:T(4,128)S(1)}, u32[]{:S(2)}, u32[]{:S(2)}) collective-permute-start(f32[3,3,512]{2,1,0:T(4,128)S(1)} %copy-done.1), channel_id=1, source_target_pairs={{0,1},{1,0},{2,3},{3,2},{4,5},{5,4},{6,7},{7,6},{8,9},{9,8},{10,11... | collective-permute-start | bytes 55304 | tf_op jit(solution)/shard_map/ppermute | solution.py:542
  46.7 14.0 %collective-permute-start.1 = (bf16[2,16,512]{2,1,0:T(8,128)(2,1)S(1)}, bf16[2,16,512]{2,1,0:T(8,128)(2,1)S(1)}, u32[]{:S(2)}, u32[]{:S(2)}) collective-permute-start(bf16[2,16,512]{2,1,0:T(8,128)(2,1)S(1)} %get-tuple-element.29), channel_id=1, source_target_pairs={{0,2},{2,4},{4,6},{6,8},{8,10},{10,12},{12,14},{14,16},{16,18},{18... | collective-permute-start | bytes 98312 | tf_op jit(solution)/shard_map/ppermute | solution.py:624
  76.1 1.7 %collective-permute-start.7 = (bf16[256,512]{1,0:T(8,128)(2,1)S(1)}, bf16[256,512]{1,0:T(8,128)(2,1)S(1)}, u32[]{:S(2)}, u32[]{:S(2)}) collective-permute-start(bf16[256,512]{1,0:T(8,128)(2,1)S(1)} %get-tuple-element.36), channel_id=1, source_target_pairs={{0,1},{1,0},{2,3},{3,2},{4,5},{5,4},{6,7},{7,6},{8,9},{9,8},{10,11... | collective-permute-start | bytes 786440 | tf_op jit(solution)/shard_map/ppermute | solution.py:664

commit v3 on v2

v3 whole, which is shorter than its diff:
```python
import functools

import jax
import jax.numpy as jnp
import ml_dtypes
import numpy as np
from jax import lax
from jax.experimental import pallas as pl
from jax.experimental.pallas import tpu as pltpu
from jax.sharding import PartitionSpec as P

BANDS = 12
KSHORT = 3
LANES = 128
HALO = 16
AHEAD = 6
EPS = 1e-05
PI_HIGH = 3.140625
PI_LOW = 9.67653589793e-4
F32 = jnp.float32
BF16 = jnp.bfloat16
VMEM_BYTES = 60 * 1024 * 1024


def matmul(left, right):
    return jnp.dot(left, right, preferred_element_type=F32)


def split_parts(values):
    high = values.astype(BF16)
    return high, (values - high.astype(F32)).astype(BF16)


def split_table(table):
    high = table.astype(np.float32).astype(ml_dtypes.bfloat16)
    low = (table - high.astype(np.float64)).astype(np.float32).astype(ml_dtypes.bfloat16)
    return high, low


def transform_tables(length):
    rows = length // LANES
    period = 2 * rows
    full = 2 * length
    kept = rows + 1
    padded = -(-kept // 8) * 8
    k2 = np.arange(padded)
    valid = (k2 < kept).astype(np.float64)[:, None]
    n2 = np.arange(rows)
    n1 = np.arange(LANES)
    first = 2 * np.pi / period * (k2[:, None] * n2[None, :] % period)
    forward = np.concatenate([np.cos(first) * valid, -np.sin(first) * valid], 0)
    weight = np.where((k2 == 0) | (k2 == rows), 1.0, 2.0)[:, None] * valid
    inverse = np.concatenate([np.cos(first) * weight, -np.sin(first) * weight], 0).T
    turn = 2 * np.pi / full * (k2[:, None] * n1[None, :] % full)
    second = 2 * np.pi / LANES * (n1[:, None] * n1[None, :] % LANES)
    cos2, sin2 = np.cos(second), np.sin(second)
    mid = np.concatenate(
        [np.concatenate([cos2, -sin2], 1), np.concatenate([sin2, cos2], 1)], 0
    )
    back = np.concatenate(
        [np.concatenate([cos2, sin2], 1), np.concatenate([-sin2, cos2], 1)], 0
    ) / full
    f_high, f_low = split_table(forward)
    i_high, i_low = split_table(inverse)
    f_high, f_low = split_table(forward)
    i_high, i_low = split_table(inverse)
    return {
        "turn": np.tile(np.stack([np.cos(turn), np.sin(turn)]), (1, 1, 2)).astype(np.float32),
        "square": np.stack([*split_table(mid), *split_table(back)]),
        "forward3": np.concatenate([f_high, f_high, f_low], 1),
        "forward2": np.concatenate([f_high, f_low], 1),
        "inverse3": np.concatenate([i_high, i_high, i_low], 1),
    }


def sine(values):
    count = jnp.floor(values * (1.0 / np.pi) + 0.5)
    rest = (values - count * PI_HIGH) - count * PI_LOW
    half = count * 0.5
    sign = 1.0 - 4.0 * (half - jnp.floor(half))
    return sign * sine_poly(rest)


def sine_poly(rest):
    square = rest * rest
    poly = -2.5052108385441720e-08
    poly = poly * square + 2.7557319223985893e-06
    poly = poly * square - 1.9841269841269841e-04
    poly = poly * square + 8.3333333333333333e-03
    poly = poly * square - 1.6666666666666667e-01
    return rest + rest * square * poly


def sine_turns(turns):
    count = jnp.floor(turns * 2.0 + 0.5)
    rest = (turns - count * 0.5) * (2.0 * np.pi)
    half = count * 0.5
    sign = 1.0 - 4.0 * (half - jnp.floor(half))
    return sign * sine_poly(rest)


def rows_to_spectrum(load_pair, group, table, turn_cos, turn_sin, mid_high, mid_low, padded):
    stacked = []
    for pair in range(group // 2):
        first = matmul(table, load_pair(pair))
        real, imag = first[:padded], first[padded:]
        turned_real = real * turn_cos + imag * turn_sin
        turned_imag = imag * turn_cos - real * turn_sin
        for side in range(2):
            lanes = slice(side * LANES, (side + 1) * LANES)
            stacked.append(jnp.concatenate([turned_real[:, lanes], turned_imag[:, lanes]], 1))
    high, low = split_parts(jnp.concatenate(stacked, 0))
    return matmul(high, mid_high) + matmul(low, mid_high) + matmul(high, mid_low)


def project_kernel(
    *refs, pieces, tokens, width, own, own_rows, share
):
    x_refs, refs = refs[:pieces], refs[pieces:]
    gain_ref, taps_ref, w_hbm, normed_hbm, rows_hbm, out_hbm, refs = *refs[:6], refs[6:]
    w_ref, proj_ref, block_ref, normed_ref, w_sems, out_sems, normed_sem, row_sems = refs
    me = lax.axis_index("chan")
    places = [lax.rem(me + p, pieces) for p in range(pieces)]
    total = pieces * width
    loads = [pltpu.make_async_copy(w_hbm.at[(role + 1) % 3], w_ref.at[role], w_sems.at[role]) for role in range(3)]
    for load in loads:
        load.start()
    chunk = 128
    for start in range(0, tokens, chunk):
        values = [ref[start : start + chunk, :].astype(F32) for ref in x_refs]
        mean = sum(jnp.sum(v, axis=1, keepdims=True) for v in values) / total
        centered = [v - mean for v in values]
        spread = sum(jnp.sum(c * c, axis=1, keepdims=True) for c in centered) / total
        scale = lax.rsqrt(spread + EPS)
        for p in range(pieces):
            gain = gain_ref[places[p]]
            normed_ref[p, start : start + chunk, :] = (centered[p] * scale * gain).astype(BF16)
    mine = pl.ds(pl.multiple_of(me * share, 16), share)
    keeps = [pltpu.make_async_copy(normed_ref, normed_hbm, normed_sem)]
    for p in range(pieces):
        keeps.append(pltpu.make_async_copy(x_refs[p].at[mine], rows_hbm.at[p], row_sems.at[p]))
    for keep in keeps:
        keep.start()
    step = min(width, 256)
    per_step = step // own
    parts = tokens // LANES
    proj_ref[:, :8, :] = jnp.zeros((2, 8, step), F32)
    for load in loads[:2]:
        load.wait()
    stores = []
    for col in range(0, width, step):
        cols = slice(col, col + step)
        for role in range(2):
            sums = 0.0
            for p in range(pieces):
                rows = pl.ds(pl.multiple_of(places[p] * width, width), width)
                sums = sums + matmul(normed_ref[p], w_ref[role, rows, cols])
            proj_ref[role, 8:, :] = sums.astype(BF16).astype(F32)
        shorted = []
        for role in range(2):
            value = taps_ref[0, role + 1 : role + 2, cols] * proj_ref[role, 8 : 8 + tokens, :]
            for lag in range(1, KSHORT):
                value = (
                    value
                    + taps_ref[lag, role + 1 : role + 2, cols] * proj_ref[role, 8 - lag : 8 - lag + tokens, :]
                )
            shorted.append(value)
        gated = (shorted[1] * shorted[0]).T
        if col == 0:
            loads[2].wait()
            last = 0.0
            for p in range(pieces):
                rows = pl.ds(pl.multiple_of(places[p] * width, width), width)
                last = last + matmul(normed_ref[p, tokens - HALO :, :], w_ref[2, rows, :])
            last = last.astype(BF16).astype(F32)
            spread_last = [
                last[row : row + 1, lane : lane + LANES]
                for row in (HALO - 2, HALO - 1)
                for lane in range(0, width, LANES)
            ]
            spread_last = jnp.concatenate(spread_last + [jnp.zeros((8 - len(spread_last), LANES), F32)][: len(spread_last) < 8], 0)
        edges = jnp.concatenate(
            [
                proj_ref[0, 8:10, :],
                proj_ref[0, 6 + tokens : 8 + tokens, :],
                proj_ref[1, 8:10, :],
                proj_ref[1, 6 + tokens : 8 + tokens, :],
            ],
            0,
        )
        first = col // own
        for d in range(per_step):
            for part in range(parts):
                block_ref[first + d, part * own_rows : part * own_rows + own, :] = gated[
                    d * own : (d + 1) * own, part * LANES : (part + 1) * LANES
                ].astype(BF16)
            block_edges = jnp.concatenate([edges[:, d * own : (d + 1) * own], jnp.zeros((8, LANES - own), F32)], 1)
            block_ref[first + d, parts * own_rows :, :] = jnp.concatenate([block_edges, spread_last], 0).astype(BF16)
        targets = pl.ds(first, per_step)
        store = pltpu.make_async_copy(block_ref.at[targets], out_hbm.at[targets], out_sems.at[col // step])
        store.start()
        stores.append(store)
    for store in stores:
        store.wait()
    for keep in keeps:
        keep.wait()


def gate_kernel(normed_ref, *refs, pieces, share, width, rest):
    side_refs, refs = refs[:pieces], refs[pieces:]
    w_hbm, refs = refs[:pieces], refs[pieces:]
    mix_hbm, (gate_ref, mix_ref, w_ref, rows_ref, proj_ref, w_sems, mix_sems) = refs[:pieces], refs[pieces:]
    fetches = []
    for p in range(pieces):
        size = width - rest if p == pieces - 1 else width
        fetches.append(
            pltpu.make_async_copy(
                mix_hbm[p].at[pl.ds(0, size)], mix_ref.at[pl.ds(p * width, size)], mix_sems.at[p]
            )
        )
    loads = [pltpu.make_async_copy(w_hbm[p].at[0], w_ref.at[p], w_sems.at[p]) for p in range(pieces)]
    for load in loads + fetches:
        load.start()
    me = lax.axis_index("chan")
    places = [lax.rem(me + p, pieces) for p in range(pieces)]
    mine = pl.ds(pl.multiple_of(me * share, 16), share)
    before = pl.ds(pl.multiple_of(jnp.maximum(me * share - HALO, 0), 16), HALO)
    for p in range(pieces):
        rows_ref[p, HALO:, :] = normed_ref[p, mine, :]
        rows_ref[p, :HALO, :] = normed_ref[p, before, :]
    for load in loads:
        load.wait()
    for out in range(pieces):
        sums = 0.0
        for p in range(pieces):
            rows = pl.ds(pl.multiple_of(places[p] * width, width), width)
            sums = sums + matmul(rows_ref[p], w_ref[out, rows, :])
        proj_ref[...] = sums.astype(BF16).astype(F32)
        proj_ref[HALO - 2 : HALO, :] = jnp.where(
            me == 0, side_refs[out][KSHORT : KSHORT + 2, :], proj_ref[HALO - 2 : HALO, :]
        )
        value = side_refs[out][0:1, :] * proj_ref[HALO : HALO + share, :]
        for lag in range(1, KSHORT):
            value = value + side_refs[out][lag : lag + 1, :] * proj_ref[HALO - lag : HALO - lag + share, :]
        gate_ref[out] = value.T
    for fetch in fetches:
        fetch.wait()


def filter_kernel(
    in_ref, bias_ref, mid_w_ref, out_w_ref, decay_ref, direct_ref, taps_ref,
    turn_ref, square_ref, forward_ref, spectrum_ref, own_taps_ref, own_direct_ref, gate_taps_ref,
    response_ref, columns_ref, scalars_ref, in_pad_ref, *, length, own, group
):
    padded = turn_ref.shape[1]
    seq_place = lax.axis_index("seq")
    width = out_w_ref.shape[1]
    feats = in_pad_ref.shape[0]
    in_pad_ref[...] = jnp.zeros(in_pad_ref.shape, F32)
    in_pad_ref[: in_ref.shape[0], :] = in_ref[...].astype(F32)
    in_columns = in_pad_ref[...].T.astype(BF16)
    mid_columns = mid_w_ref[...].astype(F32).T.astype(BF16)
    bias = jnp.broadcast_to(bias_ref[...], (8, bias_ref.shape[1])).T[:, :1]
    columns_ref[...] = out_w_ref[...].astype(F32).T
    scalars_ref[...] = jnp.concatenate(
        [jnp.broadcast_to(decay_ref[...], (4, width)), jnp.broadcast_to(direct_ref[...], (4, width))], 0
    ).T
    mine = pl.ds(seq_place * own, own)
    out_columns = columns_ref[mine, :].astype(BF16)
    decay = scalars_ref[mine, 0:1]
    own_direct_ref[...] = jnp.broadcast_to(scalars_ref[mine, 4:5], (own, LANES))
    shift = lax.rem(width - seq_place * own, width)
    for lag in range(KSHORT):
        own_taps = pltpu.roll(jnp.concatenate([taps_ref[lag], jnp.zeros((5, width), F32)], 0), shift, 1)
        own_taps_ref[lag] = own_taps[:, :LANES]
        gate_taps_ref[lag : lag + 1, :] = taps_ref[lag, 0:1, :]
    rows = length // LANES
    chunk = min(1024, length)
    row_ids = lax.broadcasted_iota(jnp.int32, (feats, chunk), 0)
    band = jnp.where(row_ids > BANDS, row_ids - (BANDS + 1), row_ids - 1)
    band = jnp.clip(band, 0, BANDS - 1)
    quarter = jnp.where(row_ids <= BANDS, 0.25, 0.0)
    for start in range(0, length, chunk):
        places = lax.broadcasted_iota(jnp.int32, (feats, chunk), 1) + start
        phase = lax.shift_left(places, band) & (length - 1)
        turns = phase.astype(F32) * (1.0 / length)
        waves = sine_turns(turns + quarter)
        features = jnp.where(
            row_ids == 0,
            places.astype(F32) / length,
            jnp.where(row_ids <= 2 * BANDS, waves, 0.0),
        ).astype(BF16)
        first = sine(matmul(in_columns, features) + bias).astype(BF16)
        second = sine(matmul(mid_columns, first)).astype(BF16)
        ramp = (lax.broadcasted_iota(jnp.int32, (1, chunk), 1) + start).astype(F32) / length
        response = matmul(out_columns, second) * jnp.exp(-decay * ramp)
        for part in range(chunk // LANES):
            row = start // LANES + part
            response_ref[pl.ds(row, own, stride=rows), :] = response[:, part * LANES : (part + 1) * LANES]

    def one_group(step, carry):
        def load_pair(pair):
            base = (step * group + 2 * pair) * rows
            both = [
                response_ref[pl.ds(pl.multiple_of(base + side * rows, 8), rows), :] for side in range(2)
            ]
            high, low = split_parts(jnp.concatenate(both, 1))
            return jnp.concatenate([high, low, high], 0)

        spectrum = rows_to_spectrum(
            load_pair, group, forward_ref[...], turn_ref[0], turn_ref[1], square_ref[0], square_ref[1], padded
        )
        spectrum_ref[pl.ds(pl.multiple_of(step * group * padded, 8), group * padded), :] = spectrum
        return carry

    if own == group:
        one_group(0, 0)
    else:
        lax.fori_loop(0, own // group, one_group, 0)


def convolve_kernel(
    x_ref, taps_ref, direct_ref, gate_taps_ref, spectrum_hbm, turn_hbm, square_hbm, forward_hbm, inverse_hbm, out_hbm, side_ref,
    signal_ref, result_ref, out_ref, spectrum_ref, turn_ref, square_ref, forward_ref, inverse_ref,
    load_sems, out_sems, *, length, own, own_rows, group, tokens, places
):
    padded = turn_ref.shape[1]
    sources = (forward_hbm, turn_hbm, square_hbm, inverse_hbm, spectrum_hbm)
    targets = (forward_ref, turn_ref, square_ref, inverse_ref, spectrum_ref)
    loads = [pltpu.make_async_copy(s, t, load_sems.at[k]) for k, (s, t) in enumerate(zip(sources, targets))]
    for load in loads:
        load.start()
    rows = length // LANES
    per_block = tokens // LANES
    blocks = length // tokens
    seq_place = lax.axis_index("seq")
    width = side_ref.shape[1]
    count = width // LANES
    before = x_ref[jnp.maximum(seq_place - 1, 0), per_block * own_rows :, :].astype(F32)
    before = jnp.where(seq_place > 0, before, 0.0)
    side_ref[...] = jnp.zeros(side_ref.shape, F32)
    side_ref[:KSHORT, :] = gate_taps_ref[...]
    for k in range(2 * count):
        row, lanes = KSHORT + k // count, slice(k % count * LANES, (k % count + 1) * LANES)
        side_ref[row : row + 1, lanes] = before[8 + k : 9 + k, :]
    lane = lax.broadcasted_iota(jnp.int32, (own, LANES), 1)
    fixes = []
    last = [jnp.zeros((2, LANES), F32)] * 2
    for block in range(blocks):
        edge = x_ref[block, per_block * own_rows :, :].astype(F32)
        starts = []
        for role in range(2):
            here, before = edge[4 * role : 4 * role + 2], last[role]
            two_back = jnp.concatenate([before[1:2], here[0:1]], 0)
            starts.append(
                taps_ref[0, role + 1 : role + 2, :] * here
                + taps_ref[1, role + 1 : role + 2, :] * two_back
                + taps_ref[2, role + 1 : role + 2, :] * before
            )
            last[role] = edge[4 * role + 2 : 4 * role + 4]
        fixes.append(starts[1] * starts[0])
    fixed = jnp.concatenate(fixes, 0)
    if 2 * blocks < LANES:
        fixed = jnp.concatenate([fixed, jnp.zeros((LANES - 2 * blocks, LANES), F32)], 0)
    fixed = fixed.T[:own]
    for row in range(rows):
        block, part = divmod(row, per_block)
        values = x_ref[block, part * own_rows : part * own_rows + own, :].astype(F32)
        if part == 0:
            values = jnp.where(lane == 0, fixed[:, 2 * block : 2 * block + 1], values)
            values = jnp.where(lane == 1, fixed[:, 2 * block + 1 : 2 * block + 2], values)
        signal_ref[pl.ds(row, own, stride=rows), :] = values
    for load in loads[:3]:
        load.wait()
    turn_cos, turn_sin = turn_ref[0], turn_ref[1]

    def one_group(step, carry):
        def load_pair(pair):
            base = (step * group + 2 * pair) * rows
            both = [
                signal_ref[pl.ds(pl.multiple_of(base + side * rows, 8), rows), :] for side in range(2)
            ]
            values = jnp.concatenate(both, 1).astype(BF16)
            return jnp.concatenate([values, values], 0)

        signal = rows_to_spectrum(
            load_pair, group, forward_ref[...], turn_cos, turn_sin, square_ref[0], square_ref[1], padded
        )
        if own == group:
            for load in loads[3:]:
                load.wait()
        other = spectrum_ref[pl.ds(pl.multiple_of(step * group * padded, 8), group * padded), :]
        s_real, s_imag = signal[:, :LANES], signal[:, LANES:]
        f_real, f_imag = other[:, :LANES], other[:, LANES:]
        product = jnp.concatenate(
            [s_real * f_real - s_imag * f_imag, s_real * f_imag + s_imag * f_real], 1
        )
        high, low = split_parts(product)
        mixed = (
            matmul(high, square_ref[2]) + matmul(low, square_ref[2]) + matmul(high, square_ref[3])
        )
        for pair in range(group // 2):
            first = mixed[2 * pair * padded : (2 * pair + 1) * padded]
            second = mixed[(2 * pair + 1) * padded : (2 * pair + 2) * padded]
            real = jnp.concatenate([first[:, :LANES], second[:, :LANES]], 1)
            imag = jnp.concatenate([first[:, LANES:], second[:, LANES:]], 1)
            turned = jnp.concatenate(
                [real * turn_cos - imag * turn_sin, imag * turn_cos + real * turn_sin], 0
            )
            t_high, t_low = split_parts(turned)
            values = matmul(inverse_ref[...], jnp.concatenate([t_high, t_low, t_high], 0))
            base = (step * group + 2 * pair) * rows
            for side in range(2):
                result_ref[pl.ds(pl.multiple_of(base + side * rows, 8), rows), :] = values[
                    :, side * LANES : (side + 1) * LANES
                ]
        return carry

    if own == group:
        one_group(0, 0)
    else:
        for load in loads[3:]:
            load.wait()
        lax.fori_loop(0, own // group, one_group, 0)
    bias = direct_ref[...]
    share_rows = per_block // places
    blocks = length // tokens
    stores, half = [], max(blocks // 2, 1)
    for row in range(rows):
        block, part = divmod(row, per_block)
        place, side = divmod(part, share_rows)
        values = result_ref[pl.ds(row, own, stride=rows), :]
        values = values + bias * signal_ref[pl.ds(row, own, stride=rows), :]
        target = place * blocks + block
        out_ref[target, :, side * LANES : (side + 1) * LANES] = values.astype(BF16)
        if part == per_block - 1 and (block + 1) % half == 0:
            for p in range(places):
                span = pl.ds(p * blocks + block + 1 - half, half)
                store = pltpu.make_async_copy(out_ref.at[span], out_hbm.at[span], out_sems.at[len(stores)])
                store.start()
                stores.append(store)
    for store in stores:
        store.wait()


def gelu(values):
    return values * (lax.erf(values * np.float32(0.5**0.5)) + 1.0) * 0.5


def tail_kernel(
    z_ref, gate_ref, mix_ref, gain_ref, rows_hbm, *refs, pieces, share, width, block, rest
):
    mix_hbm, refs = refs[0], refs[1:]
    up_hbm, refs = refs[:pieces], refs[pieces:]
    down_hbm, refs = refs[:pieces], refs[pieces:]
    out_refs, refs = refs[:pieces], refs[pieces:]
    sums_ref, rows_ref, rest_ref, up_ref, down_ref, first_sems, up_sems, down_sems = refs
    total = pieces * width
    steps = up_ref.shape[2] // block
    count = pieces * steps
    firsts = [
        pltpu.make_async_copy(mix_hbm.at[pl.ds(width - rest, rest)], rest_ref, first_sems.at[0]),
        pltpu.make_async_copy(rows_hbm, rows_ref, first_sems.at[1]),
    ]
    ups, downs = [], []
    for p in range(pieces):
        for k in range(steps):
            cols = pl.ds(k * block, block)
            ups.append(pltpu.make_async_copy(up_hbm[p].at[:, cols], up_ref.at[p, :, cols], up_sems.at[p, k]))
            downs.append(pltpu.make_async_copy(down_hbm[p].at[cols], down_ref.at[p, cols], down_sems.at[p, k]))
    copies = list(firsts)
    for k in range(count + 2):
        copies += ups[k : k + 1]
        if k >= 2:
            copies.append(downs[k - 2])
    started, waited = [0], [0]

    def start_until(limit):
        while started[0] < min(limit, len(copies)):
            copies[started[0]].start()
            started[0] += 1

    def next_copy():
        start_until(waited[0] + AHEAD)
        copies[waited[0]].wait()
        waited[0] += 1

    start_until(AHEAD)
    me = lax.axis_index("chan")
    places = [lax.rem(me + p, pieces) for p in range(pieces)]
    dims = (((0,), (0,)), ((), ()))
    sums = 0.0
    for p in range(pieces):
        mixed = (z_ref[places[p]].astype(F32) * gate_ref[p]).astype(BF16)
        size = width - rest if p == pieces - 1 else width
        kept = mix_ref[p * width : p * width + size, :]
        sums = sums + lax.dot_general(mixed[:size], kept, dims, preferred_element_type=F32)
    next_copy()
    sums = sums + lax.dot_general(mixed[width - rest :], rest_ref[...], dims, preferred_element_type=F32)
    sums_ref[...] = sums
    next_copy()
    for p in range(pieces):
        cols = pl.ds(pl.multiple_of(places[p] * width, LANES), width)
        residual = rows_ref[p].astype(F32) + sums_ref[:, cols]
        sums_ref[:, cols] = residual.astype(BF16).astype(F32)
    values = sums_ref[...]
    mean = jnp.sum(values, axis=1, keepdims=True) / total
    centered = values - mean
    spread = jnp.sum(centered * centered, axis=1, keepdims=True) / total
    normed = (centered * lax.rsqrt(spread + EPS) * gain_ref[...]).astype(BF16)
    lifted = hidden = None
    for k in range(count + 2):
        new_lifted = new_hidden = None
        if k < count:
            next_copy()
            p, part = divmod(k, steps)
            new_lifted = matmul(normed, up_ref[p, :, part * block : (part + 1) * block])
        if lifted is not None:
            new_hidden = gelu(lifted).astype(BF16)
        if k >= 2:
            next_copy()
            p, part = divmod(k - 2, steps)
            sums_ref[...] += matmul(hidden, down_ref[p, part * block : (part + 1) * block, :])
        lifted, hidden = new_lifted, new_hidden
    for p in range(pieces):
        cols = pl.ds(pl.multiple_of(places[p] * width, LANES), width)
        out_refs[p][...] = sums_ref[:, cols].astype(BF16)


def join_kernel(*refs, pieces, share):
    out_hbm, sems = refs[pieces:]
    me = lax.axis_index("chan")
    copies = []
    for p in range(pieces):
        start = lax.rem(me + pieces - p, pieces) * share
        rows = pl.ds(pl.multiple_of(start, 16), share)
        copies.append(pltpu.make_async_copy(refs[p], out_hbm.at[rows], sems.at[p]))
    for copy in copies:
        copy.start()
    for copy in copies:
        copy.wait()


HBM = pl.BlockSpec(memory_space=pltpu.HBM)
VMEM = pl.BlockSpec(memory_space=pltpu.VMEM)


def call(kernel, in_specs, out_specs, out_shape, scratch, megabytes, *args):
    kinds = {"h": HBM, "v": VMEM, "c": VMEM}
    spaces = {"h": pltpu.HBM, "v": pltpu.VMEM, "c": pltpu.HBM}
    placed = [
        pltpu.with_memory_space_constraint(arg, spaces[kind])
        for kind, arg in zip(in_specs, args, strict=True)
    ]
    return pl.pallas_call(
        kernel,
        in_specs=[kinds[kind] for kind in in_specs],
        out_specs=out_specs,
        out_shape=out_shape,
        scratch_shapes=scratch,
        compiler_params=pltpu.CompilerParams(vmem_limit_bytes=megabytes * 1024 * 1024),
    )(*placed)


def shape_of(shape, dtype):
    return jax.ShapeDtypeStruct(shape, dtype)


def per_device(
    layer_input, gain_first, in_weight, short_weight, filt_in, filt_bias, filt_mid, filt_out,
    decay_rate, conv_bias, out_weight, gain_second, up_weight, down_weight,
):
    tokens, width = layer_input.shape
    pieces = lax.axis_size("chan")
    groups = lax.axis_size("seq")
    model = pieces * width
    length = tokens * groups
    share = tokens // pieces
    own = width // groups
    own_rows = -(-own // 16) * 16
    block_rows = tokens // LANES * own_rows + 16

    def turned(array, by):
        if by == 0:
            return array
        return lax.ppermute(array, "chan", [(i, (i - by) % pieces) for i in range(pieces)])

    def all_turned(array):
        return [turned(array, p) for p in range(pieces)]

    x_pieces = all_turned(layer_input)
    by_role = jnp.transpose(in_weight, (1, 0, 2))
    step = min(width, 256)
    normed, my_rows, gated = call(
        functools.partial(
            project_kernel, pieces=pieces, tokens=tokens, width=width, own=own, own_rows=own_rows, share=share
        ),
        "c" + "v" * (pieces - 1) + "cch",
        (HBM, HBM, HBM),
        (
            pltpu.HBM((pieces, tokens, width), BF16),
            pltpu.HBM((pieces, share, width), BF16),
            pltpu.HBM((groups, block_rows, LANES), BF16),
        ),
        [
            pltpu.VMEM((3, model, width), BF16),
            pltpu.VMEM((2, tokens + 8, step), F32),
            pltpu.VMEM((groups, block_rows, LANES), BF16),
            pltpu.VMEM((pieces, tokens, width), BF16),
            pltpu.SemaphoreType.DMA((3,)),
            pltpu.SemaphoreType.DMA((width // step,)),
            pltpu.SemaphoreType.DMA,
            pltpu.SemaphoreType.DMA((pieces,)),
        ],
        20,
        *x_pieces, gain_first.reshape(pieces, 1, width), short_weight, by_role,
    )
    by_role, out_weight, up_weight, down_weight, gated = lax.optimization_barrier(
        (by_role, out_weight, up_weight, down_weight, gated)
    )
    regrouped = lax.all_to_all(gated, "seq", split_axis=0, concat_axis=0, tiled=True)

    tables = {name: jnp.asarray(table) for name, table in transform_tables(length).items()}
    padded = tables["turn"].shape[1]
    rows = length // LANES
    filters = filt_mid.shape[0]
    spectrum, own_taps, own_direct, gate_taps = call(
        functools.partial(filter_kernel, length=length, own=own, group=own),
        "c" * 10,
        (VMEM,) * 4,
        (
            pltpu.HBM((own * padded, 2 * LANES), F32),
            pltpu.VMEM((KSHORT, 8, LANES), F32),
            pltpu.VMEM((own, LANES), F32),
            pltpu.VMEM((KSHORT, width), F32),
        ),
        [
            pltpu.VMEM((own * rows, LANES), F32),
            pltpu.VMEM((width, filters), F32),
            pltpu.VMEM((width, 8), F32),
            pltpu.VMEM((32, filters), F32),
        ],
        24,
        filt_in, filt_bias[None, :], filt_mid, filt_out, decay_rate[None, :], conv_bias[None, :],
        short_weight, tables["turn"], tables["square"], tables["forward3"],
    )
    places = pieces if share % LANES == 0 else 1
    kept_tables = [tables[name] for name in ("turn", "square", "forward2", "inverse3")]
    convolved, side = call(
        functools.partial(
            convolve_kernel, length=length, own=own, own_rows=own_rows, group=own, tokens=tokens, places=places
        ),
        "vvvv" + "h" * 5,
        (HBM, VMEM),
        (pltpu.HBM((places * groups, own, tokens // places), BF16), shape_of((8, width), F32)),
        [
            pltpu.VMEM((own * rows, LANES), F32),
            pltpu.VMEM((own * rows, LANES), F32),
            pltpu.VMEM((places * groups, own, tokens // places), BF16),
            *(pltpu.VMEM(array.shape, array.dtype) for array in (spectrum, *kept_tables)),
            pltpu.SemaphoreType.DMA((5,)),
            pltpu.SemaphoreType.DMA((2 * places,)),
        ],
        40,
        regrouped, own_taps, own_direct, gate_taps, spectrum, *kept_tables,
    )
    if places != pieces:
        convolved = jnp.transpose(convolved.reshape(groups, own, pieces, share), (2, 0, 1, 3))
        convolved = convolved.reshape(pieces * groups, own, share)
    returned = lax.all_to_all(convolved, ("chan", "seq"), split_axis=0, concat_axis=0, tiled=True)
    returned = returned.reshape(pieces, width, share)

    mix_weights = all_turned(out_weight)
    up_weights = all_turned(up_weight)
    down_weights = all_turned(down_weight)
    rest = 64
    gate, mix_kept = call(
        functools.partial(gate_kernel, pieces=pieces, share=share, width=width, rest=rest),
        "c" + "v" * pieces + "h" * (2 * pieces),
        (VMEM, VMEM),
        (pltpu.VMEM((pieces, width, share), F32), pltpu.VMEM((model - rest, model), BF16)),
        [
            pltpu.VMEM((pieces, model, width), BF16),
            pltpu.VMEM((pieces, share + HALO, width), BF16),
            pltpu.VMEM((share + HALO, width), F32),
            pltpu.SemaphoreType.DMA((pieces,)),
            pltpu.SemaphoreType.DMA((pieces,)),
        ],
        16,
        normed, *all_turned(side), *all_turned(by_role), *mix_weights,
    )
    units = up_weight.shape[1]
    block = min(512, units)
    results = call(
        functools.partial(tail_kernel, pieces=pieces, share=share, width=width, block=block, rest=rest),
        "vvvch" + "h" * (1 + 2 * pieces),
        (VMEM,) * pieces,
        tuple(shape_of((share, width), BF16) for p in range(pieces)),
        [
            pltpu.VMEM((share, model), F32),
            pltpu.VMEM((pieces, share, width), BF16),
            pltpu.VMEM((rest, model), BF16),
            pltpu.VMEM((pieces, model, units), BF16),
            pltpu.VMEM((pieces, units, model), BF16),
            pltpu.SemaphoreType.DMA((2,)),
            pltpu.SemaphoreType.DMA((pieces, units // block)),
            pltpu.SemaphoreType.DMA((pieces, units // block)),
        ],
        44,
        returned, gate, mix_kept, gain_second[None, :], my_rows, mix_weights[-1], *up_weights, *down_weights,
    )
    received = [results[0]] + [
        lax.ppermute(results[p], "chan", [(i, (i + p) % pieces) for i in range(pieces)])
        for p in range(1, pieces)
    ]
    return call(
        functools.partial(join_kernel, pieces=pieces, share=share),
        "v" * pieces,
        HBM,
        pltpu.HBM((tokens, width), BF16),
        [pltpu.SemaphoreType.DMA((pieces,))],
        8,
        *received,
    )


def solution(mesh):
    placed = (
        P("seq", "chan"),
        P(),
        P(None, None, "chan"),
        P(None, None, "chan"),
        P(),
        P(),
        P(),
        P(None, "chan"),
        P("chan"),
        P("chan"),
        P("chan", None),
        P(),
        P(None, "chan"),
        P("chan", None),
    )
    return jax.shard_map(
        per_device, mesh=mesh, in_specs=placed, out_specs=P("seq", "chan"), check_vma=False
    )
```

time: 79.7 us -> 74.6 us (0.936)
  the two profiles are of different devices: /device:TPU:17 before, /device:TPU:0 now
where the time goes in v3:
time: 74.6 us; the launch traced here: 74.2 us
  Pallas kernels  39.4 us (53%)
  waiting for transfers between devices  21 us (28%)
  starting transfers between devices  13.5 us (18%)
    pallas_call x6, Pallas kernels, call(): pl.pallas_call(kernel, in_specs=[kinds[kind] for kind in in_specs], out_s...  39.4 us
    all_to_all x1, waiting for transfers between devices, per_device(): lax.all_to_all(convolved, ('chan', 'seq'), split_axis=0, concat_axis=0, t...  11.4 us
    all_to_all x1, starting transfers between devices, per_device(): lax.all_to_all(gated, 'seq', split_axis=0, concat_axis=0, tiled=True)  8.19 us
    all_to_all x1, waiting for transfers between devices, per_device(): lax.all_to_all(gated, 'seq', split_axis=0, concat_axis=0, tiled=True)  5.38 us
    all_to_all x1, starting transfers between devices, per_device(): lax.all_to_all(convolved, ('chan', 'seq'), split_axis=0, concat_axis=0, t...  3.33 us
    ppermute x6, waiting for transfers between devices, turned(): lax.ppermute(array, 'chan', [(i, (i - by) % pieces) for i in range(pieces)])  2.69 us
    ppermute x6, starting transfers between devices, turned(): lax.ppermute(array, 'chan', [(i, (i - by) % pieces) for i in range(pieces)])  1.86 us
    ppermute x1, waiting for transfers between devices, per_device(): lax.ppermute(results[p], 'chan', [(i, (i + p) % pieces) for i in range(pi...  1.52 us
  transfers between devices with their start and end apart: 9, of which 5 were waited for; matrix products, arithmetic and copies ran while one was open for 0% of the time, Pallas kernels for 31%

profile of v3, /device:TPU:0, one launch (start us, length us, event | category | flops | bytes accessed | tf_op | source)
XLA Modules:
  0.0 74.2 jit_solution(1695421333994986807)
XLA Ops:
  0.0 0.0 copy-start.1
  0.0 0.5 collective-permute-start
  0.5 1.7 %collective-permute-done.refs_1_ = bf16[512,512]{1,0:T(8,128)(2,1)S(1)} collective-permute-done((bf16[512,512]{1,0:T(8,128)(2,1)}, bf16[512,512]{1,0:T(8,128)(2,1)S(1)}, u32[]{:S(2)}, u32[]{:S(2)}) %collective-permute-start) | collective-permute-done | bytes 524320 | tf_op jit(solution)/shard_map/ppermute | solution.py:586
  2.2 6.0 %shard_map.181 = (bf16[2,512,512]{2,1,0:T(8,128)(2,1)}, bf16[2,256,512]{2,1,0:T(8,128)(2,1)}, bf16[16,144,128]{2,1,0:T(8,128)(2,1)}) custom-call(bf16[512,512]{1,0:T(8,128)(2,1)} %refs_0_.1, bf16[512,512]{1,0:T(8,128)(2,1)S(1)} %collective-permute-done.refs_1_, f32[2,1,512]{2,1,0:T(1,128)} %bitcast.8, f32[3,3,512]{2,1,0:T(4,128)} %taps_ref.1, ...), custom_call_target="tpu_custom_call" | custom-call | tf_op jit(solution)/shard_map/pallas_call | solution.py:555
  8.2 0.4 collective-permute-start.4
  8.6 0.1 collective-permute-start.5
  8.8 0.4 collective-permute-start.2
  9.1 8.2 %all-to-all-start = ((bf16[16,144,128]{2,1,0:T(8,128)(2,1)}), bf16[16,144,128]{2,1,0:T(8,128)(2,1)S(1)}, u32[]{:S(2)}, u32[]{:S(2)}) async-start(bf16[16,144,128]{2,1,0:T(8,128)(2,1)} %get-tuple-element.24), calls=%async_computation | async-start | bytes 1179648 | tf_op jit(solution)/shard_map/all_to_all | solution.py:621
  17.3 0.0 copy-done.1
  17.4 0.1 collective-permute-start.3
  17.5 10.9 %shard_map.182 = (f32[2304,256]{1,0:T(8,128)}, f32[3,8,128]{2,1,0:T(8,128)S(1)}, f32[32,128]{1,0:T(8,128)S(1)}, f32[3,512]{1,0:T(4,128)S(1)}) custom-call(bf16[25,64]{1,0:T(8,128)(2,1)} %in_ref.1, f32[1,64]{1,0:T(1,128)} %bitcast.12, bf16[64,64]{1,0:T(8,128)(2,1)} %mid_w_ref.1, bf16[64,512]{1,0:T(8,128)(2,1)} %out_w_ref.1, f32[1,512]{1,0:T(1,128)} %bitcast.10, ...), custom_call_target="tpu_custom_call" | custom-call | tf_op jit(solution)/shard_map/pallas_call | solution.py:555
  28.4 5.4 %all-to-all-done.x_ref = bf16[16,144,128]{2,1,0:T(8,128)(2,1)S(1)} async-done(((bf16[16,144,128]{2,1,0:T(8,128)(2,1)}), bf16[16,144,128]{2,1,0:T(8,128)(2,1)S(1)}, u32[]{:S(2)}, u32[]{:S(2)}) %all-to-all-start) | async-done | bytes 589856 | tf_op jit(solution)/shard_map/all_to_all | solution.py:621
  33.8 8.0 %shard_map.183 = (bf16[32,32,256]{2,1,0:T(8,128)(2,1)}, f32[8,512]{1,0:T(8,128)S(1)}) custom-call(bf16[16,144,128]{2,1,0:T(8,128)(2,1)S(1)} %all-to-all-done.x_ref, f32[3,8,128]{2,1,0:T(8,128)S(1)} %get-tuple-element.25.taps_ref, f32[32,128]{1,0:T(8,128)S(1)} %get-tuple-element.26.direct_ref, f32[3,512]{1,0:T(4,128)S(1)} %get-tuple-element.27.gate_taps_ref, ...), custom_call_target="tpu_custom_call" | custom-call | tf_op jit(solution)/shard_map/pallas_call | solution.py:555
  41.8 3.3 %all-to-all-start.1 = ((bf16[32,32,256]{2,1,0:T(8,128)(2,1)}), bf16[32,32,256]{2,1,0:T(8,128)(2,1)S(1)}, u32[]{:S(2)}, u32[]{:S(2)}) async-start(bf16[32,32,256]{2,1,0:T(8,128)(2,1)} %get-tuple-element.29), calls=%async_computation.1 | async-start | bytes 1048576 | tf_op jit(solution)/shard_map/all_to_all | solution.py:670
  45.1 0.3 collective-permute-start.1
  45.5 0.0 collective-permute-done.3.refs_5_.refs_0_
  45.5 0.0 copy-start
  45.5 0.9 %collective-permute-done.1.refs_1_ = f32[8,512]{1,0:T(8,128)S(1)} collective-permute-done((f32[8,512]{1,0:T(8,128)S(1)}, f32[8,512]{1,0:T(8,128)S(1)}, u32[]{:S(2)}, u32[]{:S(2)}) %collective-permute-start.1) | collective-permute-done | bytes 16416 | tf_op jit(solution)/shard_map/ppermute | solution.py:586
  46.4 0.0 collective-permute-done.2.refs_3_
  46.4 0.1 copy-done
  46.5 4.1 %shard_map.184 = (f32[2,512,256]{2,1,0:T(8,128)S(1)}, bf16[960,1024]{1,0:T(8,128)(2,1)S(1)}) custom-call(bf16[2,512,512]{2,1,0:T(8,128)(2,1)} %get-tuple-element.30.normed_ref, f32[8,512]{1,0:T(8,128)S(1)} %get-tuple-element.31.refs_0_, f32[8,512]{1,0:T(8,128)S(1)} %collective-permute-done.1.refs_1_, bf16[3,1024,512]{2,1,0:T(8,128)(2,1)} %bitcast.refs_4_.refs_2_, ...), custom_call_target="tpu_custom_call" | custom-call | tf_op jit(solution)/shard_map/pallas_call | solution.py:555
  50.5 11.4 %all-to-all-done.1 = bf16[32,32,256]{2,1,0:T(8,128)(2,1)S(1)} async-done(((bf16[32,32,256]{2,1,0:T(8,128)(2,1)}), bf16[32,32,256]{2,1,0:T(8,128)(2,1)S(1)}, u32[]{:S(2)}, u32[]{:S(2)}) %all-to-all-start.1) | async-done | bytes 524320 | tf_op jit(solution)/shard_map/all_to_all | solution.py:670
  62.0 0.0 collective-permute-done.4.refs_2_
  62.0 0.0 collective-permute-done.5.refs_4_
  62.0 9.6 %shard_map.185 = (bf16[256,512]{1,0:T(8,128)(2,1)S(1)}, bf16[256,512]{1,0:T(8,128)(2,1)S(1)}) custom-call(bf16[2,512,256]{2,1,0:T(8,128)(2,1)S(1)} %bitcast.7, f32[2,512,256]{2,1,0:T(8,128)S(1)} %get-tuple-element.34.gate_ref, bf16[960,1024]{1,0:T(8,128)(2,1)S(1)} %get-tuple-element.35.mix_ref, f32[1,1024]{1,0:T(1,128)} %bitcast.9, ...), custom_call_target="tpu_custom_call" | custom-call | tf_op jit(solution)/shard_map/pallas_call | solution.py:555
  71.6 0.1 collective-permute-start.6
  71.6 1.5 %collective-permute-done.6.refs_1_ = bf16[256,512]{1,0:T(8,128)(2,1)S(1)} collective-permute-done((bf16[256,512]{1,0:T(8,128)(2,1)S(1)}, bf16[256,512]{1,0:T(8,128)(2,1)S(1)}, u32[]{:S(2)}, u32[]{:S(2)}) %collective-permute-start.6) | collective-permute-done | bytes 262176 | tf_op jit(solution)/shard_map/ppermute | solution.py:713
  73.2 0.8 %shard_map.186 = bf16[512,512]{1,0:T(8,128)(2,1)} custom-call(bf16[256,512]{1,0:T(8,128)(2,1)S(1)} %get-tuple-element.39.refs_0_, bf16[256,512]{1,0:T(8,128)(2,1)S(1)} %collective-permute-done.6.refs_1_), custom_call_target="tpu_custom_call" | custom-call | tf_op jit(solution)/shard_map/pallas_call | solution.py:555
Async XLA Ops:
  0.0 17.3 %copy-start.1 = (bf16[512,1024]{1,0:T(8,128)(2,1)S(1)}, bf16[512,1024]{1,0:T(8,128)(2,1)}, u32[]{:S(2)}) copy-start(bf16[512,1024]{1,0:T(8,128)(2,1)} %refs_4_) | copy-start | bytes 3145732
  0.0 2.2 %collective-permute-start = (bf16[512,512]{1,0:T(8,128)(2,1)}, bf16[512,512]{1,0:T(8,128)(2,1)S(1)}, u32[]{:S(2)}, u32[]{:S(2)}) collective-permute-start(bf16[512,512]{1,0:T(8,128)(2,1)} %refs_0_.1), channel_id=1, source_target_pairs={{0,1},{1,0},{2,3},{3,2},{4,5},{5,4},{6,7},{7,6},{8,9},{9,8},{10,11... | collective-permute-start | bytes 1572872 | tf_op jit(solution)/shard_map/ppermute | solution.py:586
  8.2 53.8 %collective-permute-start.4 = (bf16[1024,2048]{1,0:T(8,128)(2,1)}, bf16[1024,2048]{1,0:T(8,128)(2,1)}, u32[]{:S(2)}, u32[]{:S(2)}) collective-permute-start(bf16[1024,2048]{1,0:T(8,128)(2,1)} %refs_1_), channel_id=1, source_target_pairs={{0,1},{1,0},{2,3},{3,2},{4,5},{5,4},{6,7},{7,6},{8,9},{9,8},{10,11... | collective-permute-start | bytes 12582920 | tf_op jit(solution)/shard_map/ppermute | solution.py:586
  8.6 53.3 %collective-permute-start.5 = (bf16[2048,1024]{1,0:T(8,128)(2,1)}, bf16[2048,1024]{1,0:T(8,128)(2,1)}, u32[]{:S(2)}, u32[]{:S(2)}) collective-permute-start(bf16[2048,1024]{1,0:T(8,128)(2,1)} %refs_3_.2), channel_id=1, source_target_pairs={{0,1},{1,0},{2,3},{3,2},{4,5},{5,4},{6,7},{7,6},{8,9},{9,8},{10,11... | collective-permute-start | bytes 12582920 | tf_op jit(solution)/shard_map/ppermute | solution.py:586
  8.8 37.6 %collective-permute-start.2 = (bf16[3,1024,512]{2,1,0:T(8,128)(2,1)}, bf16[3,1024,512]{2,1,0:T(8,128)(2,1)}, u32[]{:S(2)}, u32[]{:S(2)}) collective-permute-start(bf16[3,1024,512]{2,1,0:T(8,128)(2,1)} %bitcast.refs_4_.refs_2_), channel_id=1, source_target_pairs={{0,1},{1,0},{2,3},{3,2},{4,5},{5,4},{6,7},{7,6},{8,9},{9,8},{10,11... | collective-permute-start | bytes 9437192 | tf_op jit(solution)/shard_map/ppermute | solution.py:586
  9.1 24.6 %all-to-all-start = ((bf16[16,144,128]{2,1,0:T(8,128)(2,1)}), bf16[16,144,128]{2,1,0:T(8,128)(2,1)S(1)}, u32[]{:S(2)}, u32[]{:S(2)}) async-start(bf16[16,144,128]{2,1,0:T(8,128)(2,1)} %get-tuple-element.24), calls=%async_computation | async-start | bytes 1179648 | tf_op jit(solution)/shard_map/all_to_all | solution.py:621
  17.4 28.1 %collective-permute-start.3 = (bf16[512,1024]{1,0:T(8,128)(2,1)S(1)}, bf16[512,1024]{1,0:T(8,128)(2,1)S(1)}, u32[]{:S(2)}, u32[]{:S(2)}) collective-permute-start(bf16[512,1024]{1,0:T(8,128)(2,1)S(1)} %copy-done.1), channel_id=1, source_target_pairs={{0,1},{1,0},{2,3},{3,2},{4,5},{5,4},{6,7},{7,6},{8,9},{9,8},{10,11... | collective-permute-start | bytes 3145736 | tf_op jit(solution)/shard_map/ppermute | solution.py:586
  41.8 20.2 %all-to-all-start.1 = ((bf16[32,32,256]{2,1,0:T(8,128)(2,1)}), bf16[32,32,256]{2,1,0:T(8,128)(2,1)S(1)}, u32[]{:S(2)}, u32[]{:S(2)}) async-start(bf16[32,32,256]{2,1,0:T(8,128)(2,1)} %get-tuple-element.29), calls=%async_computation.1 | async-start | bytes 1048576 | tf_op jit(solution)/shard_map/all_to_all | solution.py:670
  45.1 1.2 %collective-permute-start.1 = (f32[8,512]{1,0:T(8,128)S(1)}, f32[8,512]{1,0:T(8,128)S(1)}, u32[]{:S(2)}, u32[]{:S(2)}) collective-permute-start(f32[8,512]{1,0:T(8,128)S(1)} %get-tuple-element.31.refs_0_), channel_id=1, source_target_pairs={{0,1},{1,0},{2,3},{3,2},{4,5},{5,4},{6,7},{7,6},{8,9},{9,8},{10,11... | collective-permute-start | bytes 49160 | tf_op jit(solution)/shard_map/ppermute | solution.py:586
  45.5 1.0 %copy-start = (bf16[512,1024]{1,0:T(8,128)(2,1)}, bf16[512,1024]{1,0:T(8,128)(2,1)S(1)}, u32[]{:S(2)}) copy-start(bf16[512,1024]{1,0:T(8,128)(2,1)S(1)} %collective-permute-done.3.refs_5_.refs_0_) | copy-start | bytes 3145732
  71.6 1.6 %collective-permute-start.6 = (bf16[256,512]{1,0:T(8,128)(2,1)S(1)}, bf16[256,512]{1,0:T(8,128)(2,1)S(1)}, u32[]{:S(2)}, u32[]{:S(2)}) collective-permute-start(bf16[256,512]{1,0:T(8,128)(2,1)S(1)} %get-tuple-element.40), channel_id=1, source_target_pairs={{0,1},{1,0},{2,3},{3,2},{4,5},{5,4},{6,7},{7,6},{8,9},{9,8},{10,11... | collective-permute-start | bytes 786440 | tf_op jit(solution)/shard_map/ppermute | solution.py:713

commit v4 on v3

--- a/solution.py
+++ b/solution.py
@@ -109,6 +109,8 @@
         for side in range(2):
             lanes = slice(side * LANES, (side + 1) * LANES)
             stacked.append(jnp.concatenate([turned_real[:, lanes], turned_imag[:, lanes]], 1))
+    if mid_low is None:
+        return matmul(jnp.concatenate(stacked, 0).astype(BF16), mid_high)
     high, low = split_parts(jnp.concatenate(stacked, 0))
     return matmul(high, mid_high) + matmul(low, mid_high) + matmul(high, mid_low)
 
@@ -384,7 +386,7 @@
             return jnp.concatenate([values, values], 0)
 
         signal = rows_to_spectrum(
-            load_pair, group, forward_ref[...], turn_cos, turn_sin, square_ref[0], square_ref[1], padded
+            load_pair, group, forward_ref[...], turn_cos, turn_sin, square_ref[0], None, padded
         )
         if own == group:
             for load in loads[3:]:
@@ -395,10 +397,7 @@
         product = jnp.concatenate(
             [s_real * f_real - s_imag * f_imag, s_real * f_imag + s_imag * f_real], 1
         )
-        high, low = split_parts(product)
-        mixed = (
-            matmul(high, square_ref[2]) + matmul(low, square_ref[2]) + matmul(high, square_ref[3])
-        )
+        mixed = matmul(product.astype(BF16), square_ref[2])
         for pair in range(group // 2):
             first = mixed[2 * pair * padded : (2 * pair + 1) * padded]
             second = mixed[(2 * pair + 1) * padded : (2 * pair + 2) * padded]
@@ -431,14 +430,13 @@
         place, side = divmod(part, share_rows)
         values = result_ref[pl.ds(row, own, stride=rows), :]
         values = values + bias * signal_ref[pl.ds(row, own, stride=rows), :]
-        target = place * blocks + block
+        target = block * places + place
         out_ref[target, :, side * LANES : (side + 1) * LANES] = values.astype(BF16)
         if part == per_block - 1 and (block + 1) % half == 0:
-            for p in range(places):
-                span = pl.ds(p * blocks + block + 1 - half, half)
-                store = pltpu.make_async_copy(out_ref.at[span], out_hbm.at[span], out_sems.at[len(stores)])
-                store.start()
-                stores.append(store)
+            span = pl.ds((block + 1 - half) * places, half * places)
+            store = pltpu.make_async_copy(out_ref.at[span], out_hbm.at[span], out_sems.at[len(stores)])
+            store.start()
+            stores.append(store)
     for store in stores:
         store.wait()
 
@@ -491,7 +489,7 @@
     dims = (((0,), (0,)), ((), ()))
     sums = 0.0
     for p in range(pieces):
-        mixed = (z_ref[places[p]].astype(F32) * gate_ref[p]).astype(BF16)
+        mixed = (z_ref[:, places[p]].reshape(width, share).astype(F32) * gate_ref[p]).astype(BF16)
         size = width - rest if p == pieces - 1 else width
         kept = mix_ref[p * width : p * width + size, :]
         sums = sums + lax.dot_general(mixed[:size], kept, dims, preferred_element_type=F32)
@@ -659,16 +657,18 @@
             pltpu.VMEM((places * groups, own, tokens // places), BF16),
             *(pltpu.VMEM(array.shape, array.dtype) for array in (spectrum, *kept_tables)),
             pltpu.SemaphoreType.DMA((5,)),
-            pltpu.SemaphoreType.DMA((2 * places,)),
+            pltpu.SemaphoreType.DMA((2,)),
         ],
         40,
         regrouped, own_taps, own_direct, gate_taps, spectrum, *kept_tables,
     )
     if places != pieces:
-        convolved = jnp.transpose(convolved.reshape(groups, own, pieces, share), (2, 0, 1, 3))
-        convolved = convolved.reshape(pieces * groups, own, share)
-    returned = lax.all_to_all(convolved, ("chan", "seq"), split_axis=0, concat_axis=0, tiled=True)
-    returned = returned.reshape(pieces, width, share)
+        convolved = jnp.transpose(convolved.reshape(groups, own, pieces, share), (0, 2, 1, 3))
+        convolved = convolved.reshape(groups * pieces, own, share)
+    returned = lax.all_to_all(convolved, ("seq", "chan"), split_axis=0, concat_axis=0, tiled=True)
+    returned = returned.reshape(groups, pieces, own, share)
+    if own % 16:
+        returned = jnp.transpose(returned, (1, 0, 2, 3)).reshape(1, pieces, width, share)
 
     mix_weights = all_turned(out_weight)
     up_weights = all_turned(up_weight)

time: 74.6 us -> 70.7 us (0.948)
  Pallas kernels: 39.4 us -> 36.8 us
  waiting for transfers between devices: 21 us -> 20 us
    pallas_call x6, Pallas kernels: 39.4 us -> 36.8 us  [call(): pl.pallas_call(kernel, in_specs=[kinds[kind] for kind in in_specs], out_s...]
    all_to_all x1, waiting for transfers between devices: 11.4 us -> 9.99 us  [per_device(): lax.all_to_all(convolved, ('seq', 'chan'), split_axis=0, concat_axis=0, t...]
  transfers between devices with their start and end apart: 9 -> 9, of which waited for: 5 -> 5; matrix products, arithmetic and copies ran while one was open for 0% -> 0% of each run, Pallas kernels for 31% -> 29%
where the time goes in v4:
time: 70.7 us; the launch traced here: 70.3 us
  Pallas kernels  36.8 us (52%)
  waiting for transfers between devices  20 us (28%)
  starting transfers between devices  13.3 us (19%)
    pallas_call x6, Pallas kernels, call(): pl.pallas_call(kernel, in_specs=[kinds[kind] for kind in in_specs], out_s...  36.8 us
    all_to_all x1, waiting for transfers between devices, per_device(): lax.all_to_all(convolved, ('seq', 'chan'), split_axis=0, concat_axis=0, t...  9.99 us
    all_to_all x1, starting transfers between devices, per_device(): lax.all_to_all(gated, 'seq', split_axis=0, concat_axis=0, tiled=True)  8.02 us
    all_to_all x1, waiting for transfers between devices, per_device(): lax.all_to_all(gated, 'seq', split_axis=0, concat_axis=0, tiled=True)  5.54 us
    all_to_all x1, starting transfers between devices, per_device(): lax.all_to_all(convolved, ('seq', 'chan'), split_axis=0, concat_axis=0, t...  3.55 us
    ppermute x6, waiting for transfers between devices, turned(): lax.ppermute(array, 'chan', [(i, (i - by) % pieces) for i in range(pieces)])  2.9 us
    ppermute x6, starting transfers between devices, turned(): lax.ppermute(array, 'chan', [(i, (i - by) % pieces) for i in range(pieces)])  1.65 us
    ppermute x1, waiting for transfers between devices, per_device(): lax.ppermute(results[p], 'chan', [(i, (i + p) % pieces) for i in range(pi...  1.52 us
  transfers between devices with their start and end apart: 9, of which 5 were waited for; matrix products, arithmetic and copies ran while one was open for 0% of the time, Pallas kernels for 29%

profile of v4, /device:TPU:0, one launch (start us, length us, event | category | flops | bytes accessed | tf_op | source)
XLA Modules:
  0.0 70.3 jit_solution(9576994599656887003)
XLA Ops:
  0.0 0.0 copy-start.1
  0.0 0.5 collective-permute-start
  0.5 1.7 %collective-permute-done.refs_1_ = bf16[512,512]{1,0:T(8,128)(2,1)S(1)} collective-permute-done((bf16[512,512]{1,0:T(8,128)(2,1)}, bf16[512,512]{1,0:T(8,128)(2,1)S(1)}, u32[]{:S(2)}, u32[]{:S(2)}) %collective-permute-start) | collective-permute-done | bytes 524320 | tf_op jit(solution)/shard_map/ppermute | solution.py:584
  2.2 6.0 %shard_map.181 = (bf16[2,512,512]{2,1,0:T(8,128)(2,1)}, bf16[2,256,512]{2,1,0:T(8,128)(2,1)}, bf16[16,144,128]{2,1,0:T(8,128)(2,1)}) custom-call(bf16[512,512]{1,0:T(8,128)(2,1)} %refs_0_.1, bf16[512,512]{1,0:T(8,128)(2,1)S(1)} %collective-permute-done.refs_1_, f32[2,1,512]{2,1,0:T(1,128)} %bitcast.8, f32[3,3,512]{2,1,0:T(4,128)} %taps_ref.1, ...), custom_call_target="tpu_custom_call" | custom-call | tf_op jit(solution)/shard_map/pallas_call | solution.py:553
  8.2 0.4 collective-permute-start.4
  8.6 0.1 collective-permute-start.5
  8.8 0.4 collective-permute-start.2
  9.1 8.0 %all-to-all-start = ((bf16[16,144,128]{2,1,0:T(8,128)(2,1)}), bf16[16,144,128]{2,1,0:T(8,128)(2,1)S(1)}, u32[]{:S(2)}, u32[]{:S(2)}) async-start(bf16[16,144,128]{2,1,0:T(8,128)(2,1)} %get-tuple-element.24), calls=%async_computation | async-start | bytes 1179648 | tf_op jit(solution)/shard_map/all_to_all | solution.py:619
  17.2 0.0 copy-done.1
  17.2 0.1 collective-permute-start.3
  17.3 10.9 %shard_map.182 = (f32[2304,256]{1,0:T(8,128)}, f32[3,8,128]{2,1,0:T(8,128)S(1)}, f32[32,128]{1,0:T(8,128)S(1)}, f32[3,512]{1,0:T(4,128)S(1)}) custom-call(bf16[25,64]{1,0:T(8,128)(2,1)} %in_ref.1, f32[1,64]{1,0:T(1,128)} %bitcast.12, bf16[64,64]{1,0:T(8,128)(2,1)} %mid_w_ref.1, bf16[64,512]{1,0:T(8,128)(2,1)} %out_w_ref.1, f32[1,512]{1,0:T(1,128)} %bitcast.10, ...), custom_call_target="tpu_custom_call" | custom-call | tf_op jit(solution)/shard_map/pallas_call | solution.py:553
  28.2 5.5 %all-to-all-done.x_ref = bf16[16,144,128]{2,1,0:T(8,128)(2,1)S(1)} async-done(((bf16[16,144,128]{2,1,0:T(8,128)(2,1)}), bf16[16,144,128]{2,1,0:T(8,128)(2,1)S(1)}, u32[]{:S(2)}, u32[]{:S(2)}) %all-to-all-start) | async-done | bytes 589856 | tf_op jit(solution)/shard_map/all_to_all | solution.py:619
  33.8 5.4 %shard_map.183 = (bf16[32,32,256]{2,1,0:T(8,128)(2,1)}, f32[8,512]{1,0:T(8,128)S(1)}) custom-call(bf16[16,144,128]{2,1,0:T(8,128)(2,1)S(1)} %all-to-all-done.x_ref, f32[3,8,128]{2,1,0:T(8,128)S(1)} %get-tuple-element.25.taps_ref, f32[32,128]{1,0:T(8,128)S(1)} %get-tuple-element.26.direct_ref, f32[3,512]{1,0:T(4,128)S(1)} %get-tuple-element.27.gate_taps_ref, ...), custom_call_target="tpu_custom_call" | custom-call | tf_op jit(solution)/shard_map/pallas_call | solution.py:553
  39.2 3.6 %all-to-all-start.1 = ((bf16[32,32,256]{2,1,0:T(8,128)(2,1)}), bf16[32,32,256]{2,1,0:T(8,128)(2,1)S(1)}, u32[]{:S(2)}, u32[]{:S(2)}) async-start(bf16[32,32,256]{2,1,0:T(8,128)(2,1)} %get-tuple-element.29), calls=%async_computation.1 | async-start | bytes 1048576 | tf_op jit(solution)/shard_map/all_to_all | solution.py:668
  42.7 0.1 collective-permute-start.1
  42.9 0.0 collective-permute-done.3.refs_5_.refs_0_
  42.9 0.0 copy-start
  42.9 1.1 %collective-permute-done.1.refs_1_ = f32[8,512]{1,0:T(8,128)S(1)} collective-permute-done((f32[8,512]{1,0:T(8,128)S(1)}, f32[8,512]{1,0:T(8,128)S(1)}, u32[]{:S(2)}, u32[]{:S(2)}) %collective-permute-start.1) | collective-permute-done | bytes 16416 | tf_op jit(solution)/shard_map/ppermute | solution.py:584
  44.0 0.0 collective-permute-done.2.refs_3_
  44.0 0.0 copy-done
  44.0 4.1 %shard_map.184 = (f32[2,512,256]{2,1,0:T(8,128)S(1)}, bf16[960,1024]{1,0:T(8,128)(2,1)S(1)}) custom-call(bf16[2,512,512]{2,1,0:T(8,128)(2,1)} %get-tuple-element.30.normed_ref, f32[8,512]{1,0:T(8,128)S(1)} %get-tuple-element.31.refs_0_, f32[8,512]{1,0:T(8,128)S(1)} %collective-permute-done.1.refs_1_, bf16[3,1024,512]{2,1,0:T(8,128)(2,1)} %bitcast.refs_4_.refs_2_, ...), custom_call_target="tpu_custom_call" | custom-call | tf_op jit(solution)/shard_map/pallas_call | solution.py:553
  48.1 10.0 %all-to-all-done.1 = bf16[32,32,256]{2,1,0:T(8,128)(2,1)S(1)} async-done(((bf16[32,32,256]{2,1,0:T(8,128)(2,1)}), bf16[32,32,256]{2,1,0:T(8,128)(2,1)S(1)}, u32[]{:S(2)}, u32[]{:S(2)}) %all-to-all-start.1) | async-done | bytes 524320 | tf_op jit(solution)/shard_map/all_to_all | solution.py:668
  58.1 0.0 collective-permute-done.4.refs_2_
  58.1 0.0 collective-permute-done.5.refs_4_
  58.1 9.6 %shard_map.185 = (bf16[256,512]{1,0:T(8,128)(2,1)S(1)}, bf16[256,512]{1,0:T(8,128)(2,1)S(1)}) custom-call(bf16[16,2,32,256]{3,2,1,0:T(8,128)(2,1)S(1)} %bitcast.7, f32[2,512,256]{2,1,0:T(8,128)S(1)} %get-tuple-element.34.gate_ref, bf16[960,1024]{1,0:T(8,128)(2,1)S(1)} %get-tuple-element.35.mix_ref, f32[1,1024]{1,0:T(1,128)} %bitcast.9, ...), custom_call_target="tpu_custom_call" | custom-call | tf_op jit(solution)/shard_map/pallas_call | solution.py:553
  67.7 0.1 collective-permute-start.6
  67.8 1.5 %collective-permute-done.6.refs_1_ = bf16[256,512]{1,0:T(8,128)(2,1)S(1)} collective-permute-done((bf16[256,512]{1,0:T(8,128)(2,1)S(1)}, bf16[256,512]{1,0:T(8,128)(2,1)S(1)}, u32[]{:S(2)}, u32[]{:S(2)}) %collective-permute-start.6) | collective-permute-done | bytes 262176 | tf_op jit(solution)/shard_map/ppermute | solution.py:713
  69.3 0.8 %shard_map.186 = bf16[512,512]{1,0:T(8,128)(2,1)} custom-call(bf16[256,512]{1,0:T(8,128)(2,1)S(1)} %get-tuple-element.39.refs_0_, bf16[256,512]{1,0:T(8,128)(2,1)S(1)} %collective-permute-done.6.refs_1_), custom_call_target="tpu_custom_call" | custom-call | tf_op jit(solution)/shard_map/pallas_call | solution.py:553
Async XLA Ops:
  0.0 17.2 %copy-start.1 = (bf16[512,1024]{1,0:T(8,128)(2,1)S(1)}, bf16[512,1024]{1,0:T(8,128)(2,1)}, u32[]{:S(2)}) copy-start(bf16[512,1024]{1,0:T(8,128)(2,1)} %refs_4_) | copy-start | bytes 3145732
  0.0 2.2 %collective-permute-start = (bf16[512,512]{1,0:T(8,128)(2,1)}, bf16[512,512]{1,0:T(8,128)(2,1)S(1)}, u32[]{:S(2)}, u32[]{:S(2)}) collective-permute-start(bf16[512,512]{1,0:T(8,128)(2,1)} %refs_0_.1), channel_id=1, source_target_pairs={{0,1},{1,0},{2,3},{3,2},{4,5},{5,4},{6,7},{7,6},{8,9},{9,8},{10,11... | collective-permute-start | bytes 1572872 | tf_op jit(solution)/shard_map/ppermute | solution.py:584
  8.2 49.9 %collective-permute-start.4 = (bf16[1024,2048]{1,0:T(8,128)(2,1)}, bf16[1024,2048]{1,0:T(8,128)(2,1)}, u32[]{:S(2)}, u32[]{:S(2)}) collective-permute-start(bf16[1024,2048]{1,0:T(8,128)(2,1)} %refs_1_), channel_id=1, source_target_pairs={{0,1},{1,0},{2,3},{3,2},{4,5},{5,4},{6,7},{7,6},{8,9},{9,8},{10,11... | collective-permute-start | bytes 12582920 | tf_op jit(solution)/shard_map/ppermute | solution.py:584
  8.6 49.4 %collective-permute-start.5 = (bf16[2048,1024]{1,0:T(8,128)(2,1)}, bf16[2048,1024]{1,0:T(8,128)(2,1)}, u32[]{:S(2)}, u32[]{:S(2)}) collective-permute-start(bf16[2048,1024]{1,0:T(8,128)(2,1)} %refs_3_.2), channel_id=1, source_target_pairs={{0,1},{1,0},{2,3},{3,2},{4,5},{5,4},{6,7},{7,6},{8,9},{9,8},{10,11... | collective-permute-start | bytes 12582920 | tf_op jit(solution)/shard_map/ppermute | solution.py:584
  8.8 35.2 %collective-permute-start.2 = (bf16[3,1024,512]{2,1,0:T(8,128)(2,1)}, bf16[3,1024,512]{2,1,0:T(8,128)(2,1)}, u32[]{:S(2)}, u32[]{:S(2)}) collective-permute-start(bf16[3,1024,512]{2,1,0:T(8,128)(2,1)} %bitcast.refs_4_.refs_2_), channel_id=1, source_target_pairs={{0,1},{1,0},{2,3},{3,2},{4,5},{5,4},{6,7},{7,6},{8,9},{9,8},{10,11... | collective-permute-start | bytes 9437192 | tf_op jit(solution)/shard_map/ppermute | solution.py:584
  9.1 24.6 %all-to-all-start = ((bf16[16,144,128]{2,1,0:T(8,128)(2,1)}), bf16[16,144,128]{2,1,0:T(8,128)(2,1)S(1)}, u32[]{:S(2)}, u32[]{:S(2)}) async-start(bf16[16,144,128]{2,1,0:T(8,128)(2,1)} %get-tuple-element.24), calls=%async_computation | async-start | bytes 1179648 | tf_op jit(solution)/shard_map/all_to_all | solution.py:619
  17.2 25.7 %collective-permute-start.3 = (bf16[512,1024]{1,0:T(8,128)(2,1)S(1)}, bf16[512,1024]{1,0:T(8,128)(2,1)S(1)}, u32[]{:S(2)}, u32[]{:S(2)}) collective-permute-start(bf16[512,1024]{1,0:T(8,128)(2,1)S(1)} %copy-done.1), channel_id=1, source_target_pairs={{0,1},{1,0},{2,3},{3,2},{4,5},{5,4},{6,7},{7,6},{8,9},{9,8},{10,11... | collective-permute-start | bytes 3145736 | tf_op jit(solution)/shard_map/ppermute | solution.py:584
  39.2 18.9 %all-to-all-start.1 = ((bf16[32,32,256]{2,1,0:T(8,128)(2,1)}), bf16[32,32,256]{2,1,0:T(8,128)(2,1)S(1)}, u32[]{:S(2)}, u32[]{:S(2)}) async-start(bf16[32,32,256]{2,1,0:T(8,128)(2,1)} %get-tuple-element.29), calls=%async_computation.1 | async-start | bytes 1048576 | tf_op jit(solution)/shard_map/all_to_all | solution.py:668
  42.7 1.2 %collective-permute-start.1 = (f32[8,512]{1,0:T(8,128)S(1)}, f32[8,512]{1,0:T(8,128)S(1)}, u32[]{:S(2)}, u32[]{:S(2)}) collective-permute-start(f32[8,512]{1,0:T(8,128)S(1)} %get-tuple-element.31.refs_0_), channel_id=1, source_target_pairs={{0,1},{1,0},{2,3},{3,2},{4,5},{5,4},{6,7},{7,6},{8,9},{9,8},{10,11... | collective-permute-start | bytes 49160 | tf_op jit(solution)/shard_map/ppermute | solution.py:584
  42.9 1.1 %copy-start = (bf16[512,1024]{1,0:T(8,128)(2,1)}, bf16[512,1024]{1,0:T(8,128)(2,1)S(1)}, u32[]{:S(2)}) copy-start(bf16[512,1024]{1,0:T(8,128)(2,1)S(1)} %collective-permute-done.3.refs_5_.refs_0_) | copy-start | bytes 3145732
  67.7 1.6 %collective-permute-start.6 = (bf16[256,512]{1,0:T(8,128)(2,1)S(1)}, bf16[256,512]{1,0:T(8,128)(2,1)S(1)}, u32[]{:S(2)}, u32[]{:S(2)}) collective-permute-start(bf16[256,512]{1,0:T(8,128)(2,1)S(1)} %get-tuple-element.40), channel_id=1, source_target_pairs={{0,1},{1,0},{2,3},{3,2},{4,5},{5,4},{6,7},{7,6},{8,9},{9,8},{10,11... | collective-permute-start | bytes 786440 | tf_op jit(solution)/shard_map/ppermute | solution.py:713

commit v5 on v4

--- a/solution.py
+++ b/solution.py
@@ -13,7 +13,7 @@
 KSHORT = 3
 LANES = 128
 HALO = 16
-AHEAD = 6
+AHEAD = 4
 EPS = 1e-05
 PI_HIGH = 3.140625
 PI_LOW = 9.67653589793e-4
@@ -143,7 +143,7 @@
         keeps.append(pltpu.make_async_copy(x_refs[p].at[mine], rows_hbm.at[p], row_sems.at[p]))
     for keep in keeps:
         keep.start()
-    step = min(width, 256)
+    step = min(width, 512)
     per_step = step // own
     parts = tokens // LANES
     proj_ref[:, :8, :] = jnp.zeros((2, 8, step), F32)
@@ -588,7 +588,7 @@
 
     x_pieces = all_turned(layer_input)
     by_role = jnp.transpose(in_weight, (1, 0, 2))
-    step = min(width, 256)
+    step = min(width, 512)
     normed, my_rows, gated = call(
         functools.partial(
             project_kernel, pieces=pieces, tokens=tokens, width=width, own=own, own_rows=own_rows, share=share
@@ -690,7 +690,7 @@
         normed, *all_turned(side), *all_turned(by_role), *mix_weights,
     )
     units = up_weight.shape[1]
-    block = min(512, units)
+    block = min(1024, units)
     results = call(
         functools.partial(tail_kernel, pieces=pieces, share=share, width=width, block=block, rest=rest),
         "vvvch" + "h" * (1 + 2 * pieces),

time: 70.7 us -> 70.1 us (level)
  no operation moved by 1% of the time
where the time goes in v5:
time: 70.1 us; the launch traced here: 69.7 us
  Pallas kernels  36.1 us (51%)
  waiting for transfers between devices  20 us (29%)
  starting transfers between devices  13.3 us (19%)
    pallas_call x6, Pallas kernels, call(): pl.pallas_call(kernel, in_specs=[kinds[kind] for kind in in_specs], out_s...  36.1 us
    all_to_all x1, waiting for transfers between devices, per_device(): lax.all_to_all(convolved, ('seq', 'chan'), split_axis=0, concat_axis=0, t...  9.99 us
    all_to_all x1, starting transfers between devices, per_device(): lax.all_to_all(gated, 'seq', split_axis=0, concat_axis=0, tiled=True)  8.02 us
    all_to_all x1, waiting for transfers between devices, per_device(): lax.all_to_all(gated, 'seq', split_axis=0, concat_axis=0, tiled=True)  5.55 us
    all_to_all x1, starting transfers between devices, per_device(): lax.all_to_all(convolved, ('seq', 'chan'), split_axis=0, concat_axis=0, t...  3.55 us
    ppermute x6, waiting for transfers between devices, turned(): lax.ppermute(array, 'chan', [(i, (i - by) % pieces) for i in range(pieces)])  2.9 us
    ppermute x6, starting transfers between devices, turned(): lax.ppermute(array, 'chan', [(i, (i - by) % pieces) for i in range(pieces)])  1.65 us
    ppermute x1, waiting for transfers between devices, per_device(): lax.ppermute(results[p], 'chan', [(i, (i + p) % pieces) for i in range(pi...  1.52 us
  transfers between devices with their start and end apart: 9, of which 5 were waited for; matrix products, arithmetic and copies ran while one was open for 0% of the time, Pallas kernels for 29%

profile of v5, /device:TPU:0, one launch (start us, length us, event | category | flops | bytes accessed | tf_op | source)
XLA Modules:
  0.0 69.7 jit_solution(8674442090107740355)
XLA Ops:
  0.0 0.0 copy-start.1
  0.0 0.5 collective-permute-start
  0.5 1.7 %collective-permute-done.refs_1_ = bf16[512,512]{1,0:T(8,128)(2,1)S(1)} collective-permute-done((bf16[512,512]{1,0:T(8,128)(2,1)}, bf16[512,512]{1,0:T(8,128)(2,1)S(1)}, u32[]{:S(2)}, u32[]{:S(2)}) %collective-permute-start) | collective-permute-done | bytes 524320 | tf_op jit(solution)/shard_map/ppermute | solution.py:584
  2.2 5.8 %shard_map.181 = (bf16[2,512,512]{2,1,0:T(8,128)(2,1)}, bf16[2,256,512]{2,1,0:T(8,128)(2,1)}, bf16[16,144,128]{2,1,0:T(8,128)(2,1)}) custom-call(bf16[512,512]{1,0:T(8,128)(2,1)} %refs_0_.1, bf16[512,512]{1,0:T(8,128)(2,1)S(1)} %collective-permute-done.refs_1_, f32[2,1,512]{2,1,0:T(1,128)} %bitcast.8, f32[3,3,512]{2,1,0:T(4,128)} %taps_ref.1, ...), custom_call_target="tpu_custom_call" | custom-call | tf_op jit(solution)/shard_map/pallas_call | solution.py:553
  8.0 0.4 collective-permute-start.4
  8.4 0.1 collective-permute-start.5
  8.5 0.4 collective-permute-start.2
  8.9 8.0 %all-to-all-start = ((bf16[16,144,128]{2,1,0:T(8,128)(2,1)}), bf16[16,144,128]{2,1,0:T(8,128)(2,1)S(1)}, u32[]{:S(2)}, u32[]{:S(2)}) async-start(bf16[16,144,128]{2,1,0:T(8,128)(2,1)} %get-tuple-element.24), calls=%async_computation | async-start | bytes 1179648 | tf_op jit(solution)/shard_map/all_to_all | solution.py:619
  16.9 0.0 copy-done.1
  17.0 0.1 collective-permute-start.3
  17.1 10.9 %shard_map.182 = (f32[2304,256]{1,0:T(8,128)}, f32[3,8,128]{2,1,0:T(8,128)S(1)}, f32[32,128]{1,0:T(8,128)S(1)}, f32[3,512]{1,0:T(4,128)S(1)}) custom-call(bf16[25,64]{1,0:T(8,128)(2,1)} %in_ref.1, f32[1,64]{1,0:T(1,128)} %bitcast.12, bf16[64,64]{1,0:T(8,128)(2,1)} %mid_w_ref.1, bf16[64,512]{1,0:T(8,128)(2,1)} %out_w_ref.1, f32[1,512]{1,0:T(1,128)} %bitcast.10, ...), custom_call_target="tpu_custom_call" | custom-call | tf_op jit(solution)/shard_map/pallas_call | solution.py:553
  28.0 5.6 %all-to-all-done.x_ref = bf16[16,144,128]{2,1,0:T(8,128)(2,1)S(1)} async-done(((bf16[16,144,128]{2,1,0:T(8,128)(2,1)}), bf16[16,144,128]{2,1,0:T(8,128)(2,1)S(1)}, u32[]{:S(2)}, u32[]{:S(2)}) %all-to-all-start) | async-done | bytes 589856 | tf_op jit(solution)/shard_map/all_to_all | solution.py:619
  33.6 5.4 %shard_map.183 = (bf16[32,32,256]{2,1,0:T(8,128)(2,1)}, f32[8,512]{1,0:T(8,128)S(1)}) custom-call(bf16[16,144,128]{2,1,0:T(8,128)(2,1)S(1)} %all-to-all-done.x_ref, f32[3,8,128]{2,1,0:T(8,128)S(1)} %get-tuple-element.25.taps_ref, f32[32,128]{1,0:T(8,128)S(1)} %get-tuple-element.26.direct_ref, f32[3,512]{1,0:T(4,128)S(1)} %get-tuple-element.27.gate_taps_ref, ...), custom_call_target="tpu_custom_call" | custom-call | tf_op jit(solution)/shard_map/pallas_call | solution.py:553
  39.0 3.5 %all-to-all-start.1 = ((bf16[32,32,256]{2,1,0:T(8,128)(2,1)}), bf16[32,32,256]{2,1,0:T(8,128)(2,1)S(1)}, u32[]{:S(2)}, u32[]{:S(2)}) async-start(bf16[32,32,256]{2,1,0:T(8,128)(2,1)} %get-tuple-element.29), calls=%async_computation.1 | async-start | bytes 1048576 | tf_op jit(solution)/shard_map/all_to_all | solution.py:668
  42.5 0.1 collective-permute-start.1
  42.6 0.0 collective-permute-done.3.refs_5_.refs_0_
  42.6 0.0 copy-start
  42.6 1.1 %collective-permute-done.1.refs_1_ = f32[8,512]{1,0:T(8,128)S(1)} collective-permute-done((f32[8,512]{1,0:T(8,128)S(1)}, f32[8,512]{1,0:T(8,128)S(1)}, u32[]{:S(2)}, u32[]{:S(2)}) %collective-permute-start.1) | collective-permute-done | bytes 16416 | tf_op jit(solution)/shard_map/ppermute | solution.py:584
  43.8 0.0 collective-permute-done.2.refs_3_
  43.8 0.0 copy-done
  43.8 4.1 %shard_map.184 = (f32[2,512,256]{2,1,0:T(8,128)S(1)}, bf16[960,1024]{1,0:T(8,128)(2,1)S(1)}) custom-call(bf16[2,512,512]{2,1,0:T(8,128)(2,1)} %get-tuple-element.30.normed_ref, f32[8,512]{1,0:T(8,128)S(1)} %get-tuple-element.31.refs_0_, f32[8,512]{1,0:T(8,128)S(1)} %collective-permute-done.1.refs_1_, bf16[3,1024,512]{2,1,0:T(8,128)(2,1)} %bitcast.refs_4_.refs_2_, ...), custom_call_target="tpu_custom_call" | custom-call | tf_op jit(solution)/shard_map/pallas_call | solution.py:553
  47.9 10.0 %all-to-all-done.1 = bf16[32,32,256]{2,1,0:T(8,128)(2,1)S(1)} async-done(((bf16[32,32,256]{2,1,0:T(8,128)(2,1)}), bf16[32,32,256]{2,1,0:T(8,128)(2,1)S(1)}, u32[]{:S(2)}, u32[]{:S(2)}) %all-to-all-start.1) | async-done | bytes 524320 | tf_op jit(solution)/shard_map/all_to_all | solution.py:668
  57.8 0.0 collective-permute-done.4.refs_2_
  57.9 0.0 collective-permute-done.5.refs_4_
  57.9 9.2 %shard_map.185 = (bf16[256,512]{1,0:T(8,128)(2,1)S(1)}, bf16[256,512]{1,0:T(8,128)(2,1)S(1)}) custom-call(bf16[16,2,32,256]{3,2,1,0:T(8,128)(2,1)S(1)} %bitcast.7, f32[2,512,256]{2,1,0:T(8,128)S(1)} %get-tuple-element.34.gate_ref, bf16[960,1024]{1,0:T(8,128)(2,1)S(1)} %get-tuple-element.35.mix_ref, f32[1,1024]{1,0:T(1,128)} %bitcast.9, ...), custom_call_target="tpu_custom_call" | custom-call | tf_op jit(solution)/shard_map/pallas_call | solution.py:553
  67.1 0.1 collective-permute-start.6
  67.1 1.5 %collective-permute-done.6.refs_1_ = bf16[256,512]{1,0:T(8,128)(2,1)S(1)} collective-permute-done((bf16[256,512]{1,0:T(8,128)(2,1)S(1)}, bf16[256,512]{1,0:T(8,128)(2,1)S(1)}, u32[]{:S(2)}, u32[]{:S(2)}) %collective-permute-start.6) | collective-permute-done | bytes 262176 | tf_op jit(solution)/shard_map/ppermute | solution.py:713
  68.7 0.8 %shard_map.186 = bf16[512,512]{1,0:T(8,128)(2,1)} custom-call(bf16[256,512]{1,0:T(8,128)(2,1)S(1)} %get-tuple-element.39.refs_0_, bf16[256,512]{1,0:T(8,128)(2,1)S(1)} %collective-permute-done.6.refs_1_), custom_call_target="tpu_custom_call" | custom-call | tf_op jit(solution)/shard_map/pallas_call | solution.py:553
Async XLA Ops:
  0.0 16.9 %copy-start.1 = (bf16[512,1024]{1,0:T(8,128)(2,1)S(1)}, bf16[512,1024]{1,0:T(8,128)(2,1)}, u32[]{:S(2)}) copy-start(bf16[512,1024]{1,0:T(8,128)(2,1)} %refs_4_) | copy-start | bytes 3145732
  0.0 2.2 %collective-permute-start = (bf16[512,512]{1,0:T(8,128)(2,1)}, bf16[512,512]{1,0:T(8,128)(2,1)S(1)}, u32[]{:S(2)}, u32[]{:S(2)}) collective-permute-start(bf16[512,512]{1,0:T(8,128)(2,1)} %refs_0_.1), channel_id=1, source_target_pairs={{0,1},{1,0},{2,3},{3,2},{4,5},{5,4},{6,7},{7,6},{8,9},{9,8},{10,11... | collective-permute-start | bytes 1572872 | tf_op jit(solution)/shard_map/ppermute | solution.py:584
  8.0 49.9 %collective-permute-start.4 = (bf16[1024,2048]{1,0:T(8,128)(2,1)}, bf16[1024,2048]{1,0:T(8,128)(2,1)}, u32[]{:S(2)}, u32[]{:S(2)}) collective-permute-start(bf16[1024,2048]{1,0:T(8,128)(2,1)} %refs_1_), channel_id=1, source_target_pairs={{0,1},{1,0},{2,3},{3,2},{4,5},{5,4},{6,7},{7,6},{8,9},{9,8},{10,11... | collective-permute-start | bytes 12582920 | tf_op jit(solution)/shard_map/ppermute | solution.py:584
  8.4 49.4 %collective-permute-start.5 = (bf16[2048,1024]{1,0:T(8,128)(2,1)}, bf16[2048,1024]{1,0:T(8,128)(2,1)}, u32[]{:S(2)}, u32[]{:S(2)}) collective-permute-start(bf16[2048,1024]{1,0:T(8,128)(2,1)} %refs_3_.2), channel_id=1, source_target_pairs={{0,1},{1,0},{2,3},{3,2},{4,5},{5,4},{6,7},{7,6},{8,9},{9,8},{10,11... | collective-permute-start | bytes 12582920 | tf_op jit(solution)/shard_map/ppermute | solution.py:584
  8.5 35.2 %collective-permute-start.2 = (bf16[3,1024,512]{2,1,0:T(8,128)(2,1)}, bf16[3,1024,512]{2,1,0:T(8,128)(2,1)}, u32[]{:S(2)}, u32[]{:S(2)}) collective-permute-start(bf16[3,1024,512]{2,1,0:T(8,128)(2,1)} %bitcast.refs_4_.refs_2_), channel_id=1, source_target_pairs={{0,1},{1,0},{2,3},{3,2},{4,5},{5,4},{6,7},{7,6},{8,9},{9,8},{10,11... | collective-permute-start | bytes 9437192 | tf_op jit(solution)/shard_map/ppermute | solution.py:584
  8.9 24.6 %all-to-all-start = ((bf16[16,144,128]{2,1,0:T(8,128)(2,1)}), bf16[16,144,128]{2,1,0:T(8,128)(2,1)S(1)}, u32[]{:S(2)}, u32[]{:S(2)}) async-start(bf16[16,144,128]{2,1,0:T(8,128)(2,1)} %get-tuple-element.24), calls=%async_computation | async-start | bytes 1179648 | tf_op jit(solution)/shard_map/all_to_all | solution.py:619
  17.0 25.7 %collective-permute-start.3 = (bf16[512,1024]{1,0:T(8,128)(2,1)S(1)}, bf16[512,1024]{1,0:T(8,128)(2,1)S(1)}, u32[]{:S(2)}, u32[]{:S(2)}) collective-permute-start(bf16[512,1024]{1,0:T(8,128)(2,1)S(1)} %copy-done.1), channel_id=1, source_target_pairs={{0,1},{1,0},{2,3},{3,2},{4,5},{5,4},{6,7},{7,6},{8,9},{9,8},{10,11... | collective-permute-start | bytes 3145736 | tf_op jit(solution)/shard_map/ppermute | solution.py:584
  39.0 18.9 %all-to-all-start.1 = ((bf16[32,32,256]{2,1,0:T(8,128)(2,1)}), bf16[32,32,256]{2,1,0:T(8,128)(2,1)S(1)}, u32[]{:S(2)}, u32[]{:S(2)}) async-start(bf16[32,32,256]{2,1,0:T(8,128)(2,1)} %get-tuple-element.29), calls=%async_computation.1 | async-start | bytes 1048576 | tf_op jit(solution)/shard_map/all_to_all | solution.py:668
  42.5 1.2 %collective-permute-start.1 = (f32[8,512]{1,0:T(8,128)S(1)}, f32[8,512]{1,0:T(8,128)S(1)}, u32[]{:S(2)}, u32[]{:S(2)}) collective-permute-start(f32[8,512]{1,0:T(8,128)S(1)} %get-tuple-element.31.refs_0_), channel_id=1, source_target_pairs={{0,1},{1,0},{2,3},{3,2},{4,5},{5,4},{6,7},{7,6},{8,9},{9,8},{10,11... | collective-permute-start | bytes 49160 | tf_op jit(solution)/shard_map/ppermute | solution.py:584
  42.6 1.1 %copy-start = (bf16[512,1024]{1,0:T(8,128)(2,1)}, bf16[512,1024]{1,0:T(8,128)(2,1)S(1)}, u32[]{:S(2)}) copy-start(bf16[512,1024]{1,0:T(8,128)(2,1)S(1)} %collective-permute-done.3.refs_5_.refs_0_) | copy-start | bytes 3145732
  67.1 1.6 %collective-permute-start.6 = (bf16[256,512]{1,0:T(8,128)(2,1)S(1)}, bf16[256,512]{1,0:T(8,128)(2,1)S(1)}, u32[]{:S(2)}, u32[]{:S(2)}) collective-permute-start(bf16[256,512]{1,0:T(8,128)(2,1)S(1)} %get-tuple-element.40), channel_id=1, source_target_pairs={{0,1},{1,0},{2,3},{3,2},{4,5},{5,4},{6,7},{7,6},{8,9},{9,8},{10,11... | collective-permute-start | bytes 786440 | tf_op jit(solution)/shard_map/ppermute | solution.py:713

commit v6 on v5

--- a/solution.py
+++ b/solution.py
@@ -167,7 +167,7 @@
                     + taps_ref[lag, role + 1 : role + 2, cols] * proj_ref[role, 8 - lag : 8 - lag + tokens, :]
                 )
             shorted.append(value)
-        gated = (shorted[1] * shorted[0]).T
+        gated = (shorted[1] * shorted[0]).astype(BF16).T
         if col == 0:
             loads[2].wait()
             last = 0.0
@@ -195,7 +195,7 @@
             for part in range(parts):
                 block_ref[first + d, part * own_rows : part * own_rows + own, :] = gated[
                     d * own : (d + 1) * own, part * LANES : (part + 1) * LANES
-                ].astype(BF16)
+                ]
             block_edges = jnp.concatenate([edges[:, d * own : (d + 1) * own], jnp.zeros((8, LANES - own), F32)], 1)
             block_ref[first + d, parts * own_rows :, :] = jnp.concatenate([block_edges, spread_last], 0).astype(BF16)
         targets = pl.ds(first, per_step)

time: 70.1 us -> 70 us (level)
  no operation moved by 1% of the time
where the time goes in v6:
time: 70 us; the launch traced here: 69.6 us
  Pallas kernels  36.1 us (52%)
  waiting for transfers between devices  20 us (29%)
  starting transfers between devices  13.3 us (19%)
    pallas_call x6, Pallas kernels, call(): pl.pallas_call(kernel, in_specs=[kinds[kind] for kind in in_specs], out_s...  36.1 us
    all_to_all x1, waiting for transfers between devices, per_device(): lax.all_to_all(convolved, ('seq', 'chan'), split_axis=0, concat_axis=0, t...  9.99 us
    all_to_all x1, starting transfers between devices, per_device(): lax.all_to_all(gated, 'seq', split_axis=0, concat_axis=0, tiled=True)  8.02 us
    all_to_all x1, waiting for transfers between devices, per_device(): lax.all_to_all(gated, 'seq', split_axis=0, concat_axis=0, tiled=True)  5.55 us
    all_to_all x1, starting transfers between devices, per_device(): lax.all_to_all(convolved, ('seq', 'chan'), split_axis=0, concat_axis=0, t...  3.55 us
    ppermute x6, waiting for transfers between devices, turned(): lax.ppermute(array, 'chan', [(i, (i - by) % pieces) for i in range(pieces)])  2.9 us
    ppermute x6, starting transfers between devices, turned(): lax.ppermute(array, 'chan', [(i, (i - by) % pieces) for i in range(pieces)])  1.65 us
    ppermute x1, waiting for transfers between devices, per_device(): lax.ppermute(results[p], 'chan', [(i, (i + p) % pieces) for i in range(pi...  1.52 us
  transfers between devices with their start and end apart: 9, of which 5 were waited for; matrix products, arithmetic and copies ran while one was open for 0% of the time, Pallas kernels for 29%

profile of v6, /device:TPU:0, one launch (start us, length us, event | category | flops | bytes accessed | tf_op | source)
XLA Modules:
  0.0 69.6 jit_solution(12736721412200655942)
XLA Ops:
  0.0 0.0 copy-start.1
  0.0 0.5 collective-permute-start
  0.5 1.7 %collective-permute-done.refs_1_ = bf16[512,512]{1,0:T(8,128)(2,1)S(1)} collective-permute-done((bf16[512,512]{1,0:T(8,128)(2,1)}, bf16[512,512]{1,0:T(8,128)(2,1)S(1)}, u32[]{:S(2)}, u32[]{:S(2)}) %collective-permute-start) | collective-permute-done | bytes 524320 | tf_op jit(solution)/shard_map/ppermute | solution.py:584
  2.2 5.7 %shard_map.181 = (bf16[2,512,512]{2,1,0:T(8,128)(2,1)}, bf16[2,256,512]{2,1,0:T(8,128)(2,1)}, bf16[16,144,128]{2,1,0:T(8,128)(2,1)}) custom-call(bf16[512,512]{1,0:T(8,128)(2,1)} %refs_0_.1, bf16[512,512]{1,0:T(8,128)(2,1)S(1)} %collective-permute-done.refs_1_, f32[2,1,512]{2,1,0:T(1,128)} %bitcast.8, f32[3,3,512]{2,1,0:T(4,128)} %taps_ref.1, ...), custom_call_target="tpu_custom_call" | custom-call | tf_op jit(solution)/shard_map/pallas_call | solution.py:553
  7.9 0.4 collective-permute-start.4
  8.3 0.1 collective-permute-start.5
  8.5 0.4 collective-permute-start.2
  8.8 8.0 %all-to-all-start = ((bf16[16,144,128]{2,1,0:T(8,128)(2,1)}), bf16[16,144,128]{2,1,0:T(8,128)(2,1)S(1)}, u32[]{:S(2)}, u32[]{:S(2)}) async-start(bf16[16,144,128]{2,1,0:T(8,128)(2,1)} %get-tuple-element.24), calls=%async_computation | async-start | bytes 1179648 | tf_op jit(solution)/shard_map/all_to_all | solution.py:619
  16.9 0.0 copy-done.1
  16.9 0.1 collective-permute-start.3
  17.0 10.9 %shard_map.182 = (f32[2304,256]{1,0:T(8,128)}, f32[3,8,128]{2,1,0:T(8,128)S(1)}, f32[32,128]{1,0:T(8,128)S(1)}, f32[3,512]{1,0:T(4,128)S(1)}) custom-call(bf16[25,64]{1,0:T(8,128)(2,1)} %in_ref.1, f32[1,64]{1,0:T(1,128)} %bitcast.12, bf16[64,64]{1,0:T(8,128)(2,1)} %mid_w_ref.1, bf16[64,512]{1,0:T(8,128)(2,1)} %out_w_ref.1, f32[1,512]{1,0:T(1,128)} %bitcast.10, ...), custom_call_target="tpu_custom_call" | custom-call | tf_op jit(solution)/shard_map/pallas_call | solution.py:553
  27.9 5.5 %all-to-all-done.x_ref = bf16[16,144,128]{2,1,0:T(8,128)(2,1)S(1)} async-done(((bf16[16,144,128]{2,1,0:T(8,128)(2,1)}), bf16[16,144,128]{2,1,0:T(8,128)(2,1)S(1)}, u32[]{:S(2)}, u32[]{:S(2)}) %all-to-all-start) | async-done | bytes 589856 | tf_op jit(solution)/shard_map/all_to_all | solution.py:619
  33.5 5.4 %shard_map.183 = (bf16[32,32,256]{2,1,0:T(8,128)(2,1)}, f32[8,512]{1,0:T(8,128)S(1)}) custom-call(bf16[16,144,128]{2,1,0:T(8,128)(2,1)S(1)} %all-to-all-done.x_ref, f32[3,8,128]{2,1,0:T(8,128)S(1)} %get-tuple-element.25.taps_ref, f32[32,128]{1,0:T(8,128)S(1)} %get-tuple-element.26.direct_ref, f32[3,512]{1,0:T(4,128)S(1)} %get-tuple-element.27.gate_taps_ref, ...), custom_call_target="tpu_custom_call" | custom-call | tf_op jit(solution)/shard_map/pallas_call | solution.py:553
  38.9 3.6 %all-to-all-start.1 = ((bf16[32,32,256]{2,1,0:T(8,128)(2,1)}), bf16[32,32,256]{2,1,0:T(8,128)(2,1)S(1)}, u32[]{:S(2)}, u32[]{:S(2)}) async-start(bf16[32,32,256]{2,1,0:T(8,128)(2,1)} %get-tuple-element.29), calls=%async_computation.1 | async-start | bytes 1048576 | tf_op jit(solution)/shard_map/all_to_all | solution.py:668
  42.4 0.1 collective-permute-start.1
  42.5 0.0 collective-permute-done.3.refs_5_.refs_0_
  42.5 0.0 copy-start
  42.5 1.1 %collective-permute-done.1.refs_1_ = f32[8,512]{1,0:T(8,128)S(1)} collective-permute-done((f32[8,512]{1,0:T(8,128)S(1)}, f32[8,512]{1,0:T(8,128)S(1)}, u32[]{:S(2)}, u32[]{:S(2)}) %collective-permute-start.1) | collective-permute-done | bytes 16416 | tf_op jit(solution)/shard_map/ppermute | solution.py:584
  43.7 0.0 collective-permute-done.2.refs_3_
  43.7 0.0 copy-done
  43.7 4.1 %shard_map.184 = (f32[2,512,256]{2,1,0:T(8,128)S(1)}, bf16[960,1024]{1,0:T(8,128)(2,1)S(1)}) custom-call(bf16[2,512,512]{2,1,0:T(8,128)(2,1)} %get-tuple-element.30.normed_ref, f32[8,512]{1,0:T(8,128)S(1)} %get-tuple-element.31.refs_0_, f32[8,512]{1,0:T(8,128)S(1)} %collective-permute-done.1.refs_1_, bf16[3,1024,512]{2,1,0:T(8,128)(2,1)} %bitcast.refs_4_.refs_2_, ...), custom_call_target="tpu_custom_call" | custom-call | tf_op jit(solution)/shard_map/pallas_call | solution.py:553
  47.8 10.0 %all-to-all-done.1 = bf16[32,32,256]{2,1,0:T(8,128)(2,1)S(1)} async-done(((bf16[32,32,256]{2,1,0:T(8,128)(2,1)}), bf16[32,32,256]{2,1,0:T(8,128)(2,1)S(1)}, u32[]{:S(2)}, u32[]{:S(2)}) %all-to-all-start.1) | async-done | bytes 524320 | tf_op jit(solution)/shard_map/all_to_all | solution.py:668
  57.8 0.0 collective-permute-done.4.refs_2_
  57.8 0.0 collective-permute-done.5.refs_4_
  57.8 9.2 %shard_map.185 = (bf16[256,512]{1,0:T(8,128)(2,1)S(1)}, bf16[256,512]{1,0:T(8,128)(2,1)S(1)}) custom-call(bf16[16,2,32,256]{3,2,1,0:T(8,128)(2,1)S(1)} %bitcast.7, f32[2,512,256]{2,1,0:T(8,128)S(1)} %get-tuple-element.34.gate_ref, bf16[960,1024]{1,0:T(8,128)(2,1)S(1)} %get-tuple-element.35.mix_ref, f32[1,1024]{1,0:T(1,128)} %bitcast.9, ...), custom_call_target="tpu_custom_call" | custom-call | tf_op jit(solution)/shard_map/pallas_call | solution.py:553
  67.0 0.1 collective-permute-start.6
  67.1 1.5 %collective-permute-done.6.refs_1_ = bf16[256,512]{1,0:T(8,128)(2,1)S(1)} collective-permute-done((bf16[256,512]{1,0:T(8,128)(2,1)S(1)}, bf16[256,512]{1,0:T(8,128)(2,1)S(1)}, u32[]{:S(2)}, u32[]{:S(2)}) %collective-permute-start.6) | collective-permute-done | bytes 262176 | tf_op jit(solution)/shard_map/ppermute | solution.py:713
  68.6 0.8 %shard_map.186 = bf16[512,512]{1,0:T(8,128)(2,1)} custom-call(bf16[256,512]{1,0:T(8,128)(2,1)S(1)} %get-tuple-element.39.refs_0_, bf16[256,512]{1,0:T(8,128)(2,1)S(1)} %collective-permute-done.6.refs_1_), custom_call_target="tpu_custom_call" | custom-call | tf_op jit(solution)/shard_map/pallas_call | solution.py:553
Async XLA Ops:
  0.0 16.9 %copy-start.1 = (bf16[512,1024]{1,0:T(8,128)(2,1)S(1)}, bf16[512,1024]{1,0:T(8,128)(2,1)}, u32[]{:S(2)}) copy-start(bf16[512,1024]{1,0:T(8,128)(2,1)} %refs_4_) | copy-start | bytes 3145732
  0.0 2.2 %collective-permute-start = (bf16[512,512]{1,0:T(8,128)(2,1)}, bf16[512,512]{1,0:T(8,128)(2,1)S(1)}, u32[]{:S(2)}, u32[]{:S(2)}) collective-permute-start(bf16[512,512]{1,0:T(8,128)(2,1)} %refs_0_.1), channel_id=1, source_target_pairs={{0,1},{1,0},{2,3},{3,2},{4,5},{5,4},{6,7},{7,6},{8,9},{9,8},{10,11... | collective-permute-start | bytes 1572872 | tf_op jit(solution)/shard_map/ppermute | solution.py:584
  7.9 49.9 %collective-permute-start.4 = (bf16[1024,2048]{1,0:T(8,128)(2,1)}, bf16[1024,2048]{1,0:T(8,128)(2,1)}, u32[]{:S(2)}, u32[]{:S(2)}) collective-permute-start(bf16[1024,2048]{1,0:T(8,128)(2,1)} %refs_1_), channel_id=1, source_target_pairs={{0,1},{1,0},{2,3},{3,2},{4,5},{5,4},{6,7},{7,6},{8,9},{9,8},{10,11... | collective-permute-start | bytes 12582920 | tf_op jit(solution)/shard_map/ppermute | solution.py:584
  8.3 49.4 %collective-permute-start.5 = (bf16[2048,1024]{1,0:T(8,128)(2,1)}, bf16[2048,1024]{1,0:T(8,128)(2,1)}, u32[]{:S(2)}, u32[]{:S(2)}) collective-permute-start(bf16[2048,1024]{1,0:T(8,128)(2,1)} %refs_3_.2), channel_id=1, source_target_pairs={{0,1},{1,0},{2,3},{3,2},{4,5},{5,4},{6,7},{7,6},{8,9},{9,8},{10,11... | collective-permute-start | bytes 12582920 | tf_op jit(solution)/shard_map/ppermute | solution.py:584
  8.5 35.2 %collective-permute-start.2 = (bf16[3,1024,512]{2,1,0:T(8,128)(2,1)}, bf16[3,1024,512]{2,1,0:T(8,128)(2,1)}, u32[]{:S(2)}, u32[]{:S(2)}) collective-permute-start(bf16[3,1024,512]{2,1,0:T(8,128)(2,1)} %bitcast.refs_4_.refs_2_), channel_id=1, source_target_pairs={{0,1},{1,0},{2,3},{3,2},{4,5},{5,4},{6,7},{7,6},{8,9},{9,8},{10,11... | collective-permute-start | bytes 9437192 | tf_op jit(solution)/shard_map/ppermute | solution.py:584
  8.8 24.6 %all-to-all-start = ((bf16[16,144,128]{2,1,0:T(8,128)(2,1)}), bf16[16,144,128]{2,1,0:T(8,128)(2,1)S(1)}, u32[]{:S(2)}, u32[]{:S(2)}) async-start(bf16[16,144,128]{2,1,0:T(8,128)(2,1)} %get-tuple-element.24), calls=%async_computation | async-start | bytes 1179648 | tf_op jit(solution)/shard_map/all_to_all | solution.py:619
  16.9 25.7 %collective-permute-start.3 = (bf16[512,1024]{1,0:T(8,128)(2,1)S(1)}, bf16[512,1024]{1,0:T(8,128)(2,1)S(1)}, u32[]{:S(2)}, u32[]{:S(2)}) collective-permute-start(bf16[512,1024]{1,0:T(8,128)(2,1)S(1)} %copy-done.1), channel_id=1, source_target_pairs={{0,1},{1,0},{2,3},{3,2},{4,5},{5,4},{6,7},{7,6},{8,9},{9,8},{10,11... | collective-permute-start | bytes 3145736 | tf_op jit(solution)/shard_map/ppermute | solution.py:584
  38.9 18.9 %all-to-all-start.1 = ((bf16[32,32,256]{2,1,0:T(8,128)(2,1)}), bf16[32,32,256]{2,1,0:T(8,128)(2,1)S(1)}, u32[]{:S(2)}, u32[]{:S(2)}) async-start(bf16[32,32,256]{2,1,0:T(8,128)(2,1)} %get-tuple-element.29), calls=%async_computation.1 | async-start | bytes 1048576 | tf_op jit(solution)/shard_map/all_to_all | solution.py:668
  42.4 1.2 %collective-permute-start.1 = (f32[8,512]{1,0:T(8,128)S(1)}, f32[8,512]{1,0:T(8,128)S(1)}, u32[]{:S(2)}, u32[]{:S(2)}) collective-permute-start(f32[8,512]{1,0:T(8,128)S(1)} %get-tuple-element.31.refs_0_), channel_id=1, source_target_pairs={{0,1},{1,0},{2,3},{3,2},{4,5},{5,4},{6,7},{7,6},{8,9},{9,8},{10,11... | collective-permute-start | bytes 49160 | tf_op jit(solution)/shard_map/ppermute | solution.py:584
  42.5 1.1 %copy-start = (bf16[512,1024]{1,0:T(8,128)(2,1)}, bf16[512,1024]{1,0:T(8,128)(2,1)S(1)}, u32[]{:S(2)}) copy-start(bf16[512,1024]{1,0:T(8,128)(2,1)S(1)} %collective-permute-done.3.refs_5_.refs_0_) | copy-start | bytes 3145732
  67.0 1.6 %collective-permute-start.6 = (bf16[256,512]{1,0:T(8,128)(2,1)S(1)}, bf16[256,512]{1,0:T(8,128)(2,1)S(1)}, u32[]{:S(2)}, u32[]{:S(2)}) collective-permute-start(bf16[256,512]{1,0:T(8,128)(2,1)S(1)} %get-tuple-element.40), channel_id=1, source_target_pairs={{0,1},{1,0},{2,3},{3,2},{4,5},{5,4},{6,7},{7,6},{8,9},{9,8},{10,11... | collective-permute-start | bytes 786440 | tf_op jit(solution)/shard_map/ppermute | solution.py:713
